TPU v7x, 128 devices: a whole 4x4x4 slice. The times are simulated.
128 devices in a mesh: group: 2 (over core), member: 64 (over x, y, z).
Axes of the slice: x: 4, y: 4, z: 4, core: 2. Of those that a mesh axis runs over, the one named last changes fastest.
Arguments:
- events: bfloat16 [65536, 512], P(('group', 'member')), may hold values from -6 to 6
- route: int32 [4096], P(('group', 'member')), may hold values from 0 to 2047, as said below
- block_offset: int32 [512], P(('group', 'member')), may hold values from 0 to 1, as said below
- hist_length: int32 [512], P(('group', 'member')), may hold values from 64 to 256, as said below
- cotangent: bfloat16 [65536, 512], P(('group', 'member')), may hold values from -6 to 6
- w_in: bfloat16 [512, 2048], replicated, may hold values from -0.25 to 0.25
- w_out: bfloat16 [512, 512], replicated, may hold values from -0.25 to 0.25
- rab: float32 [4, 12], replicated, may hold values from -4 to 4
Outputs:
- outputs: bfloat16 [65536, 512], P(('group', 'member'))
- events_grad: bfloat16 [65536, 512], P(('group', 'member'))
- w_in_grad: float32 [512, 2048], replicated
- w_out_grad: float32 [512, 512], replicated
Inputs may be any that keep to these rules, and one draw needn't show every extreme that they name: Within each group, route is a permutation of the group's piece places; place t lies on member t // 32 at piece t % 32. A device sends either no piece or exactly 1 pieces to each device of its group. Every device of the balanced layout holds whole histories in consecutive blocks, block_offset counting 0, 1, 2, ... within each: one history of 2 blocks and two of one block, in any order. `hist_length`: all blocks of a history carry its length; a history of n blocks has 128 * (n - 1) + 1 to 128 * n events, one of one block 64 or more.
All inputs are finite; a program needn't handle non-finite values.
Results may differ from a plain program's by a relative error of at most 0.01.
Values may be sent and summed in bfloat16 or wider, within the bound.
No kernel may reach another device: no remote copies, remote signals or barrier semaphores. Data moves between devices by JAX's collectives and lax.ppermute only.
A program may use at most 128 MiB of HBM per device.

v0:
```python
import math

import jax
import jax.numpy as jnp
from jax import lax
from jax.sharding import PartitionSpec as P

EPS = 1e-05


def normalize(vector):
    average = jnp.mean(vector, axis=-1, keepdims=True)
    centered = vector - average
    variance = jnp.mean(centered * centered, axis=-1, keepdims=True)
    return centered * lax.rsqrt(variance + EPS)


def silu_slope(inputs):
    sigmoid = jax.nn.sigmoid(inputs)
    return sigmoid * (1.0 + inputs * (1.0 - sigmoid))


def lookup(entries, indices):
    matches = indices[:, None] == jnp.arange(entries.shape[0], dtype=jnp.int32)[None, :]
    return jnp.sum(jnp.where(matches, entries[None, :], 0), axis=1)


def band_pairs(offsets):
    block_count = offsets.shape[0]
    window = block_count // 2
    total = block_count * window
    padded = -(-total // 16) * 16
    padding = padded - total
    owners = jnp.repeat(jnp.arange(block_count, dtype=jnp.int32), window)
    distance = jnp.tile(jnp.arange(window, dtype=jnp.int32), block_count)
    in_use = distance <= jnp.repeat(offsets, window)
    query_at = jnp.pad(jnp.where(in_use, owners, 0), (0, padding))
    key_at = jnp.pad(jnp.where(in_use, owners - distance, 0), (0, padding))
    return (query_at, key_at, jnp.pad(in_use, (0, padding)))


def tile_terms(offsets, lengths, rab, query_at, key_at, in_use, block_rows):
    row_ids = jnp.arange(block_rows, dtype=jnp.int32)
    query_pos = lookup(offsets, query_at)[:, None] * block_rows + row_ids[None, :]
    key_pos = lookup(offsets, key_at)[:, None] * block_rows + row_ids[None, :]
    limits = lookup(lengths, query_at)
    distance = query_pos[:, :, None] - key_pos[:, None, :]
    allowed = (
        (distance >= 0) & (query_pos[:, :, None] < limits[:, None, None]) & in_use[:, None, None]
    )
    rel_bias = (
        jnp.zeros((query_at.shape[0], rab.shape[0], block_rows, block_rows), jnp.float32)
        + rab[:, 0][None, :, None, None]
    )
    for bucket in range(1, rab.shape[1]):
        stride = rab[:, bucket] - rab[:, bucket - 1]
        reached = (distance >= 2 ** (bucket - 1)).astype(jnp.float32)
        rel_bias = rel_bias + stride[None, :, None, None] * reached[:, None, :, :]
    return (allowed[:, None, :, :], rel_bias)


def attend(queries, keys, values, offsets, lengths, rab, pairs):
    block_count, block_rows, features = queries.shape
    head_count = rab.shape[0]
    head_depth = features // head_count
    scaling = 1.0 / math.sqrt(head_depth)
    batched = tuple((member.reshape(-1, 16) for member in pairs))

    def advance(totals, element):
        query_at, key_at, in_use = element
        shape = (16, block_rows, head_count, head_depth)
        query_tile = queries[query_at].reshape(shape)
        key_tile = keys[key_at].reshape(shape)
        value_tile = values[key_at].reshape(shape)
        allowed, rel_bias = tile_terms(offsets, lengths, rab, query_at, key_at, in_use, block_rows)
        scores = (
            jnp.einsum("tiha,tjha->thij", query_tile, key_tile, preferred_element_type=jnp.float32)
            * scaling
            + rel_bias
        )
        weights = jnp.where(allowed, jax.nn.silu(scores), 0.0).astype(jnp.bfloat16)
        context = jnp.einsum(
            "thij,tjha->tiha", weights, value_tile, preferred_element_type=jnp.float32
        )
        return (totals.at[query_at].add(context.reshape(16, block_rows, features)), None)

    totals, _ = lax.scan(
        advance, jnp.zeros((block_count, block_rows, features), jnp.float32), batched
    )
    return totals


def attend_back(queries, keys, values, grad_context, offsets, lengths, rab, pairs):
    block_count, block_rows, features = queries.shape
    head_count = rab.shape[0]
    head_depth = features // head_count
    scaling = 1.0 / math.sqrt(head_depth)
    batched = tuple((member.reshape(-1, 16) for member in pairs))

    def advance(totals, element):
        query_at, key_at, in_use = element
        shape = (16, block_rows, head_count, head_depth)
        query_tile = queries[query_at].reshape(shape)
        key_tile = keys[key_at].reshape(shape)
        value_tile = values[key_at].reshape(shape)
        grad_tile = grad_context[query_at].reshape(shape)
        allowed, rel_bias = tile_terms(offsets, lengths, rab, query_at, key_at, in_use, block_rows)
        scores = (
            jnp.einsum("tiha,tjha->thij", query_tile, key_tile, preferred_element_type=jnp.float32)
            * scaling
            + rel_bias
        )
        weights = jnp.where(allowed, jax.nn.silu(scores), 0.0).astype(jnp.bfloat16)
        grad_weights = jnp.einsum(
            "tiha,tjha->thij", grad_tile, value_tile, preferred_element_type=jnp.float32
        )
        grad_scores = jnp.where(allowed, grad_weights * silu_slope(scores), 0.0).astype(
            jnp.bfloat16
        )
        grad_v = jnp.einsum(
            "thij,tiha->tjha", weights, grad_tile, preferred_element_type=jnp.float32
        )
        grad_q = (
            jnp.einsum("thij,tjha->tiha", grad_scores, key_tile, preferred_element_type=jnp.float32)
            * scaling
        )
        grad_k = (
            jnp.einsum(
                "thij,tiha->tjha", grad_scores, query_tile, preferred_element_type=jnp.float32
            )
            * scaling
        )
        sum_q, sum_k, sum_v = totals
        sum_q = sum_q.at[query_at].add(grad_q.reshape(16, block_rows, features))
        sum_k = sum_k.at[key_at].add(grad_k.reshape(16, block_rows, features))
        sum_v = sum_v.at[key_at].add(grad_v.reshape(16, block_rows, features))
        return ((sum_q, sum_k, sum_v), None)

    empty = jnp.zeros((block_count, block_rows, features), jnp.float32)
    totals, _ = lax.scan(advance, (empty, empty, empty), batched)
    return totals


def layer(inputs, upstream_raw, offsets, lengths, w_in, w_out, rab, pairs):
    block_count, block_rows, features = inputs.shape
    row_count = block_count * block_rows
    flat = inputs.reshape(row_count, features).astype(jnp.float32)
    normed_f, norm_back = jax.vjp(normalize, flat)
    normed = normed_f.astype(jnp.bfloat16)
    preact = jnp.dot(normed, w_in, preferred_element_type=jnp.float32)
    hidden = jax.nn.silu(preact).astype(jnp.bfloat16)
    gate_u = hidden[:, :features]
    values = hidden[:, features : 2 * features].reshape(block_count, block_rows, features)
    queries = hidden[:, 2 * features : 3 * features].reshape(block_count, block_rows, features)
    keys = hidden[:, 3 * features :].reshape(block_count, block_rows, features)
    context = attend(queries, keys, values, offsets, lengths, rab, pairs).reshape(
        row_count, features
    )

    def combine(context_in, gate_in):
        return normalize(context_in) * gate_in

    mixed_f, mix_back = jax.vjp(combine, context, gate_u.astype(jnp.float32))
    mixed = mixed_f.astype(jnp.bfloat16)
    row_ids = jnp.arange(block_rows, dtype=jnp.int32)
    valid_rows = (offsets[:, None] * block_rows + row_ids[None, :] < lengths[:, None]).reshape(
        row_count, 1
    )
    outputs = jnp.where(
        valid_rows, flat + jnp.dot(mixed, w_out, preferred_element_type=jnp.float32), 0.0
    ).astype(jnp.bfloat16)
    upstream = jnp.where(
        valid_rows, upstream_raw.reshape(row_count, features), jnp.zeros((), jnp.bfloat16)
    )
    grad_mixed = jnp.dot(upstream, w_out.T, preferred_element_type=jnp.float32)
    grad_context, grad_gate = mix_back(grad_mixed)
    grad_context_b = grad_context.astype(jnp.bfloat16).reshape(block_count, block_rows, features)
    grad_q, grad_k, grad_v = attend_back(
        queries, keys, values, grad_context_b, offsets, lengths, rab, pairs
    )
    joined = jnp.concatenate(
        [
            grad_gate,
            grad_v.reshape(row_count, features),
            grad_q.reshape(row_count, features),
            grad_k.reshape(row_count, features),
        ],
        axis=1,
    )
    grad_hidden = (joined * silu_slope(preact)).astype(jnp.bfloat16)
    grad_w_in = jnp.dot(normed.T, grad_hidden, preferred_element_type=jnp.float32)
    grad_w_out = jnp.dot(mixed.T, upstream, preferred_element_type=jnp.float32)
    (grad_normed,) = norm_back(jnp.dot(grad_hidden, w_in.T, preferred_element_type=jnp.float32))
    grad_inputs = (upstream.astype(jnp.float32) + grad_normed).astype(jnp.bfloat16)
    return (outputs, grad_inputs, grad_w_in, grad_w_out)


def body(events, route, block_offset, hist_length, cotangent, w_in, w_out, rab):
    members = lax.axis_size("member")
    piece_count = route.shape[0]
    block_count = block_offset.shape[0]
    row_count, features = events.shape
    piece_rows = row_count // piece_count
    block_rows = row_count // block_count
    capacity = max(1, piece_count // members)
    piece_ids = jnp.arange(piece_count, dtype=jnp.int32)
    target_dev = route // piece_count
    target_place = route % piece_count
    earlier = (target_dev[None, :] == target_dev[:, None]) & (
        piece_ids[None, :] < piece_ids[:, None]
    )
    order_in = jnp.sum(earlier.astype(jnp.int32), axis=1)
    slot_of = target_dev * capacity + order_in
    outgoing = (
        jnp.zeros((members * capacity, piece_rows, features), jnp.bfloat16)
        .at[slot_of]
        .set(events.reshape(piece_count, piece_rows, features))
    )
    labels = jnp.zeros((members * capacity,), jnp.int32).at[slot_of].set(target_place + 1)
    arrived, arrived_slots = (
        lax.all_to_all(outgoing, "member", split_axis=0, concat_axis=0, tiled=True),
        lax.all_to_all(labels, "member", split_axis=0, concat_axis=0, tiled=True),
    )
    matches = arrived_slots[None, :] == (piece_ids + 1)[:, None]
    cell_ids = jnp.arange(members * capacity, dtype=jnp.int32)
    source_cell = jnp.sum(jnp.where(matches, cell_ids[None, :], 0), axis=1)
    balanced = arrived[source_cell].reshape(block_count, block_rows, features)
    pairs = band_pairs(block_offset)
    upstream = cotangent.reshape(block_count, block_rows, features)
    outputs, grad_balanced, grad_in, grad_out = layer(
        balanced, upstream, block_offset, hist_length, w_in, w_out, rab, pairs
    )
    scaling = 1.0 / math.sqrt(row_count * lax.axis_size("group") * members)
    sum_in, sum_out = lax.psum((grad_in, grad_out), ("group", "member"))
    backward = (
        jnp.zeros((members * capacity, piece_rows, features), jnp.bfloat16)
        .at[source_cell]
        .set(grad_balanced.reshape(piece_count, piece_rows, features))
    )
    returned = lax.all_to_all(backward, "member", split_axis=0, concat_axis=0, tiled=True)
    events_grad = returned[slot_of].reshape(row_count, features)
    return (outputs, events_grad, sum_in * scaling, sum_out * scaling)


def solution(mesh):
    placed = (
        P(("group", "member"), None),
        P(("group", "member")),
        P(("group", "member")),
        P(("group", "member")),
        P(("group", "member"), None),
        P(),
        P(),
        P(),
    )
    return jax.shard_map(
        body,
        mesh=mesh,
        in_specs=placed,
        out_specs=(P(("group", "member"), None), P(("group", "member"), None), P(), P()),
        check_vma=False,
    )
```

profile of v0, /device:TPU:1, one launch (start us, length us, event | category | flops | bytes accessed | tf_op | source)
XLA Modules:
  0.0 365.1 jit_solution(9862523005863471971)
XLA Ops:
  7.2 0.8 fusion.19
  8.2 0.7 scatter_custom_fusion.1
  8.9 0.7 copy.70
  9.6 12.0 %all-to-all-start.1 = ((s32[64,1,1]{2,1,0:T(1,128)}), s32[64,1,1]{2,1,0:T(1,128)S(1)}, u32[]{:S(2)}, u32[]{:S(2)}) async-start(s32[64,1,1]{2,1,0:T(1,128)} %copy.70), calls=%async_computation.1 | async-start | bytes 65536 | tf_op jit(solution)/shard_map/all_to_all | solution.py:222
  21.5 1.5 slice_reduce_fusion.11
  23.1 0.7 broadcast_multiply_fusion.6
  23.8 0.7 broadcast_in_dim.335
  24.8 0.8 select_reduce_fusion.1
  25.8 0.7 fusion.18
  26.5 1.1 broadcast.462.clone
  27.6 4.8 %scatter_fusion = bf16[64,16,512]{2,1,0:T(8,128)(2,1)} fusion(bf16[64,16,512]{2,1,0:T(8,128)(2,1)} %broadcast.462.clone, s32[32]{0:T(128)S(1)} %compare_select_fusion.3, bf16[32,16,512]{2,1,0:T(8,128)(2,1)} %bitcast.108), kind=kCustom, calls=%fused_computation.6 | custom fusion | bytes 1572992 | tf_op jit(solution)/shard_map/scatter | solution.py:217
  32.4 10.0 %all-to-all-start = ((bf16[64,16,512]{2,1,0:T(8,128)(2,1)}), bf16[64,16,512]{2,1,0:T(8,128)(2,1)}, u32[]{:S(2)}, u32[]{:S(2)}) async-start(bf16[64,16,512]{2,1,0:T(8,128)(2,1)} %scatter_fusion), calls=%async_computation | async-start | bytes 2097152 | tf_op jit(solution)/shard_map/all_to_all | solution.py:221
  42.5 0.2 all-reduce.6.cloned.1.call-start
  42.7 5.3 %fusion.5 = (pred[16,128,128]{2,1,0:T(8,128)(4,1)S(1)}, f32[16,128,128]{2,1,0:T(8,128)}, f32[16,128,128]{2,1,0:T(8,128)}, f32[16,128,128]{2,1,0:T(8,128)}, f32[1...) fusion(s32[16,128]{1,0:T(8,128)S(1)} %iota_add_fusion, ...), kind=kLoop, calls=%fused_computation.54 | loop fusion | flops 6815744 | bytes 11814928 | tf_op jit(solution)/shard_map/while/body/eval_jaxpr/and | solution.py:49
  48.0 1.2 reduce.4
  49.4 9.1 %all-to-all-done = bf16[64,16,512]{2,1,0:T(8,128)(2,1)} async-done(((bf16[64,16,512]{2,1,0:T(8,128)(2,1)}), bf16[64,16,512]{2,1,0:T(8,128)(2,1)}, u32[]{:S(2)}, u32[]{:S(2)}) %all-to-all-start) | async-done | bytes 1048608 | tf_op jit(solution)/shard_map/all_to_all | solution.py:221
  58.5 1.8 gather_fusion
  60.5 0.3 multiply_reduce_fusion.3
  61.2 3.6 multiply_convert_fusion
  64.8 1.3 copy-done.11
  66.1 0.9 fusion.28
  67.1 3.1 gather_fusion.3
  70.1 3.9 %copy.73 = bf16[16,128,512]{1,2,0:T(8,128)(2,1)} copy(bf16[16,128,512]{2,1,0:T(8,128)(2,1)} %gather_fusion.3) | data formatting | bytes 4194304 | tf_op jit(solution)/shard_map/while/body/eval_jaxpr/gather | solution.py:73
  74.0 2.0 gather_fusion.2
  76.1 3.9 %copy.72 = bf16[16,128,512]{1,2,0:T(8,128)(2,1)} copy(bf16[16,128,512]{2,1,0:T(8,128)(2,1)} %gather_fusion.2) | data formatting | bytes 4194304 | tf_op jit(solution)/shard_map/while/body/eval_jaxpr/gather | solution.py:72
  80.0 2.0 gather_fusion.1
  82.0 4.0 %copy.71 = bf16[16,128,512]{1,2,0:T(8,128)(2,1)} copy(bf16[16,128,512]{2,1,0:T(8,128)(2,1)} %gather_fusion.1) | data formatting | bytes 4194304 | tf_op jit(solution)/shard_map/while/body/eval_jaxpr/gather | solution.py:74
  86.0 12.0 %select_convert_fusion.1 = (bf16[16,4,128,128]{3,2,1,0:T(8,128)(2,1)S(1)}, f32[16,4,128,128]{3,2,1,0:T(8,128)}) fusion(pred[16,128,128]{2,1,0:T(8,128)(4,1)S(1)} %get-tuple-element.105, f32[16,128,128]{2,1,0:T(8,128)S(1)} %copy-done.15, f32[4]{0:T(128)S(1)} %get-tuple-element.131, f32[16,128,128]{2,1,0:T(8,128)} %get-tuple-element.107, ...), kind=kOutput, calls=%fused_computation.28 | convolution fusion | flops 299892736 | bytes 22282432 | tf_op jit(solution)/shard_map/while/body/eval_jaxpr/tiha,tjha->thij/dot_general | solution.py:77
  98.1 3.5 fusion.32
  101.6 5.3 %copy.76 = f32[16,128,512]{2,1,0:T(8,128)} copy(f32[16,128,512]{1,2,0:T(8,128)} %bitcast.94) | data formatting | bytes 8388608 | tf_op jit(solution)/shard_map/while/body/eval_jaxpr/reshape | solution.py:85
  107.1 6.3 %scatter_fusion.1 = f32[4,128,512]{2,1,0:T(8,128)S(1)} fusion(f32[4,128,512]{2,1,0:T(8,128)S(1)} %broadcast.467.clone, s32[16]{0:T(128)S(1)} %get-tuple-element.146, f32[16,128,512]{2,1,0:T(8,128)} %copy.76), kind=kCustom, calls=%fused_computation.8 | custom fusion | flops 1048576 | bytes 12582976 | tf_op jit(solution)/shard_map/while/body/eval_jaxpr/scatter-add | solution.py:85
  113.5 0.3 multiply_reduce_fusion.2
  113.8 2.0 multiply_reduce_fusion.1
  115.8 2.9 fusion.27
  118.9 2.0 gather_fusion.4
  120.9 3.9 %copy.77 = bf16[16,128,512]{1,2,0:T(8,128)(2,1)} copy(bf16[16,128,512]{2,1,0:T(8,128)(2,1)} %gather_fusion.4) | data formatting | bytes 4194304 | tf_op jit(solution)/shard_map/while/body/eval_jaxpr/gather | solution.py:106
  124.9 5.2 %fusion.33 = f32[16,4,128,128]{3,2,1,0:T(8,128)} fusion(bf16[16,128,4,128]{1,3,2,0:T(8,128)(2,1)} %bitcast.105, bf16[16,4,128,128]{3,2,1,0:T(8,128)(2,1)} %copy-done.10), kind=kOutput, calls=%fused_computation.139 | convolution fusion | flops 268435456 | bytes 8388608 | tf_op jit(solution)/shard_map/while/body/eval_jaxpr/thij,tiha->tjha/dot_general | solution.py:120
  130.1 1.0 copy-done.18
  131.1 2.3 select_convert_fusion
  133.4 3.5 convolution_multiply_fusion.1
  136.9 2.7 convolution_multiply_fusion
  139.6 5.4 %copy.78 = f32[16,128,512]{2,1,0:T(8,128)} copy(f32[16,128,512]{1,2,0:T(8,128)} %bitcast.91) | data formatting | bytes 8388608 | tf_op jit(solution)/shard_map/while/body/eval_jaxpr/reshape | solution.py:136
  145.0 5.3 %copy.81 = f32[16,128,512]{2,1,0:T(8,128)} copy(f32[16,128,512]{1,2,0:T(8,128)} %bitcast.92) | data formatting | bytes 8388608 | tf_op jit(solution)/shard_map/while/body/eval_jaxpr/reshape | solution.py:134
  150.3 5.3 %copy.82 = f32[16,128,512]{2,1,0:T(8,128)} copy(f32[16,128,512]{1,2,0:T(8,128)} %bitcast.93) | data formatting | bytes 8388608 | tf_op jit(solution)/shard_map/while/body/eval_jaxpr/reshape | solution.py:135
  155.8 6.1 %scatter_fusion.2 = f32[4,128,512]{2,1,0:T(8,128)S(1)} fusion(f32[4,128,512]{2,1,0:T(8,128)S(1)} %broadcast.467.clone.3, s32[16]{0:T(128)S(1)} %get-tuple-element.133, f32[16,128,512]{2,1,0:T(8,128)} %copy.78), kind=kCustom, calls=%fused_computation.9 | custom fusion | flops 1048576 | bytes 12582976 | tf_op jit(solution)/shard_map/while/body/eval_jaxpr/scatter-add | solution.py:136
  161.9 1.3 broadcast.467.clone.2
  163.3 9.1 %scatter_fusion.3 = f32[4,128,512]{2,1,0:T(8,128)} fusion(f32[4,128,512]{2,1,0:T(8,128)} %broadcast.467.clone.2, s32[16]{0:T(128)S(1)} %get-tuple-element.146, f32[16,128,512]{2,1,0:T(8,128)} %copy.81), kind=kCustom, calls=%fused_computation.10 | custom fusion | flops 1048576 | bytes 12582976 | tf_op jit(solution)/shard_map/while/body/eval_jaxpr/scatter-add | solution.py:134
  172.5 6.1 %scatter_fusion.4 = f32[4,128,512]{2,1,0:T(8,128)S(1)} fusion(f32[4,128,512]{2,1,0:T(8,128)S(1)} %broadcast.467.clone.1, s32[16]{0:T(128)S(1)} %get-tuple-element.133, f32[16,128,512]{2,1,0:T(8,128)} %copy.82), kind=kCustom, calls=%fused_computation.11 | custom fusion | flops 1048576 | bytes 12582976 | tf_op jit(solution)/shard_map/while/body/eval_jaxpr/scatter-add | solution.py:135
  178.6 4.2 %fusion = bf16[512,2048]{1,0:T(8,128)(2,1)S(1)} fusion(f32[512,512]{1,0:T(8,128)S(1)} %bitcast.88, f32[512,512]{1,0:T(8,128)} %bitcast.24, f32[512,512]{1,0:T(8,128)} %bitcast.89, f32[512,512]{1,0:T(8,128)} %get-tuple-element.101, f32[512,2048]{1,0:T(8,128)} %get-tuple-element.139), kind=kLoop, calls=%fused_computation.26 | loop fusion | flops 12582912 | bytes 10485760 | tf_op jit(solution)/shard_map/convert_element_type | solution.py:190
  182.9 1.3 copy-done.4
  184.2 3.3 fusion.34
  187.5 1.5 fusion.24
  189.0 3.0 multiply_reduce_fusion
  192.0 0.4 fusion.26
  192.5 1.3 add_convert_fusion
  193.7 1.1 broadcast.462
  194.8 5.0 %scatter_fusion.5 = bf16[64,16,512]{2,1,0:T(8,128)(2,1)} fusion(bf16[64,16,512]{2,1,0:T(8,128)(2,1)} %broadcast.462, s32[32]{0:T(128)S(1)} %fusion.20, bf16[32,16,512]{2,1,0:T(8,128)(2,1)} %bitcast.107), kind=kCustom, calls=%fused_computation.12 | custom fusion | bytes 1572992 | tf_op jit(solution)/shard_map/scatter | solution.py:238
  199.9 6.3 %all-to-all-start.2 = ((bf16[64,16,512]{2,1,0:T(8,128)(2,1)}), bf16[64,16,512]{2,1,0:T(8,128)(2,1)}, u32[]{:S(2)}, u32[]{:S(2)}) async-start(bf16[64,16,512]{2,1,0:T(8,128)(2,1)} %scatter_fusion.5), calls=%async_computation.2 | async-start | bytes 2097152 | tf_op jit(solution)/shard_map/all_to_all | solution.py:240
  206.2 2.5 fusion.2
  208.6 15.9 %all-to-all-done.2 = bf16[64,16,512]{2,1,0:T(8,128)(2,1)} async-done(((bf16[64,16,512]{2,1,0:T(8,128)(2,1)}), bf16[64,16,512]{2,1,0:T(8,128)(2,1)}, u32[]{:S(2)}, u32[]{:S(2)}) %all-to-all-start.2) | async-done | bytes 1048608 | tf_op jit(solution)/shard_map/all_to_all | solution.py:240
  224.5 2.6 gather_fusion.5
  227.1 125.2 %all-reduce.6.cloned.1.call-done = (f32[512,2048]{1,0:T(8,128)}, f32[512,512]{1,0:T(8,128)}) async-done(((f32[512,2048]{1,0:T(8,128)}, f32[512,512]{1,0:T(8,128)}), (f32[512,2048]{1,0:T(8,128)}, f32[512,512]{1,0:T(8,128)})) %all-reduce.6.cloned.1.call-update) | async-done | bytes 5242896 | tf_op jit(solution)/shard_map/psum | solution.py:234
  352.3 4.9 %broadcast_multiply_fusion = f32[512,2048]{1,0:T(8,128)} fusion(f32[512,2048]{1,0:T(8,128)} %get-tuple-element.80), kind=kLoop, calls=%fused_computation.35 | loop fusion | flops 1048576 | bytes 8388608 | tf_op jit(solution)/shard_map/mul | solution.py:242
  357.2 1.1 broadcast_multiply_fusion.1
  (78 shorter events, 2.4 us)
Async XLA Ops:
  7.2 54.0 %copy-start = (bf16[512,2048]{1,0:T(8,128)(2,1)S(1)}, bf16[512,2048]{1,0:T(8,128)(2,1)}, u32[]{:S(2)}) copy-start(bf16[512,2048]{1,0:T(8,128)(2,1)} %param.13) | copy-start | bytes 6291460
  9.6 22.9 %all-to-all-start.1 = ((s32[64,1,1]{2,1,0:T(1,128)}), s32[64,1,1]{2,1,0:T(1,128)S(1)}, u32[]{:S(2)}, u32[]{:S(2)}) async-start(s32[64,1,1]{2,1,0:T(1,128)} %copy.70), calls=%async_computation.1 | async-start | bytes 65536 | tf_op jit(solution)/shard_map/all_to_all | solution.py:222
  32.4 26.0 %all-to-all-start = ((bf16[64,16,512]{2,1,0:T(8,128)(2,1)}), bf16[64,16,512]{2,1,0:T(8,128)(2,1)}, u32[]{:S(2)}, u32[]{:S(2)}) async-start(bf16[64,16,512]{2,1,0:T(8,128)(2,1)} %scatter_fusion), calls=%async_computation | async-start | bytes 2097152 | tf_op jit(solution)/shard_map/all_to_all | solution.py:221
  42.5 309.9 %all-reduce.6.cloned.1.call-start = ((), (), s32[]{:S(2)}) async-start(), calls=%async_computation.3 | async-start | bytes 10485760 | tf_op jit(solution)/shard_map/psum | solution.py:234
  60.3 4.5 %copy-start.2 = (bf16[32,16,512]{2,1,0:T(8,128)(2,1)}, bf16[32,16,512]{2,1,0:T(8,128)(2,1)S(1)}, u32[]{:S(2)}) copy-start(bf16[32,16,512]{2,1,0:T(8,128)(2,1)S(1)} %gather_fusion) | copy-start | bytes 1572868
  61.2 3.6 copy-start.13
  64.8 1.4 copy-start.11
  82.0 4.0 %copy-start.15 = (f32[16,128,128]{2,1,0:T(8,128)S(1)}, f32[16,128,128]{2,1,0:T(8,128)}, u32[]{:S(2)}) copy-start(f32[16,128,128]{2,1,0:T(8,128)} %get-tuple-element.106) | copy-start | bytes 3145732
  86.0 12.0 %copy-start.7 = (bf16[16,128,512]{1,2,0:T(8,128)(2,1)S(1)}, bf16[16,128,512]{1,2,0:T(8,128)(2,1)}, u32[]{:S(2)}) copy-start(bf16[16,128,512]{1,2,0:T(8,128)(2,1)} %copy.71) | copy-start | bytes 6291460
  98.1 3.6 copy-start.10
  124.9 5.2 %copy-start.8 = (bf16[16,128,512]{1,2,0:T(8,128)(2,1)S(1)}, bf16[16,128,512]{1,2,0:T(8,128)(2,1)}, u32[]{:S(2)}) copy-start(bf16[16,128,512]{1,2,0:T(8,128)(2,1)} %copy.71) | copy-start | bytes 6291460
  124.9 5.2 %copy-start.9 = (bf16[16,128,512]{1,2,0:T(8,128)(2,1)S(1)}, bf16[16,128,512]{1,2,0:T(8,128)(2,1)}, u32[]{:S(2)}) copy-start(bf16[16,128,512]{1,2,0:T(8,128)(2,1)} %copy.77) | copy-start | bytes 6291460
  124.9 6.2 %copy-start.18 = (f32[16,4,128,128]{3,2,1,0:T(8,128)S(1)}, f32[16,4,128,128]{3,2,1,0:T(8,128)}, u32[]{:S(2)}) copy-start(f32[16,4,128,128]{3,2,1,0:T(8,128)} %get-tuple-element.141) | copy-start | bytes 12582916
  131.1 2.3 copy-start.5
  133.4 3.5 copy-start.6
  161.9 1.4 copy-start.1
  178.6 5.6 %copy-start.14 = (bf16[512,512]{1,0:T(8,128)(2,1)S(1)}, bf16[512,512]{1,0:T(8,128)(2,1)}, u32[]{:S(2)}) copy-start(bf16[512,512]{1,0:T(8,128)(2,1)} %copy-done.13) | copy-start | bytes 1572868
  182.9 1.3 copy-start.4
  184.2 3.3 copy-start.12
  184.2 3.3 copy-start.17
  187.5 1.5 copy-start.3
  199.9 24.6 %all-to-all-start.2 = ((bf16[64,16,512]{2,1,0:T(8,128)(2,1)}), bf16[64,16,512]{2,1,0:T(8,128)(2,1)}, u32[]{:S(2)}, u32[]{:S(2)}) async-start(bf16[64,16,512]{2,1,0:T(8,128)(2,1)} %scatter_fusion.5), calls=%async_computation.2 | async-start | bytes 2097152 | tf_op jit(solution)/shard_map/all_to_all | solution.py:240
  352.3 4.9 %copy-start.16 = (f32[512,512]{1,0:T(8,128)S(1)}, f32[512,512]{1,0:T(8,128)}, u32[]{:S(2)}) copy-start(f32[512,512]{1,0:T(8,128)} %get-tuple-element.81) | copy-start | bytes 3145732
Sparse Core Ops, SparseCore 0:
  189.1 163.1 all-reduce.5
where the time goes:
time: 367 us; the launch traced here: 365 us
  waiting for transfers between devices  150 us (41%)
  local copies, waits for them, and re-layouts  73.2 us (20%)
  other arithmetic  53.7 us (15%)
  matrix products  45.1 us (12%)
  starting transfers between devices  28.5 us (8%)
  between operations  14.4 us (4%)
    psum x1, waiting for transfers between devices, body(): sum_in, sum_out = lax.psum((grad_in, grad_out), ('group', 'member'))  125 us
    all_to_all x1, waiting for transfers between devices, body(): lax.all_to_all(backward, 'member', split_axis=0, concat_axis=0, tiled=True)  15.9 us
    dot_general x1, matrix products, advance(): jnp.einsum('tiha,tjha->thij', query_tile, key_tile, preferred_element_typ...  12 us
    all_to_all x1, starting transfers between devices, body(): lax.all_to_all(labels, 'member', split_axis=0, concat_axis=0, tiled=True)  12 us
    all_to_all x1, starting transfers between devices, body(): lax.all_to_all(outgoing, 'member', split_axis=0, concat_axis=0, tiled=True)  10 us
    scatter-add x1, other arithmetic, advance(): sum_q = sum_q.at[query_at].add(grad_q.reshape(16, block_rows, features))  9.12 us
    all_to_all x1, waiting for transfers between devices, body(): lax.all_to_all(outgoing, 'member', split_axis=0, concat_axis=0, tiled=True)  9.07 us
  transfers between devices with their start and end apart: 4, of which 3 were waited for; matrix products, arithmetic and copies ran while one was open for 9% of the time, Pallas kernels for 0%

commit v1 on v0

v1 whole, which is shorter than its diff:
```python
import functools
import math

import jax
import jax.numpy as jnp
from jax import lax
from jax.experimental import pallas as pl
from jax.experimental.pallas import tpu as pltpu
from jax.sharding import PartitionSpec as P

EPS = 1e-05
BF16 = jnp.bfloat16
F32 = jnp.float32
VMEM_LIMIT = 48 * 1024 * 1024

ROWS, D, HID = 512, 512, 2048
BLOCK, BLOCKS, HEADS, BUCKETS = 128, 4, 4, 12
PIECE, PIECES, MEMBERS = 16, 32, 64
LABEL = 128
CHUNK = 640
SCALE = 1.0 / math.sqrt(128)


def dot(a, b):
    return jnp.dot(a, b, preferred_element_type=F32)


def dot_nt(a, b):
    return lax.dot_general(a, b, (((1,), (1,)), ((), ())), preferred_element_type=F32)


def dot_tn(a, b):
    return lax.dot_general(a, b, (((0,), (0,)), ((), ())), preferred_element_type=F32)


def sigmoid(v):
    return 0.5 * jnp.tanh(0.5 * v) + 0.5


def full_spec(memory=pltpu.VMEM):
    return pl.BlockSpec(memory_space=memory)


def pack_kernel(route_ref, events_ref, out_ref):
    out_ref[...] = jnp.zeros_like(out_ref)
    for j in range(PIECES):
        target = route_ref[j]
        device = lax.shift_right_logical(target, 5)
        place = lax.bitwise_and(target, PIECES - 1)
        out_ref[device, :, :D] = events_ref[j * PIECE : (j + 1) * PIECE, :]
        label = jnp.full((PIECE, LABEL), (place + 1).astype(F32), F32)
        out_ref[device, :, D:] = label.astype(BF16)


def pack(route, events):
    return pl.pallas_call(
        pack_kernel,
        out_shape=jax.ShapeDtypeStruct((MEMBERS, PIECE, D + LABEL), BF16),
        in_specs=[full_spec(pltpu.SMEM), full_spec()],
        out_specs=full_spec(),
        compiler_params=pltpu.CompilerParams(vmem_limit_bytes=VMEM_LIMIT),
        name="pack_pieces",
    )(route, events)


def layer_kernel(
    core_ref,
    offset_ref,
    length_ref,
    rab_ref,
    arrived_ref,
    cot_ref,
    w_in_ref,
    w_out_ref,
    out_ref,
    own_ref,
    other_ref,
    back_ref,
    place_s,
    bal_s,
    norm_s,
    xhat_s,
    rstd_s,
    hid_s,
    slope_s,
    att_s,
    asl_s,
    ctx_s,
    gm_s,
    mixed_s,
    up_s,
    gctx_s,
    g_s,
    gh_s,
    normt_s,
    gb_s,
):
    core = core_ref[0]
    pick = (lax.broadcasted_iota(jnp.int32, (8, LABEL), 1) == 0).astype(BF16)
    labels = dot_nt(pick, arrived_ref[:, D:])[0:1, :]
    cell_row = lax.bitwise_and(
        lax.broadcasted_iota(jnp.int32, (1, MEMBERS * PIECE), 1), PIECE - 1
    ).astype(F32)
    goal = (labels - 1.0) * PIECE + cell_row
    for b in range(BLOCKS):
        rows = lax.broadcasted_iota(jnp.int32, (BLOCK, 1), 0).astype(F32) + float(b * BLOCK)
        place_s[b * BLOCK : (b + 1) * BLOCK, :] = jnp.where(goal == rows, 1.0, 0.0).astype(BF16)
    for n in range(0, D, 256):
        bal_s[:, n : n + 256] = dot(place_s[...], arrived_ref[:, n : n + 256]).astype(BF16)

    for r in range(0, ROWS, 64):
        sl = slice(r, r + 64)
        x = bal_s[sl, :].astype(F32)
        centered = x - jnp.mean(x, axis=-1, keepdims=True)
        variance = jnp.mean(centered * centered, axis=-1, keepdims=True)
        rstd = lax.rsqrt(variance + EPS)
        xhat = centered * rstd
        xhat_s[sl, :] = xhat
        rstd_s[sl, :] = jnp.broadcast_to(rstd, (64, 128))
        norm_s[sl, :] = xhat.astype(BF16)

    for n in range(0, HID, 256):
        cols = slice(n, n + 256)
        v = dot(norm_s[...], w_in_ref[:, cols])
        g = sigmoid(v)
        h = v * g
        hid_s[:, cols] = h.astype(BF16)
        slope_s[:, cols] = g + h * (1.0 - g)

    row_id = lax.broadcasted_iota(jnp.int32, (BLOCK, BLOCK), 0)
    col_id = lax.broadcasted_iota(jnp.int32, (BLOCK, BLOCK), 1)

    def bias(head, distance):
        total = jnp.full((BLOCK, BLOCK), rab_ref[head, 0], F32)
        for bucket in range(1, 9):
            total = jnp.where(distance >= 2 ** (bucket - 1), rab_ref[head, bucket], total)
        return total

    def head_cols(part, head):
        return slice(part * D + head * 128, part * D + head * 128 + 128)

    second = jnp.int32(0)
    for b in range(1, BLOCKS):
        second = jnp.where(offset_ref[b] == 1, b, second)
    first = jnp.maximum(second - 1, 0)
    second_rows = pl.ds(pl.multiple_of(second * BLOCK, BLOCK), BLOCK)
    first_rows = pl.ds(pl.multiple_of(first * BLOCK, BLOCK), BLOCK)

    def live_rows(block):
        position = row_id + offset_ref[block] * BLOCK
        return position < length_ref[block]

    def attend(q_rows, k_rows, allowed, relative, head, tile):
        q = hid_s[q_rows, head_cols(2, head)]
        k = hid_s[k_rows, head_cols(3, head)]
        s = dot_nt(q, k) * SCALE + relative
        g = sigmoid(s)
        a = s * g
        asl_s[tile, head] = jnp.where(allowed, g + a * (1.0 - g), 0.0)
        a = jnp.where(allowed, a, 0.0).astype(BF16)
        att_s[tile, head] = a
        return dot(a, hid_s[k_rows, head_cols(1, head)])

    own_distance = row_id - col_id
    for head in range(HEADS):
        relative = bias(head, own_distance)
        for b in range(BLOCKS):
            rows = slice(b * BLOCK, (b + 1) * BLOCK)
            allowed = (own_distance >= 0) & live_rows(b)
            ctx_s[rows, head_cols(0, head)] = attend(rows, rows, allowed, relative, head, b)
    far_allowed = live_rows(second)
    for head in range(HEADS):
        relative = bias(head, own_distance + BLOCK)
        cols = head_cols(0, head)
        ctx_s[second_rows, cols] += attend(
            second_rows, first_rows, far_allowed, relative, head, BLOCKS
        )

    for b in range(BLOCKS):
        rows = slice(b * BLOCK, (b + 1) * BLOCK)
        live = (
            lax.broadcasted_iota(jnp.int32, (BLOCK, 1), 0) + offset_ref[b] * BLOCK < length_ref[b]
        )
        up_s[rows, :] = jnp.where(live, cot_ref[rows, :].astype(F32), 0.0).astype(BF16)
    gm_s[...] = dot_nt(up_s[...], w_out_ref[...])
    for r in range(0, ROWS, 64):
        sl = slice(r, r + 64)
        c = ctx_s[sl, :]
        centered = c - jnp.mean(c, axis=-1, keepdims=True)
        variance = jnp.mean(centered * centered, axis=-1, keepdims=True)
        rstd = lax.rsqrt(variance + EPS)
        n = centered * rstd
        u = hid_s[sl, 0:D].astype(F32)
        mixed_s[sl, :] = (n * u).astype(BF16)
        gm = gm_s[sl, :]
        gh_s[sl, 0:D] = (gm * n * slope_s[sl, 0:D]).astype(BF16)
        gn = gm * u
        gctx = rstd * (
            gn
            - jnp.mean(gn, axis=-1, keepdims=True)
            - n * jnp.mean(gn * n, axis=-1, keepdims=True)
        )
        gctx_s[sl, :] = gctx.astype(BF16)
    gm_s[...] = dot(mixed_s[...], w_out_ref[...])
    for b in range(BLOCKS):
        rows = slice(b * BLOCK, (b + 1) * BLOCK)
        live = (
            lax.broadcasted_iota(jnp.int32, (BLOCK, 1), 0) + offset_ref[b] * BLOCK < length_ref[b]
        )
        out_ref[rows, :] = jnp.where(live, bal_s[rows, :].astype(F32) + gm_s[rows, :], 0.0).astype(
            BF16
        )

    def attend_back(q_rows, k_rows, head, tile):
        gc = gctx_s[q_rows, head_cols(0, head)]
        q = hid_s[q_rows, head_cols(2, head)]
        k = hid_s[k_rows, head_cols(3, head)]
        v = hid_s[k_rows, head_cols(1, head)]
        ds = (dot_nt(gc, v) * asl_s[tile, head]).astype(BF16)
        gv = dot_tn(att_s[tile, head], gc)
        gq = dot(ds, k) * SCALE
        gk = dot_tn(ds, q) * SCALE
        return gv, gq, gk

    for head in range(HEADS):
        for b in range(BLOCKS):
            rows = slice(b * BLOCK, (b + 1) * BLOCK)
            gv, gq, gk = attend_back(rows, rows, head, b)
            g_s[rows, head_cols(0, head)] = gv
            g_s[rows, head_cols(1, head)] = gq
            g_s[rows, head_cols(2, head)] = gk
    for head in range(HEADS):
        gv, gq, gk = attend_back(second_rows, first_rows, head, BLOCKS)
        g_s[first_rows, head_cols(0, head)] += gv
        g_s[second_rows, head_cols(1, head)] += gq
        g_s[first_rows, head_cols(2, head)] += gk
    for r in range(0, ROWS, 64):
        sl = slice(r, r + 64)
        for n in range(0, 3 * D, D):
            gh_s[sl, D + n : 2 * D + n] = (
                g_s[sl, n : n + D] * slope_s[sl, D + n : 2 * D + n]
            ).astype(BF16)

    normt_s[...] = norm_s[...].T

    def store(quarter, start, value):
        half, side = quarter // 2, quarter % 2
        value = value.astype(BF16).reshape(PIECES, PIECE, value.shape[1])
        stop = start + value.shape[2]

        @pl.when(core == half)
        def _():
            own_ref[:, side, :, start:stop] = value

        @pl.when(core != half)
        def _():
            other_ref[:, side, :, start:stop] = value

    for quarter in range(4):
        for n in range(0, CHUNK, 128):
            at = quarter * CHUNK + n
            if at < HID:
                store(quarter, n, dot(normt_s[...], gh_s[:, at : at + 128]))
    normt_s[...] = mixed_s[...].T
    store(3, 128, dot(normt_s[...], up_s[...]))

    gm_s[...] = dot_nt(gh_s[...], w_in_ref[...])
    for r in range(0, ROWS, 64):
        sl = slice(r, r + 64)
        gx = gm_s[sl, :]
        xhat = xhat_s[sl, :]
        rstd = rstd_s[sl, 0:1]
        gx = rstd * (
            gx
            - jnp.mean(gx, axis=-1, keepdims=True)
            - xhat * jnp.mean(gx * xhat, axis=-1, keepdims=True)
        )
        gb_s[sl, :] = (up_s[sl, :].astype(F32) + gx).astype(BF16)
    for n in range(0, D, 256):
        back_ref[:, n : n + 256] = dot_tn(place_s[...], gb_s[:, n : n + 256]).astype(BF16)


def layer(core, offsets, lengths, rab, arrived, cotangent, w_in, w_out):
    half = jax.ShapeDtypeStruct((PIECES, 2, PIECE, CHUNK), BF16)
    scratch = [
        ((ROWS, MEMBERS * PIECE), BF16),
        ((ROWS, D), BF16),
        ((ROWS, D), BF16),
        ((ROWS, D), F32),
        ((ROWS, 128), F32),
        ((ROWS, HID), BF16),
        ((ROWS, HID), F32),
        ((BLOCKS + 1, HEADS, BLOCK, BLOCK), BF16),
        ((BLOCKS + 1, HEADS, BLOCK, BLOCK), F32),
        ((ROWS, D), F32),
        ((ROWS, D), F32),
        ((ROWS, D), BF16),
        ((ROWS, D), BF16),
        ((ROWS, D), BF16),
        ((ROWS, 3 * D), F32),
        ((ROWS, HID), BF16),
        ((ROWS, D), BF16),
        ((ROWS, D), BF16),
    ]
    return pl.pallas_call(
        layer_kernel,
        out_shape=(
            jax.ShapeDtypeStruct((ROWS, D), BF16),
            half,
            half,
            jax.ShapeDtypeStruct((MEMBERS * PIECE, D), BF16),
        ),
        in_specs=[full_spec(pltpu.SMEM)] * 4 + [full_spec()] * 4,
        out_specs=(full_spec(),) * 4,
        scratch_shapes=[pltpu.VMEM(shape, kind) for shape, kind in scratch],
        compiler_params=pltpu.CompilerParams(vmem_limit_bytes=VMEM_LIMIT),
        cost_estimate=pl.CostEstimate(
            flops=5_000_000_000, bytes_accessed=9_000_000, transcendentals=1_500_000
        ),
        name="layer",
    )(core, offsets, lengths, rab, arrived, cotangent, w_in, w_out)


def join_kernel(own_ref, got_ref, back_ref, out_ref):
    out_ref[:, :, :CHUNK] = (own_ref[...].astype(F32) + got_ref[...].astype(F32)).astype(BF16)
    out_ref[:, :, CHUNK:] = back_ref[...]


def join(own, got, back):
    step = 16
    spec = lambda width: pl.BlockSpec((step, PIECE, width), lambda i: (i, 0, 0))
    return pl.pallas_call(
        join_kernel,
        out_shape=jax.ShapeDtypeStruct((MEMBERS, PIECE, CHUNK + D), BF16),
        grid=(MEMBERS // step,),
        in_specs=[spec(CHUNK), spec(CHUNK), spec(D)],
        out_specs=spec(CHUNK + D),
        compiler_params=pltpu.CompilerParams(vmem_limit_bytes=VMEM_LIMIT),
        name="join",
    )(own, got, back)


def total_kernel(route_ref, mixed_ref, share_ref, events_ref):
    total = mixed_ref[0, :, :CHUNK].astype(F32)
    for m in range(1, MEMBERS):
        total += mixed_ref[m, :, :CHUNK].astype(F32)
    total = (total * (1.0 / 256.0)).astype(BF16)
    share_ref[...] = jnp.broadcast_to(total[None], (MEMBERS, PIECE, CHUNK))
    for j in range(PIECES):
        device = lax.shift_right_logical(route_ref[j], 5)
        events_ref[j * PIECE : (j + 1) * PIECE, :] = mixed_ref[device, :, CHUNK:]


def total(route, received):
    return pl.pallas_call(
        total_kernel,
        out_shape=(
            jax.ShapeDtypeStruct((MEMBERS, PIECE, CHUNK), BF16),
            jax.ShapeDtypeStruct((ROWS, D), BF16),
        ),
        in_specs=[full_spec(pltpu.SMEM), full_spec()],
        out_specs=(full_spec(),) * 2,
        compiler_params=pltpu.CompilerParams(vmem_limit_bytes=VMEM_LIMIT),
        name="total",
    )(route, received)


def spread_kernel(core_ref, own_ref, other_ref, w_in_ref, w_out_ref):
    core = core_ref[0]
    rows = w_in_ref.shape[0]

    def put(source, half):
        for side in range(2):
            value = source[:, side].astype(F32).reshape(rows, CHUNK)
            at = (2 * half + side) * CHUNK
            keep = min(CHUNK, HID - at)
            w_in_ref[:, at : at + keep] = value[:, :keep]
            if keep < CHUNK:
                w_out_ref[...] = value[:, keep:]

    @pl.when(core == 0)
    def _():
        put(own_ref, 0)
        put(other_ref, 1)

    @pl.when(core != 0)
    def _():
        put(other_ref, 0)
        put(own_ref, 1)


def spread(core, own, other):
    step = 8
    shape = (PIECES, 2, PIECE, CHUNK)
    half = pl.BlockSpec((step, 2, PIECE, CHUNK), lambda i: (i, 0, 0, 0))
    rows = step * PIECE
    return pl.pallas_call(
        spread_kernel,
        out_shape=(
            jax.ShapeDtypeStruct((D, HID), F32),
            jax.ShapeDtypeStruct((D, D), F32),
        ),
        grid=(PIECES // step,),
        in_specs=[full_spec(pltpu.SMEM), half, half],
        out_specs=(
            pl.BlockSpec((rows, HID), lambda i: (i, 0)),
            pl.BlockSpec((rows, D), lambda i: (i, 0)),
        ),
        compiler_params=pltpu.CompilerParams(vmem_limit_bytes=VMEM_LIMIT),
        name="spread",
    )(core, own.reshape(shape), other.reshape(shape))


def body(events, route, block_offset, hist_length, cotangent, w_in, w_out, rab):
    core = lax.axis_index("group").astype(jnp.int32).reshape(1)
    exchange = functools.partial(
        lax.all_to_all, axis_name="member", split_axis=0, concat_axis=0, tiled=True
    )
    swap = functools.partial(lax.ppermute, axis_name="group", perm=[(0, 1), (1, 0)])
    arrived = exchange(pack(route, events))
    outputs, own, other, back = layer(
        core,
        block_offset,
        hist_length,
        rab,
        arrived.reshape(MEMBERS * PIECE, D + LABEL),
        cotangent,
        w_in,
        w_out,
    )
    got = swap(other)
    slots = (MEMBERS, PIECE, CHUNK)
    received = exchange(
        join(own.reshape(slots), got.reshape(slots), back.reshape(MEMBERS, PIECE, D))
    )
    share, events_grad = total(route, received)
    mine = exchange(share)
    theirs = swap(mine)
    w_in_grad, w_out_grad = spread(core, mine, theirs)
    return outputs, events_grad, w_in_grad, w_out_grad


def solution(mesh):
    placed = (
        P(("group", "member"), None),
        P(("group", "member")),
        P(("group", "member")),
        P(("group", "member")),
        P(("group", "member"), None),
        P(),
        P(),
        P(),
    )
    return jax.shard_map(
        body,
        mesh=mesh,
        in_specs=placed,
        out_specs=(P(("group", "member"), None), P(("group", "member"), None), P(), P()),
        check_vma=False,
    )
```

time: 367 us -> 134 us (0.37)
  waiting for transfers between devices: 150 us -> 24.6 us
  local copies, waits for them, and re-layouts: 73.2 us -> 1.72 us
  blocking collectives: 0 us -> 59.5 us
  other arithmetic: 53.7 us -> 0 us
  matrix products: 45.1 us -> 0 us
  Pallas kernels: 0 us -> 28.3 us
  between operations: 14.4 us -> 0.71 us
  starting transfers between devices: 28.5 us -> 19.3 us
    psum x1 -> x0, waiting for transfers between devices: 125 us -> none  [body(): sum_in, sum_out = lax.psum((grad_in, grad_out), ('group', 'member'))]
    all_to_all x0 -> x2, blocking collectives: none -> 59.5 us  [the longest x1 35.8 us: body(): exchange(join(own.reshape(slots), got.reshape(slots), back.reshape(MEMBER...]
    dot_general x12 -> x0, matrix products: 45.1 us -> none  [the longest x1 12 us: advance(): jnp.einsum('tiha,tjha->thij', query_tile, key_tile, preferred_element_typ...]
    gather x10 -> x0, local copies, waits for them, and re-layouts: 29.3 us -> none  [the longest x2 6.96 us: advance(): key_tile = keys[key_at].reshape(shape)]
    pallas_call x0 -> x5, Pallas kernels: none -> 28.3 us  [the longest x1 22 us: layer(): pl.pallas_call(layer_kernel, out_shape=(jax.ShapeDtypeStruct((ROWS, D), B...]
    scatter-add x4 -> x0, other arithmetic: 27.6 us -> none  [the longest x1 9.12 us: advance(): sum_q = sum_q.at[query_at].add(grad_q.reshape(16, block_rows, features))]
    reshape x6 -> x0, local copies, waits for them, and re-layouts: 21.6 us -> none  [the longest x1 5.37 us: advance(): sum_v = sum_v.at[key_at].add(grad_v.reshape(16, block_rows, features))]
    all_to_all x3 -> x1, starting transfers between devices: 28.3 us -> 12.1 us  [body(): arrived = exchange(pack(route, events))]
  transfers between devices with their start and end apart: 4 -> 3, of which waited for: 3 -> 3; matrix products, arithmetic and copies ran while one was open for 9% -> 0% of each run, Pallas kernels for 0% -> 0%
where the time goes in v1:
time: 134 us
  blocking collectives  59.5 us (44%)
  Pallas kernels  28.3 us (21%)
  waiting for transfers between devices  24.6 us (18%)
  starting transfers between devices  19.3 us (14%)
  local copies, waits for them, and re-layouts  1.72 us (1%)
    all_to_all x1, blocking collectives, body(): exchange(join(own.reshape(slots), got.reshape(slots), back.reshape(MEMBER...  35.8 us
    all_to_all x1, blocking collectives, body(): mine = exchange(share)  23.6 us
    pallas_call x1, Pallas kernels, layer(): pl.pallas_call(layer_kernel, out_shape=(jax.ShapeDtypeStruct((ROWS, D), B...  22 us
    all_to_all x1, waiting for transfers between devices, body(): arrived = exchange(pack(route, events))  19.3 us
    all_to_all x1, starting transfers between devices, body(): arrived = exchange(pack(route, events))  12.1 us
    ppermute x1, starting transfers between devices, body(): theirs = swap(mine)  4.07 us
    ppermute x1, starting transfers between devices, body(): got = swap(other)  3.14 us
    pallas_call x1, Pallas kernels, spread(): pl.pallas_call(spread_kernel, out_shape=(jax.ShapeDtypeStruct((D, HID), F...  2.7 us
  transfers between devices with their start and end apart: 3, of which 3 were waited for; matrix products, arithmetic and copies ran while one was open for 0% of the time, Pallas kernels for 0%

profile of v1, /device:TPU:1, one launch (start us, length us, event | category | flops | bytes accessed | tf_op | source)
XLA Modules:
  0.0 134.1 jit_solution(10043831239740175343)
XLA Ops:
  0.6 0.0 copy-start
  0.6 1.0 copy-done
  1.7 0.0 copy-start.1
  1.7 0.7 copy-done.1
  2.3 1.8 %pack_pieces.1 = bf16[64,16,640]{2,1,0:T(8,128)(2,1)} custom-call(s32[32]{0:T(128)S(1)} %copy-done.1, bf16[512,512]{1,0:T(8,128)(2,1)S(1)} %copy-done), custom_call_target="tpu_custom_call" | custom-call | tf_op jit(solution)/shard_map/pack_pieces/pallas_call | solution.py:56
  4.1 0.0 copy-start.3
  4.1 0.0 copy-start.4
  4.1 0.0 copy-start.5
  4.1 0.0 copy-start.6
  4.1 0.0 copy-start.7
  4.1 12.1 %all-to-all-start = ((bf16[64,16,640]{2,1,0:T(8,128)(2,1)}), bf16[64,16,640]{2,1,0:T(8,128)(2,1)S(1)}, u32[]{:S(2)}, u32[]{:S(2)}) async-start(bf16[64,16,640]{2,1,0:T(8,128)(2,1)} %pack_pieces.1), calls=%async_computation | async-start | bytes 2621440 | tf_op jit(solution)/shard_map/all_to_all | solution.py:420
  16.2 19.3 %all-to-all-done = bf16[64,16,640]{2,1,0:T(8,128)(2,1)S(1)} async-done(((bf16[64,16,640]{2,1,0:T(8,128)(2,1)}), bf16[64,16,640]{2,1,0:T(8,128)(2,1)S(1)}, u32[]{:S(2)}, u32[]{:S(2)}) %all-to-all-start) | async-done | bytes 1310752 | tf_op jit(solution)/shard_map/all_to_all | solution.py:420
  35.5 0.0 copy-done.3
  35.5 0.0 copy-done.4
  35.6 0.0 copy-done.5
  35.6 0.0 copy-done.6
  35.6 0.0 copy-done.7
  35.6 22.0 %layer.1 = (bf16[512,512]{1,0:T(8,128)(2,1)}, bf16[32,2,16,640]{3,2,1,0:T(8,128)(2,1)S(1)}, bf16[32,2,16,640]{3,2,1,0:T(8,128)(2,1)S(1)}, bf16[1024,512]{1,0:T(8,128)(2,1)S(1)}) custom-call(s32[1]{0:T(128)} %bitcast.core_ref, s32[4]{0:T(128)S(1)} %copy-done.6, s32[4]{0:T(128)S(1)} %copy-done.7, f32[4,12]{1,0:T(4,128)S(1)} %copy-done.5, ...), custom_call_target="tpu_custom_call" | custom-call | flops 5000000000 | bytes 9000000 | tf_op jit(solution)/shard_map/layer/pallas_call | solution.py:305
  57.6 3.1 %collective-permute-start = (bf16[32,2,16,640]{3,2,1,0:T(8,128)(2,1)S(1)}, bf16[32,2,16,640]{3,2,1,0:T(8,128)(2,1)S(1)}, u32[]{:S(2)}, u32[]{:S(2)}) collective-permute-start(bf16[32,2,16,640]{3,2,1,0:T(8,128)(2,1)S(1)} %get-tuple-element.14), channel_id=1, source_target_pairs={{0,64},{64,0},{1,65},{65,1},{2,66},{66,2},{3,67},{67,3},{4,68},{68... | collective-permute-start | bytes 3932168 | tf_op jit(solution)/shard_map/ppermute | solution.py:431
  60.7 2.7 %collective-permute-done = bf16[32,2,16,640]{3,2,1,0:T(8,128)(2,1)S(1)} collective-permute-done((bf16[32,2,16,640]{3,2,1,0:T(8,128)(2,1)S(1)}, bf16[32,2,16,640]{3,2,1,0:T(8,128)(2,1)S(1)}, u32[]{:S(2)}, u32[]{:S(2)}) %collective-permute-start) | collective-permute-done | bytes 1310752 | tf_op jit(solution)/shard_map/ppermute | solution.py:431
  63.4 0.4 join.1
  63.8 0.0 copy-start.2
  63.8 35.8 %all_to_all.15.mixed_ref = bf16[64,16,1152]{2,1,0:T(8,128)(2,1)S(1)} all-to-all(bf16[64,16,1152]{2,1,0:T(8,128)(2,1)S(1)} %join.1), channel_id=1, replica_groups=mesh['group'=2,'member'=64] {'member'}, dimensions={0} | all-to-all | bytes 4718592 | tf_op jit(solution)/shard_map/all_to_all | solution.py:433
  99.7 0.0 copy-done.2
  99.7 1.4 %total.1 = (bf16[64,16,640]{2,1,0:T(8,128)(2,1)S(1)}, bf16[512,512]{1,0:T(8,128)(2,1)}) custom-call(s32[32]{0:T(128)S(1)} %copy-done.2, bf16[64,16,1152]{2,1,0:T(8,128)(2,1)S(1)} %all_to_all.15.mixed_ref), custom_call_target="tpu_custom_call" | custom-call | tf_op jit(solution)/shard_map/total/pallas_call | solution.py:355
  101.1 23.6 %all_to_all.16 = bf16[64,16,640]{2,1,0:T(8,128)(2,1)S(1)} all-to-all(bf16[64,16,640]{2,1,0:T(8,128)(2,1)S(1)} %get-tuple-element.17), channel_id=1, replica_groups=mesh['group'=2,'member'=64] {'member'}, dimensions={0} | all-to-all | bytes 2621440 | tf_op jit(solution)/shard_map/all_to_all | solution.py:437
  124.7 4.1 %collective-permute-start.1 = (bf16[64,16,640]{2,1,0:T(8,128)(2,1)S(1)}, bf16[64,16,640]{2,1,0:T(8,128)(2,1)S(1)}, u32[]{:S(2)}, u32[]{:S(2)}) collective-permute-start(bf16[64,16,640]{2,1,0:T(8,128)(2,1)S(1)} %all_to_all.16), channel_id=1, source_target_pairs={{0,64},{64,0},{1,65},{65,1},{2,66},{66,2},{3,67},{67,3},{4,68},{68... | collective-permute-start | bytes 3932168 | tf_op jit(solution)/shard_map/ppermute | solution.py:438
  128.7 2.7 %collective-permute-done.1 = bf16[64,16,640]{2,1,0:T(8,128)(2,1)S(1)} collective-permute-done((bf16[64,16,640]{2,1,0:T(8,128)(2,1)S(1)}, bf16[64,16,640]{2,1,0:T(8,128)(2,1)S(1)}, u32[]{:S(2)}, u32[]{:S(2)}) %collective-permute-start.1) | collective-permute-done | bytes 1310752 | tf_op jit(solution)/shard_map/ppermute | solution.py:438
  131.4 2.7 %spread.1 = (f32[512,2048]{1,0:T(8,128)}, f32[512,512]{1,0:T(8,128)}) custom-call(s32[1]{0:T(128)} %bitcast.core_ref, bf16[32,2,16,640]{3,2,1,0:T(8,128)(2,1)S(1)} %bitcast.7, bf16[32,2,16,640]{3,2,1,0:T(8,128)(2,1)S(1)} %bitcast.9), custom_call_target="tpu_custom_call" | custom-call | tf_op jit(solution)/shard_map/spread/pallas_call | solution.py:397
Async XLA Ops:
  0.6 1.0 copy-start
  1.7 0.7 copy-start.1
  4.1 31.5 %copy-start.3 = (bf16[512,512]{1,0:T(8,128)(2,1)S(1)}, bf16[512,512]{1,0:T(8,128)(2,1)}, u32[]{:S(2)}) copy-start(bf16[512,512]{1,0:T(8,128)(2,1)} %cot_ref.1) | copy-start | bytes 1572868
  4.1 31.5 %copy-start.4 = (bf16[512,512]{1,0:T(8,128)(2,1)S(1)}, bf16[512,512]{1,0:T(8,128)(2,1)}, u32[]{:S(2)}) copy-start(bf16[512,512]{1,0:T(8,128)(2,1)} %w_out_ref.1) | copy-start | bytes 1572868
  4.1 31.5 %copy-start.5 = (f32[4,12]{1,0:T(4,128)S(1)}, f32[4,12]{1,0:T(4,128)}, u32[]{:S(2)}) copy-start(f32[4,12]{1,0:T(4,128)} %rab_ref.1) | copy-start | bytes 580
  4.1 31.5 %copy-start.6 = (s32[4]{0:T(128)S(1)}, s32[4]{0:T(128)}, u32[]{:S(2)}) copy-start(s32[4]{0:T(128)} %offset_ref.1) | copy-start | bytes 52
  4.1 31.5 %copy-start.7 = (s32[4]{0:T(128)S(1)}, s32[4]{0:T(128)}, u32[]{:S(2)}) copy-start(s32[4]{0:T(128)} %length_ref.1) | copy-start | bytes 52
  4.1 31.4 %all-to-all-start = ((bf16[64,16,640]{2,1,0:T(8,128)(2,1)}), bf16[64,16,640]{2,1,0:T(8,128)(2,1)S(1)}, u32[]{:S(2)}, u32[]{:S(2)}) async-start(bf16[64,16,640]{2,1,0:T(8,128)(2,1)} %pack_pieces.1), calls=%async_computation | async-start | bytes 2621440 | tf_op jit(solution)/shard_map/all_to_all | solution.py:420
  57.6 5.8 %collective-permute-start = (bf16[32,2,16,640]{3,2,1,0:T(8,128)(2,1)S(1)}, bf16[32,2,16,640]{3,2,1,0:T(8,128)(2,1)S(1)}, u32[]{:S(2)}, u32[]{:S(2)}) collective-permute-start(bf16[32,2,16,640]{3,2,1,0:T(8,128)(2,1)S(1)} %get-tuple-element.14), channel_id=1, source_target_pairs={{0,64},{64,0},{1,65},{65,1},{2,66},{66,2},{3,67},{67,3},{4,68},{68... | collective-permute-start | bytes 3932168 | tf_op jit(solution)/shard_map/ppermute | solution.py:431
  63.8 35.9 %copy-start.2 = (s32[32]{0:T(128)S(1)}, s32[32]{0:T(128)}, u32[]{:S(2)}) copy-start(s32[32]{0:T(128)} %route_ref.3) | copy-start | bytes 388
  124.7 6.7 %collective-permute-start.1 = (bf16[64,16,640]{2,1,0:T(8,128)(2,1)S(1)}, bf16[64,16,640]{2,1,0:T(8,128)(2,1)S(1)}, u32[]{:S(2)}, u32[]{:S(2)}) collective-permute-start(bf16[64,16,640]{2,1,0:T(8,128)(2,1)S(1)} %all_to_all.16), channel_id=1, source_target_pairs={{0,64},{64,0},{1,65},{65,1},{2,66},{66,2},{3,67},{67,3},{4,68},{68... | collective-permute-start | bytes 3932168 | tf_op jit(solution)/shard_map/ppermute | solution.py:438

commit v2 on v1

v2 whole, which is shorter than its diff:
```python
import functools
import math

import jax
import jax.numpy as jnp
from jax import lax
from jax.experimental import pallas as pl
from jax.experimental.pallas import tpu as pltpu
from jax.sharding import PartitionSpec as P

EPS = 1e-05
BF16 = jnp.bfloat16
F32 = jnp.float32
VMEM_LIMIT = 32 * 1024 * 1024
VMEM_SMALL = 16 * 1024 * 1024
VMEM_MOST = 56 * 1024 * 1024

ROWS, D, HID = 512, 512, 2048
BLOCK, BLOCKS, HEADS, BUCKETS = 128, 4, 4, 12
PIECE, PIECES, MEMBERS = 16, 32, 64
SLOT = 72
CHUNK = 640
SCALE = 1.0 / math.sqrt(128)
HALF = D // 2
SHARES = (HALF // PIECE, 4, PIECE, CHUNK)


def dot(a, b):
    return jnp.dot(a, b, preferred_element_type=F32)


def dot_nt(a, b):
    return lax.dot_general(a, b, (((1,), (1,)), ((), ())), preferred_element_type=F32)


def dot_tn(a, b):
    return lax.dot_general(a, b, (((0,), (0,)), ((), ())), preferred_element_type=F32)


def sigmoid(v):
    return 0.5 * jnp.tanh(0.5 * v) + 0.5


def in_hbm(array):
    return pltpu.with_memory_space_constraint(array, pltpu.HBM)


def full_spec(memory=pltpu.VMEM):
    return pl.BlockSpec(memory_space=memory)


def pack_kernel(route_hbm, events_hbm, out_ref, route_s, events_s, sems):
    copies = [
        pltpu.make_async_copy(route_hbm, route_s, sems.at[0]),
        pltpu.make_async_copy(events_hbm, events_s, sems.at[1]),
    ]
    for copy in copies:
        copy.start()
    out_ref[...] = jnp.zeros_like(out_ref)
    for copy in copies:
        copy.wait()
    for j in range(PIECES):
        target = route_s[j]
        device = lax.shift_right_logical(target, 5)
        place = lax.bitwise_and(target, PIECES - 1)
        for k in range(D // 128):
            out_ref[device, k * PIECE : (k + 1) * PIECE, :] = events_s[
                j * PIECE : (j + 1) * PIECE, k * 128 : (k + 1) * 128
            ]
        label = jnp.full((SLOT - 4 * PIECE, 128), (place + 1).astype(F32), F32)
        out_ref[device, 4 * PIECE :, :] = label.astype(BF16)


def pack(route, events):
    return pl.pallas_call(
        pack_kernel,
        out_shape=jax.ShapeDtypeStruct((MEMBERS, SLOT, 128), BF16),
        in_specs=[full_spec(pltpu.HBM)] * 2,
        out_specs=full_spec(),
        scratch_shapes=[
            pltpu.SMEM((PIECES,), jnp.int32),
            pltpu.VMEM((ROWS, D), BF16),
            pltpu.SemaphoreType.DMA((2,)),
        ],
        compiler_params=pltpu.CompilerParams(vmem_limit_bytes=VMEM_MOST),
        name="pack_pieces",
    )(in_hbm(route), in_hbm(events))


def cell_goals(arrived_ref):
    labels = arrived_ref[:, 4 * PIECE :, :].astype(F32)
    if labels.shape[1] < PIECE:
        labels = jnp.concatenate([labels, labels], axis=1)
    within = lax.broadcasted_iota(jnp.int32, labels.shape, 1).astype(F32)
    return ((labels - 1.0) * PIECE + within).reshape(MEMBERS * PIECE, 128)


def layer_kernel(
    core_ref,
    offset_ref,
    length_ref,
    rab_ref,
    arrived_ref,
    cot_hbm,
    w_in_hbm,
    w_out_hbm,
    out_ref,
    other_ref,
    left_ref,
    up_s,
    gh_s,
    bal_s,
    place_s,
    norm_s,
    hid_s,
    slope_s,
    att_s,
    asl_s,
    ctx_s,
    gm_s,
    mixed_s,
    gctx_s,
    g_s,
    trans_s,
    cot_ref,
    w_in_ref,
    w_out_ref,
    sems,
):
    copies = [
        pltpu.make_async_copy(w_in_hbm, w_in_ref, sems.at[0]),
        pltpu.make_async_copy(cot_hbm, cot_ref, sems.at[1]),
        pltpu.make_async_copy(w_out_hbm, w_out_ref, sems.at[2]),
    ]
    for copy in copies:
        copy.start()
    core = core_ref[0]
    goals = cell_goals(arrived_ref)
    pick = (lax.broadcasted_iota(jnp.int32, (8, 128), 1) == 0).astype(BF16)
    tens = dot_nt(pick, jnp.floor(goals * (1.0 / 16.0)).astype(BF16))[0:1, :]
    ones = lax.bitwise_and(
        lax.broadcasted_iota(jnp.int32, (1, MEMBERS * PIECE), 1), PIECE - 1
    ).astype(F32)
    goal = tens * PIECE + ones
    for b in range(BLOCKS):
        rows = lax.broadcasted_iota(jnp.int32, (BLOCK, 1), 0).astype(F32) + float(b * BLOCK)
        place_s[b * BLOCK : (b + 1) * BLOCK, :] = jnp.where(goal == rows, 1.0, 0.0).astype(BF16)
    for k in range(0, D // 128, 2):
        cells = jnp.concatenate(
            [
                arrived_ref[:, n * PIECE : (n + 1) * PIECE, :].reshape(MEMBERS * PIECE, 128)
                for n in (k, k + 1)
            ],
            axis=1,
        )
        bal_s[:, k * 128 : k * 128 + 256] = dot(place_s[...], cells).astype(BF16)

    for r in range(0, ROWS, 64):
        sl = slice(r, r + 64)
        x = bal_s[sl, :].astype(F32)
        centered = x - jnp.mean(x, axis=-1, keepdims=True)
        variance = jnp.mean(centered * centered, axis=-1, keepdims=True)
        rstd = lax.rsqrt(variance + EPS)
        xhat = centered * rstd
        norm_s[sl, :] = xhat.astype(BF16)

    copies[0].wait()
    for n in range(0, HID, 256):
        cols = slice(n, n + 256)
        v = dot(norm_s[...], w_in_ref[:, cols])
        g = sigmoid(v)
        h = v * g
        hid_s[:, cols] = h.astype(BF16)
        slope_s[:, cols] = g + h * (1.0 - g)

    row_id = lax.broadcasted_iota(jnp.int32, (BLOCK, BLOCK), 0)
    col_id = lax.broadcasted_iota(jnp.int32, (BLOCK, BLOCK), 1)

    def bias(head, distance):
        total = jnp.full((BLOCK, BLOCK), rab_ref[head, 0], F32)
        for bucket in range(1, 9):
            total = jnp.where(distance >= 2 ** (bucket - 1), rab_ref[head, bucket], total)
        return total

    def head_cols(part, head):
        return slice(part * D + head * 128, part * D + head * 128 + 128)

    second = jnp.int32(0)
    for b in range(1, BLOCKS):
        second = jnp.where(offset_ref[b] == 1, b, second)
    first = jnp.maximum(second - 1, 0)
    second_rows = pl.ds(pl.multiple_of(second * BLOCK, BLOCK), BLOCK)
    first_rows = pl.ds(pl.multiple_of(first * BLOCK, BLOCK), BLOCK)

    def live_rows(block):
        position = row_id + offset_ref[block] * BLOCK
        return position < length_ref[block]

    def attend(q_rows, k_rows, allowed, relative, head, tile):
        q = hid_s[q_rows, head_cols(2, head)]
        k = hid_s[k_rows, head_cols(3, head)]
        s = dot_nt(q, k) * SCALE + relative
        g = sigmoid(s)
        a = s * g
        asl_s[tile, head] = jnp.where(allowed, g + a * (1.0 - g), 0.0)
        a = jnp.where(allowed, a, 0.0).astype(BF16)
        att_s[tile, head] = a
        return dot(a, hid_s[k_rows, head_cols(1, head)])

    own_distance = row_id - col_id
    for head in range(HEADS):
        relative = bias(head, own_distance)
        for b in range(BLOCKS):
            rows = slice(b * BLOCK, (b + 1) * BLOCK)
            allowed = (own_distance >= 0) & live_rows(b)
            ctx_s[rows, head_cols(0, head)] = attend(rows, rows, allowed, relative, head, b)
    far_allowed = live_rows(second)
    for head in range(HEADS):
        relative = bias(head, own_distance + BLOCK)
        cols = head_cols(0, head)
        ctx_s[second_rows, cols] += attend(
            second_rows, first_rows, far_allowed, relative, head, BLOCKS
        )

    for copy in copies[1:]:
        copy.wait()
    for b in range(BLOCKS):
        rows = slice(b * BLOCK, (b + 1) * BLOCK)
        live = (
            lax.broadcasted_iota(jnp.int32, (BLOCK, 1), 0) + offset_ref[b] * BLOCK < length_ref[b]
        )
        up_s[rows, :] = jnp.where(live, cot_ref[rows, :].astype(F32), 0.0).astype(BF16)
    gm_s[...] = dot_nt(up_s[...], w_out_ref[...])
    for r in range(0, ROWS, 64):
        sl = slice(r, r + 64)
        c = ctx_s[sl, :]
        centered = c - jnp.mean(c, axis=-1, keepdims=True)
        variance = jnp.mean(centered * centered, axis=-1, keepdims=True)
        rstd = lax.rsqrt(variance + EPS)
        n = centered * rstd
        u = hid_s[sl, 0:D].astype(F32)
        mixed_s[sl, :] = (n * u).astype(BF16)
        gm = gm_s[sl, :]
        gh_s[sl, 0:D] = (gm * n * slope_s[sl, 0:D]).astype(BF16)
        gn = gm * u
        gctx = rstd * (
            gn
            - jnp.mean(gn, axis=-1, keepdims=True)
            - n * jnp.mean(gn * n, axis=-1, keepdims=True)
        )
        gctx_s[sl, :] = gctx.astype(BF16)
    gm_s[...] = dot(mixed_s[...], w_out_ref[...])
    for b in range(BLOCKS):
        rows = slice(b * BLOCK, (b + 1) * BLOCK)
        live = (
            lax.broadcasted_iota(jnp.int32, (BLOCK, 1), 0) + offset_ref[b] * BLOCK < length_ref[b]
        )
        out_ref[rows, :] = jnp.where(live, bal_s[rows, :].astype(F32) + gm_s[rows, :], 0.0).astype(
            BF16
        )

    def attend_back(q_rows, k_rows, head, tile):
        gc = gctx_s[q_rows, head_cols(0, head)]
        q = hid_s[q_rows, head_cols(2, head)]
        k = hid_s[k_rows, head_cols(3, head)]
        v = hid_s[k_rows, head_cols(1, head)]
        ds = (dot_nt(gc, v) * asl_s[tile, head]).astype(BF16)
        gv = dot_tn(att_s[tile, head], gc)
        gq = dot(ds, k) * SCALE
        gk = dot_tn(ds, q) * SCALE
        return gv, gq, gk

    for head in range(HEADS):
        for b in range(BLOCKS):
            rows = slice(b * BLOCK, (b + 1) * BLOCK)
            gv, gq, gk = attend_back(rows, rows, head, b)
            g_s[rows, head_cols(0, head)] = gv
            g_s[rows, head_cols(1, head)] = gq
            g_s[rows, head_cols(2, head)] = gk
    for head in range(HEADS):
        gv, gq, gk = attend_back(second_rows, first_rows, head, BLOCKS)
        g_s[first_rows, head_cols(0, head)] += gv
        g_s[second_rows, head_cols(1, head)] += gq
        g_s[first_rows, head_cols(2, head)] += gk
    for r in range(0, ROWS, 64):
        sl = slice(r, r + 64)
        for n in range(0, 3 * D, D):
            gh_s[sl, D + n : 2 * D + n] = (
                g_s[sl, n : n + D] * slope_s[sl, D + n : 2 * D + n]
            ).astype(BF16)

    own_rows = pl.ds(pl.multiple_of(core * HALF, HALF), HALF)
    other_rows = pl.ds(pl.multiple_of((1 - core) * HALF, HALF), HALF)
    trans_s[0] = norm_s[...].T
    trans_s[1] = mixed_s[...].T
    left_ref[0] = trans_s[0, own_rows, :]
    left_ref[1] = trans_s[1, own_rows, :]

    def store(at, value):
        other_ref[at] = value.astype(BF16)

    weight_grads(trans_s[0, other_rows, :], trans_s[1, other_rows, :], gh_s, up_s, store)


def weight_grads(normed_t, mixed_t, gh_ref, up_ref, store):
    for at in range(0, HID + D, 256):
        if at < HID:
            value = dot(normed_t, gh_ref[:, at : at + 256])
        else:
            value = dot(mixed_t, up_ref[:, at - HID : at - HID + 256])
        for n in (0, 128):
            side, start = (at + n) // CHUNK, (at + n) % CHUNK
            shares = value[:, n : n + 128].reshape(HALF // PIECE, PIECE, 128)
            store((slice(None), side, slice(None), slice(start, start + 128)), shares)


def own_kernel(left_ref, up_ref, gh_ref, out_ref):
    def store(at, value):
        out_ref[at] = value.astype(BF16)

    weight_grads(left_ref[0], left_ref[1], gh_ref, up_ref, store)


def own_part(left, up, gh):
    return pl.pallas_call(
        own_kernel,
        out_shape=jax.ShapeDtypeStruct(SHARES, BF16),
        in_specs=[full_spec()] * 3,
        out_specs=full_spec(),
        compiler_params=pltpu.CompilerParams(vmem_limit_bytes=VMEM_SMALL),
        cost_estimate=pl.CostEstimate(
            flops=700_000_000, bytes_accessed=6_000_000, transcendentals=0
        ),
        name="own_part",
    )(left, up, gh)


def join_kernel(own_ref, got_ref, out_ref):
    out_ref[...] = (own_ref[...].astype(F32) + got_ref[...].astype(F32)).astype(BF16)


def join(own, got):
    return pl.pallas_call(
        join_kernel,
        out_shape=jax.ShapeDtypeStruct(SHARES, BF16),
        in_specs=[full_spec()] * 2,
        out_specs=full_spec(),
        compiler_params=pltpu.CompilerParams(vmem_limit_bytes=VMEM_SMALL),
        cost_estimate=pl.CostEstimate(flops=1_000_000, bytes_accessed=4_000_000, transcendentals=0),
        name="join",
    )(own, got)


def rest_kernel(
    arrived_hbm,
    up_hbm,
    gh_hbm,
    bal_hbm,
    w_in_hbm,
    back_hbm,
    arrived_ref,
    up_ref,
    gh_ref,
    bal_ref,
    w_in_ref,
    back_ref,
    gx_s,
    gb_s,
    place_s,
    sems,
):
    loads = [
        pltpu.make_async_copy(source, target, sems.at[n])
        for n, (source, target) in enumerate(
            (
                (gh_hbm, gh_ref),
                (w_in_hbm, w_in_ref),
                (bal_hbm, bal_ref),
                (up_hbm, up_ref),
                (arrived_hbm, arrived_ref),
            )
        )
    ]
    for load in loads:
        load.start()
    loads[0].wait()
    loads[1].wait()
    gx_s[...] = dot_nt(gh_ref[...], w_in_ref[...])
    loads[2].wait()
    loads[3].wait()
    for r in range(0, ROWS, 64):
        sl = slice(r, r + 64)
        x = bal_ref[sl, :].astype(F32)
        centered = x - jnp.mean(x, axis=-1, keepdims=True)
        variance = jnp.mean(centered * centered, axis=-1, keepdims=True)
        rstd = lax.rsqrt(variance + EPS)
        xhat = centered * rstd
        gx = gx_s[sl, :]
        gx = rstd * (
            gx
            - jnp.mean(gx, axis=-1, keepdims=True)
            - xhat * jnp.mean(gx * xhat, axis=-1, keepdims=True)
        )
        gb_s[sl, :] = (up_ref[sl, :].astype(F32) + gx).astype(BF16)
    loads[4].wait()
    goals = cell_goals(arrived_ref)
    for b in range(BLOCKS):
        row = lax.broadcasted_iota(jnp.int32, (1, BLOCK), 1).astype(F32) + float(b * BLOCK)
        place_s[:, b * BLOCK : (b + 1) * BLOCK] = jnp.where(goals == row, 1.0, 0.0).astype(BF16)
    for n in range(0, D, 256):
        back_ref[:, n : n + 256] = dot(place_s[...], gb_s[:, n : n + 256]).astype(BF16)
    out = pltpu.make_async_copy(back_ref, back_hbm, sems.at[5])
    out.start()
    out.wait()


def rest(arrived, up, gh, bal, w_in):
    shapes = [(MEMBERS, SLOT, 128), (ROWS, D), (ROWS, HID), (ROWS, D), (D, HID)]
    shapes += [(MEMBERS * PIECE, D)]
    return pl.pallas_call(
        rest_kernel,
        out_shape=pltpu.HBM((MEMBERS * PIECE, D), BF16),
        in_specs=[full_spec(pltpu.HBM)] * 5,
        out_specs=full_spec(pltpu.HBM),
        scratch_shapes=[pltpu.VMEM(shape, BF16) for shape in shapes]
        + [
            pltpu.VMEM((ROWS, D), F32),
            pltpu.VMEM((ROWS, D), BF16),
            pltpu.VMEM((MEMBERS * PIECE, ROWS), BF16),
            pltpu.SemaphoreType.DMA((6,)),
        ],
        compiler_params=pltpu.CompilerParams(vmem_limit_bytes=VMEM_SMALL),
        cost_estimate=pl.CostEstimate(
            flops=2_500_000_000, bytes_accessed=9_000_000, transcendentals=1_000
        ),
        name="rest",
    )(*map(in_hbm, (arrived, up, gh, bal, w_in)))


def layer(core, offsets, lengths, rab, arrived, cotangent, w_in, w_out):
    scratch = [
        ((ROWS, MEMBERS * PIECE), BF16),
        ((ROWS, D), BF16),
        ((ROWS, HID), BF16),
        ((ROWS, HID), F32),
        ((BLOCKS + 1, HEADS, BLOCK, BLOCK), BF16),
        ((BLOCKS + 1, HEADS, BLOCK, BLOCK), F32),
        ((ROWS, D), F32),
        ((ROWS, D), F32),
        ((ROWS, D), BF16),
        ((ROWS, D), BF16),
        ((ROWS, 3 * D), F32),
        ((2, D, ROWS), BF16),
        ((ROWS, D), BF16),
        ((D, HID), BF16),
        ((D, D), BF16),
    ]
    return pl.pallas_call(
        layer_kernel,
        out_shape=(
            jax.ShapeDtypeStruct((ROWS, D), BF16),
            jax.ShapeDtypeStruct(SHARES, BF16),
            jax.ShapeDtypeStruct((2, HALF, ROWS), BF16),
            jax.ShapeDtypeStruct((ROWS, D), BF16),
            jax.ShapeDtypeStruct((ROWS, HID), BF16),
            jax.ShapeDtypeStruct((ROWS, D), BF16),
        ),
        in_specs=[full_spec(pltpu.SMEM)] * 4
        + [full_spec()]
        + [full_spec(pltpu.HBM)] * 3,
        out_specs=(full_spec(),) * 6,
        scratch_shapes=[pltpu.VMEM(shape, kind) for shape, kind in scratch]
        + [pltpu.SemaphoreType.DMA((3,))],
        compiler_params=pltpu.CompilerParams(vmem_limit_bytes=VMEM_LIMIT),
        cost_estimate=pl.CostEstimate(
            flops=4_000_000_000, bytes_accessed=9_000_000, transcendentals=1_500_000
        ),
        name="layer",
    )(core, offsets, lengths, rab, arrived, in_hbm(cotangent), in_hbm(w_in), in_hbm(w_out))


def total_kernel(received_ref, back_hbm, out_ref, sem):
    copy = pltpu.make_async_copy(back_hbm, out_ref.at[:, :, CHUNK:], sem)
    copy.start()
    total = received_ref[0].astype(F32)
    for m in range(1, MEMBERS):
        total += received_ref[m].astype(F32)
    total = (total * (1.0 / 256.0)).astype(BF16)
    out_ref[:, :, :CHUNK] = jnp.broadcast_to(total[None], (MEMBERS, PIECE, CHUNK))
    copy.wait()


def total(received, back):
    return pl.pallas_call(
        total_kernel,
        out_shape=jax.ShapeDtypeStruct((MEMBERS, PIECE, CHUNK + D), BF16),
        in_specs=[full_spec(), full_spec(pltpu.HBM)],
        out_specs=full_spec(),
        scratch_shapes=[pltpu.SemaphoreType.DMA],
        compiler_params=pltpu.CompilerParams(vmem_limit_bytes=VMEM_SMALL),
        cost_estimate=pl.CostEstimate(flops=1_000_000, bytes_accessed=4_000_000, transcendentals=0),
        name="total",
    )(received, in_hbm(back))


def put_shares(source, rows_s, groups):
    for side in range(4):
        at = side * CHUNK
        for g in groups:
            value = source[g, side, :, :CHUNK].astype(F32)
            rows_s[g * PIECE : (g + 1) * PIECE, at : at + CHUNK] = value


def put_rows(rows_s, half, w_in_hbm, w_out_hbm, sems, source):
    copies = []
    parts = 4
    height = HALF // parts
    for part in range(parts):
        put_shares(source, rows_s, range(part * height // PIECE, (part + 1) * height // PIECE))
        here = slice(part * height, (part + 1) * height)
        there = pl.ds(pl.multiple_of(half * HALF + part * height, height), height)
        for n, copy in enumerate(
            (
                (rows_s.at[here, :HID], w_in_hbm.at[there]),
                (rows_s.at[here, HID:], w_out_hbm.at[there]),
            )
        ):
            copies.append(pltpu.make_async_copy(*copy, sems.at[2 * part + n]))
            copies[-1].start()
    return copies


def mine_kernel(
    core_ref, route_ref, received_ref, events_hbm, w_in_hbm, w_out_hbm, rows_s, events_s, sems
):
    copies = put_rows(rows_s, core_ref[0], w_in_hbm, w_out_hbm, sems, received_ref)
    for j in range(PIECES):
        slot = lax.shift_right_logical(route_ref[j], 5)
        piece = received_ref[lax.shift_right_logical(slot, 2), lax.bitwise_and(slot, 3)]
        events_s[j * PIECE : (j + 1) * PIECE, :] = piece[:, CHUNK:]
    copies.append(pltpu.make_async_copy(events_s, events_hbm, sems.at[8]))
    copies[-1].start()
    for copy in copies:
        copy.wait()


def mine_out(core, route, received):
    return pl.pallas_call(
        mine_kernel,
        out_shape=(
            jax.ShapeDtypeStruct((ROWS, D), BF16),
            jax.ShapeDtypeStruct((D, HID), F32),
            jax.ShapeDtypeStruct((D, D), F32),
        ),
        in_specs=[full_spec(pltpu.SMEM)] * 2 + [full_spec()],
        out_specs=(full_spec(pltpu.HBM),) * 3,
        scratch_shapes=[
            pltpu.VMEM((HALF, HID + D), F32),
            pltpu.VMEM((ROWS, D), BF16),
            pltpu.SemaphoreType.DMA((9,)),
        ],
        compiler_params=pltpu.CompilerParams(vmem_limit_bytes=VMEM_SMALL),
        cost_estimate=pl.CostEstimate(flops=0, bytes_accessed=6_000_000, transcendentals=0),
        name="mine_out",
    )(core, route, received)


def theirs_kernel(core_ref, theirs_ref, _, __, w_in_hbm, w_out_hbm, rows_s, sems):
    for copy in put_rows(rows_s, 1 - core_ref[0], w_in_hbm, w_out_hbm, sems, theirs_ref):
        copy.wait()


def theirs_out(core, theirs, w_in_grad, w_out_grad):
    return pl.pallas_call(
        theirs_kernel,
        out_shape=(
            jax.ShapeDtypeStruct((D, HID), F32),
            jax.ShapeDtypeStruct((D, D), F32),
        ),
        in_specs=[full_spec(pltpu.SMEM), full_spec()] + [full_spec(pltpu.HBM)] * 2,
        out_specs=(full_spec(pltpu.HBM),) * 2,
        scratch_shapes=[
            pltpu.VMEM((HALF, HID + D), F32),
            pltpu.SemaphoreType.DMA((8,)),
        ],
        input_output_aliases={2: 0, 3: 1},
        compiler_params=pltpu.CompilerParams(vmem_limit_bytes=VMEM_SMALL),
        cost_estimate=pl.CostEstimate(flops=0, bytes_accessed=4_000_000, transcendentals=0),
        name="theirs_out",
    )(core, theirs, w_in_grad, w_out_grad)


def body(events, route, block_offset, hist_length, cotangent, w_in, w_out, rab):
    core = lax.axis_index("group").astype(jnp.int32).reshape(1)
    exchange = functools.partial(
        lax.all_to_all, axis_name="member", split_axis=0, concat_axis=0, tiled=True
    )
    swap = functools.partial(lax.ppermute, axis_name="group", perm=[(0, 1), (1, 0)])
    arrived = exchange(pack(route, events))
    outputs, other, left, up, gh, bal = layer(
        core, block_offset, hist_length, rab, arrived, cotangent, w_in, w_out
    )
    got = swap(other)
    joined = join(own_part(left, up, gh), got)
    received = exchange(joined.reshape(MEMBERS, PIECE, CHUNK))
    back = rest(arrived, up, gh, bal, w_in)
    received = exchange(total(received, back.reshape(MEMBERS, PIECE, D)))
    theirs = swap(received[:, :, :CHUNK])
    events_grad, w_in_grad, w_out_grad = mine_out(
        core, route, received.reshape(*SHARES[:3], CHUNK + D)
    )
    w_in_grad, w_out_grad = theirs_out(core, theirs.reshape(SHARES), w_in_grad, w_out_grad)
    return outputs, events_grad, w_in_grad, w_out_grad


def solution(mesh):
    placed = (
        P(("group", "member"), None),
        P(("group", "member")),
        P(("group", "member")),
        P(("group", "member")),
        P(("group", "member"), None),
        P(),
        P(),
        P(),
    )
    return jax.shard_map(
        body,
        mesh=mesh,
        in_specs=placed,
        out_specs=(P(("group", "member"), None), P(("group", "member"), None), P(), P()),
        check_vma=False,
    )
```

time: 134 us -> 123 us (0.918)
  blocking collectives: 59.5 us -> 36.8 us
  waiting for transfers between devices: 24.6 us -> 34 us
  starting transfers between devices: 19.3 us -> 22.7 us
  local copies, waits for them, and re-layouts: 1.72 us -> 0.16 us
    all_to_all x2 -> x1, blocking collectives: 59.5 us -> 36.8 us  [body(): received = exchange(total(received, back.reshape(MEMBERS, PIECE, D)))]
    all_to_all x0 -> x1, waiting for transfers between devices: none -> 13.9 us  [body(): received = exchange(joined.reshape(MEMBERS, PIECE, CHUNK))]
    pallas_call x1, Pallas kernels: 22 us -> 12.6 us  [layer(): pl.pallas_call(layer_kernel, out_shape=(jax.ShapeDtypeStruct((ROWS, D), B...]
    pallas_call x4 -> x7, Pallas kernels: 6.23 us -> 15.4 us  [the longest x1 5.88 us: rest(): pl.pallas_call(rest_kernel, out_shape=pltpu.HBM((MEMBERS * PIECE, D), BF1...]
    all_to_all x0 -> x1, starting transfers between devices: none -> 4.84 us  [body(): received = exchange(joined.reshape(MEMBERS, PIECE, CHUNK))]
    ppermute x1, waiting for transfers between devices: 2.66 us -> 0.34 us  [body(): theirs = swap(received[:, :, :CHUNK])]
    unnamed x16, local copies, waits for them, and re-layouts: 1.72 us -> 0.04 us
    ppermute x1, starting transfers between devices: 4.07 us -> 2.61 us  [body(): theirs = swap(received[:, :, :CHUNK])]
  transfers between devices with their start and end apart: 3 -> 4, of which waited for: 3 -> 4; matrix products, arithmetic and copies ran while one was open for 0% -> 0% of each run, Pallas kernels for 0% -> 7%
where the time goes in v2:
time: 123 us
  blocking collectives  36.8 us (30%)
  waiting for transfers between devices  34 us (28%)
  Pallas kernels  28 us (23%)
  starting transfers between devices  22.7 us (18%)
    all_to_all x1, blocking collectives, body(): received = exchange(total(received, back.reshape(MEMBERS, PIECE, D)))  36.8 us
    all_to_all x1, waiting for transfers between devices, body(): arrived = exchange(pack(route, events))  17.9 us
    all_to_all x1, waiting for transfers between devices, body(): received = exchange(joined.reshape(MEMBERS, PIECE, CHUNK))  13.9 us
    pallas_call x1, Pallas kernels, layer(): pl.pallas_call(layer_kernel, out_shape=(jax.ShapeDtypeStruct((ROWS, D), B...  12.6 us
    all_to_all x1, starting transfers between devices, body(): arrived = exchange(pack(route, events))  12.1 us
    pallas_call x1, Pallas kernels, rest(): pl.pallas_call(rest_kernel, out_shape=pltpu.HBM((MEMBERS * PIECE, D), BF1...  5.88 us
    all_to_all x1, starting transfers between devices, body(): received = exchange(joined.reshape(MEMBERS, PIECE, CHUNK))  4.84 us
    ppermute x1, starting transfers between devices, body(): got = swap(other)  3.19 us
  transfers between devices with their start and end apart: 4, of which 4 were waited for; matrix products, arithmetic and copies ran while one was open for 0% of the time, Pallas kernels for 7%

profile of v2, /device:TPU:1, one launch (start us, length us, event | category | flops | bytes accessed | tf_op | source)
XLA Modules:
  0.0 122.7 jit_solution(12336932255628395584)
XLA Ops:
  0.6 2.2 %pack_pieces.1 = bf16[64,72,128]{2,1,0:T(8,128)(2,1)} custom-call(s32[32]{0:T(128)} %route_ref.1, bf16[512,512]{1,0:T(8,128)(2,1)} %events_hbm.1), custom_call_target="tpu_custom_call" | custom-call | tf_op jit(solution)/shard_map/pack_pieces/pallas_call | solution.py:75
  2.8 0.0 copy-start.4
  2.8 0.0 copy-start.5
  2.8 0.0 copy-start.6
  2.9 12.1 %all-to-all-start = ((bf16[64,72,128]{2,1,0:T(8,128)(2,1)}), bf16[64,72,128]{2,1,0:T(8,128)(2,1)S(1)}, u32[]{:S(2)}, u32[]{:S(2)}) async-start(bf16[64,72,128]{2,1,0:T(8,128)(2,1)} %pack_pieces.1), calls=%async_computation | async-start | bytes 2359296 | tf_op jit(solution)/shard_map/all_to_all | solution.py:599
  15.0 17.9 %all-to-all-done.arrived_ref.arrived_hbm = bf16[64,72,128]{2,1,0:T(8,128)(2,1)S(1)} async-done(((bf16[64,72,128]{2,1,0:T(8,128)(2,1)}), bf16[64,72,128]{2,1,0:T(8,128)(2,1)S(1)}, u32[]{:S(2)}, u32[]{:S(2)}) %all-to-all-start) | async-done | bytes 1179680 | tf_op jit(solution)/shard_map/all_to_all | solution.py:599
  32.9 0.0 copy-start.1
  32.9 0.0 copy-done.4
  32.9 0.0 copy-done.5
  32.9 0.0 copy-done.6
  32.9 12.6 %layer.1 = (bf16[512,512]{1,0:T(8,128)(2,1)}, bf16[16,4,16,640]{3,2,1,0:T(8,128)(2,1)S(1)}, bf16[2,256,512]{2,1,0:T(8,128)(2,1)S(1)}, bf16[512,512]{1,0:T(8,128)...) custom-call(s32[1]{0:T(128)} %bitcast.core_ref, s32[4]{0:T(128)S(1)} %copy-done.5, ...), custom_call_target="tpu_custom_call" | custom-call | flops 4000000000 | bytes 9000000 | tf_op jit(solution)/shard_map/layer/pallas_call | solution.py:458
  45.5 0.0 copy-done.1
  45.5 0.0 copy-start
  45.5 0.0 copy-start.2
  45.6 0.0 copy-start.7
  45.6 3.2 %collective-permute-start = (bf16[16,4,16,640]{3,2,1,0:T(8,128)(2,1)S(1)}, bf16[16,4,16,640]{3,2,1,0:T(8,128)(2,1)S(1)}, u32[]{:S(2)}, u32[]{:S(2)}) collective-permute-start(bf16[16,4,16,640]{3,2,1,0:T(8,128)(2,1)S(1)} %get-tuple-element.19), channel_id=1, source_target_pairs={{0,64},{64,0},{1,65},{65,1},{2,66},{66,2},{3,67},{67,3},{4,68},{68... | collective-permute-start | bytes 3932168 | tf_op jit(solution)/shard_map/ppermute | solution.py:603
  48.8 0.8 own_part.1.own_ref
  49.6 0.0 copy-done
  49.6 0.0 copy-done.2
  49.6 0.0 copy-done.7
  49.6 1.8 %collective-permute-done.got_ref = bf16[16,4,16,640]{3,2,1,0:T(8,128)(2,1)S(1)} collective-permute-done((bf16[16,4,16,640]{3,2,1,0:T(8,128)(2,1)S(1)}, bf16[16,4,16,640]{3,2,1,0:T(8,128)(2,1)S(1)}, u32[]{:S(2)}, u32[]{:S(2)}) %collective-permute-start) | collective-permute-done | bytes 1310752 | tf_op jit(solution)/shard_map/ppermute | solution.py:603
  51.4 1.4 %join.1 = bf16[16,4,16,640]{3,2,1,0:T(8,128)(2,1)} custom-call(bf16[16,4,16,640]{3,2,1,0:T(8,128)(2,1)S(1)} %own_part.1.own_ref, bf16[16,4,16,640]{3,2,1,0:T(8,128)(2,1)S(1)} %collective-permute-done.got_ref), custom_call_target="tpu_custom_call" | custom-call | flops 1000000 | bytes 4000000 | tf_op jit(solution)/shard_map/join/pallas_call | solution.py:343
  52.8 4.8 %all-to-all-start.1 = ((bf16[64,16,640]{2,1,0:T(8,128)(2,1)}), bf16[64,16,640]{2,1,0:T(8,128)(2,1)S(1)}, u32[]{:S(2)}, u32[]{:S(2)}) async-start(bf16[64,16,640]{2,1,0:T(8,128)(2,1)} %bitcast.1), calls=%async_computation.1 | async-start | bytes 2621440 | tf_op jit(solution)/shard_map/all_to_all | solution.py:605
  57.6 5.9 %rest.1 = bf16[1024,512]{1,0:T(8,128)(2,1)} custom-call(bf16[64,72,128]{2,1,0:T(8,128)(2,1)} %copy-done.1, bf16[512,512]{1,0:T(8,128)(2,1)} %copy-done.2, bf16[512,2048]{1,0:T(8,128)(2,1)} %copy-done, bf16[512,512]{1,0:T(8,128)(2,1)} %copy-done.7, bf16[512,2048]{1,0:T(8,128)(2,1)} %w_in_hbm.3), custom_call_target="tpu_custom_call" | custom-call | flops 2500000000 | bytes 9000000 | tf_op jit(solution)/shard_map/rest/pallas_call | solution.py:420
  63.5 13.9 %all-to-all-done.1.received_ref = bf16[64,16,640]{2,1,0:T(8,128)(2,1)S(1)} async-done(((bf16[64,16,640]{2,1,0:T(8,128)(2,1)}), bf16[64,16,640]{2,1,0:T(8,128)(2,1)S(1)}, u32[]{:S(2)}, u32[]{:S(2)}) %all-to-all-start.1) | async-done | bytes 1310752 | tf_op jit(solution)/shard_map/all_to_all | solution.py:605
  77.4 1.2 %total.1 = bf16[64,16,1152]{2,1,0:T(8,128)(2,1)S(1)} custom-call(bf16[64,16,640]{2,1,0:T(8,128)(2,1)S(1)} %all-to-all-done.1.received_ref, bf16[64,16,512]{2,1,0:T(8,128)(2,1)} %bitcast.7), custom_call_target="tpu_custom_call" | custom-call | flops 1000000 | bytes 4000000 | tf_op jit(solution)/shard_map/total/pallas_call | solution.py:494
  78.7 36.8 %all_to_all.15 = bf16[64,16,1152]{2,1,0:T(8,128)(2,1)S(1)} all-to-all(bf16[64,16,1152]{2,1,0:T(8,128)(2,1)S(1)} %total.1), channel_id=1, replica_groups=mesh['group'=2,'member'=64] {'member'}, dimensions={0} | all-to-all | bytes 4718592 | tf_op jit(solution)/shard_map/all_to_all | solution.py:607
  115.5 0.0 copy-start.3
  115.5 0.1 slice.4
  115.6 2.6 %collective-permute-start.1 = (bf16[64,16,640]{2,1,0:T(8,128)(2,1)S(1)}, bf16[64,16,640]{2,1,0:T(8,128)(2,1)S(1)}, u32[]{:S(2)}, u32[]{:S(2)}) collective-permute-start(bf16[64,16,640]{2,1,0:T(8,128)(2,1)S(1)} %slice.4), channel_id=1, source_target_pairs={{0,64},{64,0},{1,65},{65,1},{2,66},{66,2},{3,67},{67,3},{4,68},{68... | collective-permute-start | bytes 3932168 | tf_op jit(solution)/shard_map/ppermute | solution.py:608
  118.3 0.0 copy-done.3
  118.3 2.3 %mine_out.1 = (bf16[512,512]{1,0:T(8,128)(2,1)}, f32[512,2048]{1,0:T(8,128)}, f32[512,512]{1,0:T(8,128)}) custom-call(s32[1]{0:T(128)} %bitcast.core_ref, s32[32]{0:T(128)S(1)} %copy-done.3, bf16[16,4,16,1152]{3,2,1,0:T(8,128)(2,1)S(1)} %bitcast.5), custom_call_target="tpu_custom_call" | custom-call | bytes 6000000 | tf_op jit(solution)/shard_map/mine_out/pallas_call | solution.py:548
  120.6 0.3 collective-permute-done.1
  120.9 1.6 %theirs_out.1 = (f32[512,2048]{1,0:T(8,128)}, f32[512,512]{1,0:T(8,128)}) custom-call(s32[1]{0:T(128)} %bitcast.core_ref, bf16[16,4,16,640]{3,2,1,0:T(8,128)(2,1)S(1)} %bitcast.6, f32[512,2048]{1,0:T(8,128)} %get-tuple-element.22._, f32[512,512]{1,0:T(8,128)} %get-tuple-element.23.__), custom_call_target="tpu_custom_call", output_to_operand_aliasing={{0}: (2, {}), {1}: (3, {})} | custom-call | bytes 4000000 | tf_op jit(solution)/shard_map/theirs_out/pallas_call | solution.py:574
Async XLA Ops:
  2.8 30.1 %copy-start.4 = (f32[4,12]{1,0:T(4,128)S(1)}, f32[4,12]{1,0:T(4,128)}, u32[]{:S(2)}) copy-start(f32[4,12]{1,0:T(4,128)} %rab_ref.1) | copy-start | bytes 580
  2.8 30.1 %copy-start.5 = (s32[4]{0:T(128)S(1)}, s32[4]{0:T(128)}, u32[]{:S(2)}) copy-start(s32[4]{0:T(128)} %offset_ref.1) | copy-start | bytes 52
  2.8 30.1 %copy-start.6 = (s32[4]{0:T(128)S(1)}, s32[4]{0:T(128)}, u32[]{:S(2)}) copy-start(s32[4]{0:T(128)} %length_ref.1) | copy-start | bytes 52
  2.9 30.0 %all-to-all-start = ((bf16[64,72,128]{2,1,0:T(8,128)(2,1)}), bf16[64,72,128]{2,1,0:T(8,128)(2,1)S(1)}, u32[]{:S(2)}, u32[]{:S(2)}) async-start(bf16[64,72,128]{2,1,0:T(8,128)(2,1)} %pack_pieces.1), calls=%async_computation | async-start | bytes 2359296 | tf_op jit(solution)/shard_map/all_to_all | solution.py:599
  32.9 12.6 %copy-start.1 = (bf16[64,72,128]{2,1,0:T(8,128)(2,1)}, bf16[64,72,128]{2,1,0:T(8,128)(2,1)S(1)}, u32[]{:S(2)}) copy-start(bf16[64,72,128]{2,1,0:T(8,128)(2,1)S(1)} %all-to-all-done.arrived_ref.arrived_hbm) | copy-start | bytes 3538948
  45.5 4.1 %copy-start = (bf16[512,2048]{1,0:T(8,128)(2,1)}, bf16[512,2048]{1,0:T(8,128)(2,1)S(1)}, u32[]{:S(2)}) copy-start(bf16[512,2048]{1,0:T(8,128)(2,1)S(1)} %get-tuple-element.18.gh_ref.gh_hbm) | copy-start | bytes 6291460
  45.5 4.1 %copy-start.2 = (bf16[512,512]{1,0:T(8,128)(2,1)}, bf16[512,512]{1,0:T(8,128)(2,1)S(1)}, u32[]{:S(2)}) copy-start(bf16[512,512]{1,0:T(8,128)(2,1)S(1)} %get-tuple-element.17.up_ref.up_hbm) | copy-start | bytes 1572868
  45.6 4.1 %copy-start.7 = (bf16[512,512]{1,0:T(8,128)(2,1)}, bf16[512,512]{1,0:T(8,128)(2,1)S(1)}, u32[]{:S(2)}) copy-start(bf16[512,512]{1,0:T(8,128)(2,1)S(1)} %get-tuple-element.20.bal_hbm) | copy-start | bytes 1572868
  45.6 5.8 %collective-permute-start = (bf16[16,4,16,640]{3,2,1,0:T(8,128)(2,1)S(1)}, bf16[16,4,16,640]{3,2,1,0:T(8,128)(2,1)S(1)}, u32[]{:S(2)}, u32[]{:S(2)}) collective-permute-start(bf16[16,4,16,640]{3,2,1,0:T(8,128)(2,1)S(1)} %get-tuple-element.19), channel_id=1, source_target_pairs={{0,64},{64,0},{1,65},{65,1},{2,66},{66,2},{3,67},{67,3},{4,68},{68... | collective-permute-start | bytes 3932168 | tf_op jit(solution)/shard_map/ppermute | solution.py:603
  52.8 24.7 %all-to-all-start.1 = ((bf16[64,16,640]{2,1,0:T(8,128)(2,1)}), bf16[64,16,640]{2,1,0:T(8,128)(2,1)S(1)}, u32[]{:S(2)}, u32[]{:S(2)}) async-start(bf16[64,16,640]{2,1,0:T(8,128)(2,1)} %bitcast.1), calls=%async_computation.1 | async-start | bytes 2621440 | tf_op jit(solution)/shard_map/all_to_all | solution.py:605
  115.5 2.7 %copy-start.3 = (s32[32]{0:T(128)S(1)}, s32[32]{0:T(128)}, u32[]{:S(2)}) copy-start(s32[32]{0:T(128)} %route_ref.1) | copy-start | bytes 388
  115.6 5.3 %collective-permute-start.1 = (bf16[64,16,640]{2,1,0:T(8,128)(2,1)S(1)}, bf16[64,16,640]{2,1,0:T(8,128)(2,1)S(1)}, u32[]{:S(2)}, u32[]{:S(2)}) collective-permute-start(bf16[64,16,640]{2,1,0:T(8,128)(2,1)S(1)} %slice.4), channel_id=1, source_target_pairs={{0,64},{64,0},{1,65},{65,1},{2,66},{66,2},{3,67},{67,3},{4,68},{68... | collective-permute-start | bytes 3932168 | tf_op jit(solution)/shard_map/ppermute | solution.py:608

commit v3 on v2

v3 whole, which is shorter than its diff:
```python
import functools
import math

import jax
import jax.numpy as jnp
from jax import lax
from jax.experimental import pallas as pl
from jax.experimental.pallas import tpu as pltpu
from jax.sharding import PartitionSpec as P

EPS = 1e-05
BF16 = jnp.bfloat16
F32 = jnp.float32
VMEM_LIMIT = 32 * 1024 * 1024
VMEM_SMALL = 16 * 1024 * 1024
VMEM_MOST = 56 * 1024 * 1024

ROWS, D, HID = 512, 512, 2048
BLOCK, BLOCKS, HEADS, BUCKETS = 128, 4, 4, 12
PIECE, PIECES, MEMBERS = 16, 32, 64
SLOT = 72
CHUNK = 640
SCALE = 1.0 / math.sqrt(128)
HALF = D // 2
SHARES = (HALF // PIECE, 4, PIECE, CHUNK)


def dot(a, b):
    return jnp.dot(a, b, preferred_element_type=F32)


def dot_nt(a, b):
    return lax.dot_general(a, b, (((1,), (1,)), ((), ())), preferred_element_type=F32)


def dot_tn(a, b):
    return lax.dot_general(a, b, (((0,), (0,)), ((), ())), preferred_element_type=F32)


def sigmoid(v):
    return 0.5 * jnp.tanh(0.5 * v) + 0.5


def in_hbm(array):
    return pltpu.with_memory_space_constraint(array, pltpu.HBM)


def full_spec(memory=pltpu.VMEM):
    return pl.BlockSpec(memory_space=memory)


def pack_kernel(route_hbm, events_hbm, out_hbm, route_s, events_s, out_s, sems):
    half = ROWS // 2
    loads = [pltpu.make_async_copy(route_hbm, route_s, sems.at[0])]
    for n in range(2):
        rows = pl.ds(n * half, half)
        loads.append(
            pltpu.make_async_copy(events_hbm.at[rows], events_s.at[rows], sems.at[1 + n])
        )
    for load in loads:
        load.start()
    out_s[...] = jnp.zeros_like(out_s)
    for load in loads:
        load.wait()
    for j in range(PIECES):
        target = route_s[j]
        device = lax.shift_right_logical(target, 5)
        place = lax.bitwise_and(target, PIECES - 1)
        for k in range(D // 128):
            out_s[device, k * PIECE : (k + 1) * PIECE, :] = events_s[
                j * PIECE : (j + 1) * PIECE, k * 128 : (k + 1) * 128
            ]
        label = jnp.full((SLOT - 4 * PIECE, 128), (place + 1).astype(F32), F32)
        out_s[device, 4 * PIECE :, :] = label.astype(BF16)
    stores = []
    for n in range(4):
        part = pl.ds(n * (MEMBERS // 4), MEMBERS // 4)
        stores.append(pltpu.make_async_copy(out_s.at[part], out_hbm.at[part], sems.at[3 + n]))
        stores[-1].start()
    for store in stores:
        store.wait()


def pack(route, events):
    slots = (MEMBERS, SLOT, 128)
    return pl.pallas_call(
        pack_kernel,
        out_shape=pltpu.HBM(slots, BF16),
        in_specs=[full_spec(pltpu.HBM)] * 2,
        out_specs=full_spec(pltpu.HBM),
        scratch_shapes=[
            pltpu.SMEM((PIECES,), jnp.int32),
            pltpu.VMEM((ROWS, D), BF16),
            pltpu.VMEM(slots, BF16),
            pltpu.SemaphoreType.DMA((7,)),
        ],
        compiler_params=pltpu.CompilerParams(vmem_limit_bytes=VMEM_MOST),
        name="pack_pieces",
    )(in_hbm(route), in_hbm(events))


def cell_goals(arrived_ref):
    labels = arrived_ref[:, 4 * PIECE :, :].astype(F32)
    if labels.shape[1] < PIECE:
        labels = jnp.concatenate([labels, labels], axis=1)
    within = lax.broadcasted_iota(jnp.int32, labels.shape, 1).astype(F32)
    return ((labels - 1.0) * PIECE + within).reshape(MEMBERS * PIECE, 128)


def block_order(offset_ref):
    second = jnp.int32(1)
    for b in range(2, BLOCKS):
        second = jnp.where(offset_ref[b] == 1, b, second)
    return (
        second - 1,
        second,
        jnp.where(second == 1, 2, 0),
        jnp.where(second == 3, 1, 3),
    )


def block_rows(order, i):
    return pl.ds(pl.multiple_of(order[i] * BLOCK, BLOCK), BLOCK)


def inner_goals(goals, order):
    block = jnp.floor(goals * (1.0 / BLOCK))
    moved = goals
    for i in range(BLOCKS):
        at = order[i].astype(F32)
        moved = jnp.where(block == at, goals + (float(i) - at) * BLOCK, moved)
    return moved


def live_column(length_ref, order, i):
    first = BLOCK if i == 1 else 0
    return lax.broadcasted_iota(jnp.int32, (BLOCK, 1), 0) + first < length_ref[order[i]]


def normalized(x):
    centered = x - jnp.mean(x, axis=-1, keepdims=True)
    variance = jnp.mean(centered * centered, axis=-1, keepdims=True)
    rstd = lax.rsqrt(variance + EPS)
    return centered * rstd, rstd


def normalized_back(grad, hat, rstd):
    return rstd * (
        grad
        - jnp.mean(grad, axis=-1, keepdims=True)
        - hat * jnp.mean(grad * hat, axis=-1, keepdims=True)
    )


def head_cols(part, head):
    return slice(part * D + head * 128, part * D + head * 128 + 128)


def layer_kernel(
    offset_ref,
    length_ref,
    rab_ref,
    arrived_ref,
    cot_hbm,
    w_in_hbm,
    w_out_hbm,
    other_ref,
    left_ref,
    up_ref,
    gh_ref,
    bal_ref,
    mixed_ref,
    place_s,
    norm_s,
    hid_s,
    slope_s,
    long_att_s,
    long_ds_s,
    long_slope_s,
    short_att_s,
    short_slope_s,
    ctx_s,
    gm_s,
    gctx_s,
    trans_s,
    cot_ref,
    w_in_ref,
    w_out_ref,
    sems,
):
    copies = [
        pltpu.make_async_copy(w_in_hbm, w_in_ref, sems.at[0]),
        pltpu.make_async_copy(cot_hbm, cot_ref, sems.at[1]),
        pltpu.make_async_copy(w_out_hbm, w_out_ref, sems.at[2]),
    ]
    for copy in copies:
        copy.start()
    core = lax.axis_index("group")
    order = block_order(offset_ref)
    long_rows, short_rows = slice(0, 2 * BLOCK), slice(2 * BLOCK, 4 * BLOCK)

    tens = jnp.floor(cell_goals(arrived_ref) * (1.0 / PIECE)).astype(BF16)
    pick = (lax.broadcasted_iota(jnp.int32, (8, 128), 1) == 0).astype(BF16)
    ones = lax.bitwise_and(
        lax.broadcasted_iota(jnp.int32, (1, MEMBERS * PIECE), 1), PIECE - 1
    ).astype(F32)
    goal = inner_goals(dot_nt(pick, tens)[0:1, :] * PIECE + ones, order)

    def gather(rows):
        for r in range(rows.start, rows.stop, BLOCK):
            row = lax.broadcasted_iota(jnp.int32, (BLOCK, 1), 0).astype(F32) + float(r)
            place_s[r : r + BLOCK, :] = jnp.where(goal == row, 1.0, 0.0).astype(BF16)
        for k in range(0, D // 128, 2):
            cells = jnp.concatenate(
                [
                    arrived_ref[:, n * PIECE : (n + 1) * PIECE, :].reshape(MEMBERS * PIECE, 128)
                    for n in (k, k + 1)
                ],
                axis=1,
            )
            bal_ref[rows, k * 128 : k * 128 + 256] = dot(place_s[rows, :], cells).astype(BF16)

    def norm(r):
        sl = slice(r, r + 64)
        norm_s[sl, :] = normalized(bal_ref[sl, :].astype(F32))[0].astype(BF16)

    def project(rows, n):
        cols = slice(n, n + 256)
        v = dot(norm_s[rows, :], w_in_ref[:, cols])
        g = sigmoid(v)
        h = v * g
        hid_s[rows, cols] = h.astype(BF16)
        slope_s[rows, cols] = g + h * (1.0 - g)

    row_id = lax.broadcasted_iota(jnp.int32, (BLOCK, BLOCK), 0)
    col_id = lax.broadcasted_iota(jnp.int32, (BLOCK, BLOCK), 1)
    distance = row_id - col_id
    near_pairs = distance >= 0

    def bias(head, apart, buckets):
        total = jnp.full((BLOCK, BLOCK), rab_ref[head, 0], F32)
        for bucket in range(1, buckets):
            total = jnp.where(apart >= 2 ** (bucket - 1), rab_ref[head, bucket], total)
        return total

    def weigh(scores, relative, allowed):
        s = scores * SCALE + relative
        g = sigmoid(s)
        a = s * g
        return (
            jnp.where(allowed, a, 0.0).astype(BF16),
            jnp.where(allowed, g + a * (1.0 - g), 0.0),
        )

    def live_rows(i):
        return row_id + (BLOCK if i == 1 else 0) < length_ref[order[i]]

    allowed = [near_pairs & live_rows(i) for i in range(BLOCKS)] + [live_rows(1)]
    near = [None] * HEADS
    low, high = slice(0, BLOCK), slice(BLOCK, 2 * BLOCK)
    long_tiles = ((low, low, 0), (high, high, 1), (high, low, BLOCKS))

    def long_attend(head):
        near[head] = bias(head, distance, 8)
        far = bias(head, distance + BLOCK, 9)
        scores = dot_nt(hid_s[long_rows, head_cols(2, head)], hid_s[long_rows, head_cols(3, head)])
        long_att_s[head, low, high] = jnp.zeros((BLOCK, BLOCK), BF16)
        long_ds_s[head, low, high] = jnp.zeros((BLOCK, BLOCK), BF16)
        for tile, (i, j, pairs) in enumerate(long_tiles):
            a, slope = weigh(scores[i, j], far if tile == 2 else near[head], allowed[pairs])
            long_att_s[head, i, j] = a
            long_slope_s[head, tile] = slope
        ctx_s[long_rows, head_cols(0, head)] = dot(
            long_att_s[head], hid_s[long_rows, head_cols(1, head)]
        )

    def short_attend(head):
        for i in (2, 3):
            rows = slice(i * BLOCK, (i + 1) * BLOCK)
            scores = dot_nt(hid_s[rows, head_cols(2, head)], hid_s[rows, head_cols(3, head)])
            a, slope = weigh(scores, near[head], allowed[i])
            short_att_s[head, i - 2] = a
            short_slope_s[head, i - 2] = slope
            ctx_s[rows, head_cols(0, head)] = dot(a, hid_s[rows, head_cols(1, head)])

    def upstream(i):
        kept = jnp.where(
            live_column(length_ref, order, i), cot_ref[block_rows(order, i), :].astype(F32), 0.0
        )
        up_ref[i * BLOCK : (i + 1) * BLOCK, :] = kept.astype(BF16)

    def middle(r):
        sl = slice(r, r + 64)
        n, rstd = normalized(ctx_s[sl, :])
        u = hid_s[sl, 0:D].astype(F32)
        mixed_ref[sl, :] = (n * u).astype(BF16)
        gm = gm_s[sl, :]
        gh_ref[sl, 0:D] = (gm * n * slope_s[sl, 0:D]).astype(BF16)
        gctx_s[sl, :] = normalized_back(gm * u, n, rstd).astype(BF16)

    def finish_grads(rows, head, gv, gq, gk):
        for part, grad in ((1, gv), (2, gq * SCALE), (3, gk * SCALE)):
            cols = head_cols(part, head)
            gh_ref[rows, cols] = (grad * slope_s[rows, cols]).astype(BF16)

    def long_back(head):
        gc = gctx_s[long_rows, head_cols(0, head)]
        grads = dot_nt(gc, hid_s[long_rows, head_cols(1, head)])
        for tile, (i, j, _) in enumerate(long_tiles):
            long_ds_s[head, i, j] = (grads[i, j] * long_slope_s[head, tile]).astype(BF16)
        ds = long_ds_s[head]
        finish_grads(
            long_rows,
            head,
            dot_tn(long_att_s[head], gc),
            dot(ds, hid_s[long_rows, head_cols(3, head)]),
            dot_tn(ds, hid_s[long_rows, head_cols(2, head)]),
        )

    def short_back(head):
        for i in (2, 3):
            rows = slice(i * BLOCK, (i + 1) * BLOCK)
            gc = gctx_s[rows, head_cols(0, head)]
            grads = dot_nt(gc, hid_s[rows, head_cols(1, head)])
            ds = (grads * short_slope_s[head, i - 2]).astype(BF16)
            finish_grads(
                rows,
                head,
                dot_tn(short_att_s[head, i - 2], gc),
                dot(ds, hid_s[rows, head_cols(3, head)]),
                dot_tn(ds, hid_s[rows, head_cols(2, head)]),
            )

    parts = (1024, 1536, 1280, 1792, 512, 768, 0, 256)
    gather(long_rows)
    gather(short_rows)
    for r in range(0, 256, 64):
        norm(r)
    copies[0].wait()
    for k, n in enumerate(parts):
        project(long_rows, n)
        if k < 4:
            norm(256 + 64 * k)
    for copy in copies[1:]:
        copy.wait()
    for i in range(BLOCKS):
        upstream(i)
    gm_s[...] = dot_nt(up_ref[...], w_out_ref[...])
    for k, n in enumerate(parts):
        if k % 2 == 0:
            long_attend(k // 2)
        project(short_rows, n)
    for head in range(HEADS):
        middle(64 * head)
        short_attend(head)
    trans_s[0] = norm_s[...].T
    for head in range(HEADS):
        long_back(head)
        middle(256 + 64 * head)
    trans_s[1] = mixed_ref[...].T
    for head in range(HEADS):
        short_back(head)

    own_rows = pl.ds(pl.multiple_of(core * HALF, HALF), HALF)
    other_rows = pl.ds(pl.multiple_of((1 - core) * HALF, HALF), HALF)
    left_ref[0] = trans_s[0, own_rows, :]
    left_ref[1] = trans_s[1, own_rows, :]

    def store(at, value):
        other_ref[at] = value.astype(BF16)

    weight_grads(trans_s[0, other_rows, :], trans_s[1, other_rows, :], gh_ref, up_ref, store)


def weight_grads(normed_t, mixed_t, gh_ref, up_ref, store):
    for at in range(0, HID + D, 256):
        if at < HID:
            value = dot(normed_t, gh_ref[:, at : at + 256])
        else:
            value = dot(mixed_t, up_ref[:, at - HID : at - HID + 256])
        for n in (0, 128):
            side, start = (at + n) // CHUNK, (at + n) % CHUNK
            shares = value[:, n : n + 128].reshape(HALF // PIECE, PIECE, 128)
            store((slice(None), side, slice(None), slice(start, start + 128)), shares)


def own_kernel(left_ref, up_ref, gh_ref, out_ref):
    def store(at, value):
        out_ref[at] = value.astype(BF16)

    weight_grads(left_ref[0], left_ref[1], gh_ref, up_ref, store)


def own_part(left, up, gh):
    return pl.pallas_call(
        own_kernel,
        out_shape=jax.ShapeDtypeStruct(SHARES, BF16),
        in_specs=[full_spec()] * 3,
        out_specs=full_spec(),
        compiler_params=pltpu.CompilerParams(vmem_limit_bytes=VMEM_SMALL),
        cost_estimate=pl.CostEstimate(
            flops=700_000_000, bytes_accessed=6_000_000, transcendentals=0
        ),
        name="own_part",
    )(left, up, gh)


def join_kernel(own_ref, got_ref, out_hbm, out_s, sems):
    parts = 4
    step = SHARES[0] // parts
    copies = []
    for n in range(parts):
        part = pl.ds(n * step, step)
        out_s[part] = (own_ref[part].astype(F32) + got_ref[part].astype(F32)).astype(BF16)
        copies.append(pltpu.make_async_copy(out_s.at[part], out_hbm.at[part], sems.at[n]))
        copies[-1].start()
    for copy in copies:
        copy.wait()


def join(own, got):
    return pl.pallas_call(
        join_kernel,
        out_shape=pltpu.HBM(SHARES, BF16),
        in_specs=[full_spec()] * 2,
        out_specs=full_spec(pltpu.HBM),
        scratch_shapes=[pltpu.VMEM(SHARES, BF16), pltpu.SemaphoreType.DMA((4,))],
        compiler_params=pltpu.CompilerParams(vmem_limit_bytes=VMEM_SMALL),
        cost_estimate=pl.CostEstimate(flops=1_000_000, bytes_accessed=4_000_000, transcendentals=0),
        name="join",
    )(own, got)


def rest_kernel(offset_ref, length_ref, *refs):
    hbm, (out_hbm, back_hbm) = refs[:7], refs[7:9]
    here, (out_ref, back_ref, gx_s, gb_s, place_s, sems) = refs[9:16], refs[16:]
    loads = [pltpu.make_async_copy(hbm[n], here[n], sems.at[n]) for n in range(7)]
    for load in loads:
        load.start()
    gh_ref, w_in_ref, bal_ref, up_ref, arrived_ref, mixed_ref, w_out_ref = here
    order = block_order(offset_ref)
    loads[0].wait()
    loads[1].wait()
    gx_s[...] = dot_nt(gh_ref[...], w_in_ref[...])
    loads[2].wait()
    loads[3].wait()
    for r in range(0, ROWS, 64):
        sl = slice(r, r + 64)
        hat, rstd = normalized(bal_ref[sl, :].astype(F32))
        grad = normalized_back(gx_s[sl, :], hat, rstd)
        gb_s[sl, :] = (up_ref[sl, :].astype(F32) + grad).astype(BF16)
    loads[4].wait()
    goals = inner_goals(cell_goals(arrived_ref), order)
    for b in range(BLOCKS):
        row = lax.broadcasted_iota(jnp.int32, (1, BLOCK), 1).astype(F32) + float(b * BLOCK)
        place_s[:, b * BLOCK : (b + 1) * BLOCK] = jnp.where(goals == row, 1.0, 0.0).astype(BF16)
    for n in range(0, D, 256):
        back_ref[:, n : n + 256] = dot(place_s[...], gb_s[:, n : n + 256]).astype(BF16)
    stores = [pltpu.make_async_copy(back_ref, back_hbm, sems.at[7])]
    stores[0].start()
    loads[5].wait()
    loads[6].wait()
    gx_s[...] = dot(mixed_ref[...], w_out_ref[...])
    for i in range(BLOCKS):
        rows = slice(i * BLOCK, (i + 1) * BLOCK)
        value = bal_ref[rows, :].astype(F32) + gx_s[rows, :]
        value = jnp.where(live_column(length_ref, order, i), value, 0.0)
        out_ref[block_rows(order, i), :] = value.astype(BF16)
    stores.append(pltpu.make_async_copy(out_ref, out_hbm, sems.at[8]))
    stores[1].start()
    for store in stores:
        store.wait()


def rest(offsets, lengths, gh, w_in, bal, up, arrived, mixed, w_out):
    operands = (gh, w_in, bal, up, arrived, mixed, w_out)
    rows, cells = (ROWS, D), (MEMBERS * PIECE, D)
    return pl.pallas_call(
        rest_kernel,
        out_shape=(pltpu.HBM(rows, BF16), pltpu.HBM(cells, BF16)),
        in_specs=[full_spec(pltpu.SMEM)] * 2 + [full_spec(pltpu.HBM)] * 7,
        out_specs=(full_spec(pltpu.HBM),) * 2,
        scratch_shapes=[pltpu.VMEM(x.shape, BF16) for x in operands]
        + [
            pltpu.VMEM(rows, BF16),
            pltpu.VMEM(cells, BF16),
            pltpu.VMEM(rows, F32),
            pltpu.VMEM(rows, BF16),
            pltpu.VMEM((MEMBERS * PIECE, ROWS), BF16),
            pltpu.SemaphoreType.DMA((9,)),
        ],
        compiler_params=pltpu.CompilerParams(vmem_limit_bytes=VMEM_SMALL),
        cost_estimate=pl.CostEstimate(
            flops=2_500_000_000, bytes_accessed=9_000_000, transcendentals=1_000
        ),
        name="rest",
    )(offsets, lengths, *map(in_hbm, operands))


def layer(offsets, lengths, rab, arrived, cotangent, w_in, w_out):
    scratch = [
        ((ROWS, MEMBERS * PIECE), BF16),
        ((ROWS, D), BF16),
        ((ROWS, HID), BF16),
        ((ROWS, HID), F32),
        ((HEADS, 2 * BLOCK, 2 * BLOCK), BF16),
        ((HEADS, 2 * BLOCK, 2 * BLOCK), BF16),
        ((HEADS, 3, BLOCK, BLOCK), F32),
        ((HEADS, 2, BLOCK, BLOCK), BF16),
        ((HEADS, 2, BLOCK, BLOCK), F32),
        ((ROWS, D), F32),
        ((ROWS, D), F32),
        ((ROWS, D), BF16),
        ((2, D, ROWS), BF16),
        ((ROWS, D), BF16),
        ((D, HID), BF16),
        ((D, D), BF16),
    ]
    rows = jax.ShapeDtypeStruct((ROWS, D), BF16)
    return pl.pallas_call(
        layer_kernel,
        out_shape=(
            jax.ShapeDtypeStruct(SHARES, BF16),
            jax.ShapeDtypeStruct((2, HALF, ROWS), BF16),
            rows,
            jax.ShapeDtypeStruct((ROWS, HID), BF16),
            rows,
            rows,
        ),
        in_specs=[full_spec(pltpu.SMEM)] * 3 + [full_spec()] + [full_spec(pltpu.HBM)] * 3,
        out_specs=(full_spec(),) * 6,
        scratch_shapes=[pltpu.VMEM(shape, kind) for shape, kind in scratch]
        + [pltpu.SemaphoreType.DMA((3,))],
        compiler_params=pltpu.CompilerParams(vmem_limit_bytes=VMEM_LIMIT),
        cost_estimate=pl.CostEstimate(
            flops=4_000_000_000, bytes_accessed=9_000_000, transcendentals=1_500_000
        ),
        name="layer",
    )(offsets, lengths, rab, arrived, *map(in_hbm, (cotangent, w_in, w_out)))


def total_kernel(received_ref, back_hbm, out_ref, sems):
    parts = 4
    step = MEMBERS // parts
    copies = []
    for n in range(parts):
        part = pl.ds(n * step, step)
        copies.append(
            pltpu.make_async_copy(back_hbm.at[part], out_ref.at[part, :, CHUNK:], sems.at[n])
        )
        copies[-1].start()
    total = received_ref[0].astype(F32)
    for m in range(1, MEMBERS):
        total += received_ref[m].astype(F32)
    total = (total * (1.0 / 256.0)).astype(BF16)
    out_ref[:, :, :CHUNK] = jnp.broadcast_to(total[None], (MEMBERS, PIECE, CHUNK))
    for copy in copies:
        copy.wait()


def total(received, back):
    return pl.pallas_call(
        total_kernel,
        out_shape=jax.ShapeDtypeStruct((MEMBERS, PIECE, CHUNK + D), BF16),
        in_specs=[full_spec(), full_spec(pltpu.HBM)],
        out_specs=full_spec(),
        scratch_shapes=[pltpu.SemaphoreType.DMA((4,))],
        compiler_params=pltpu.CompilerParams(vmem_limit_bytes=VMEM_SMALL),
        cost_estimate=pl.CostEstimate(flops=1_000_000, bytes_accessed=4_000_000, transcendentals=0),
        name="total",
    )(received, in_hbm(back))


def put_shares(source, rows_s, groups):
    for side in range(4):
        at = side * CHUNK
        for g in groups:
            value = source[g, side, :, :CHUNK].astype(F32)
            rows_s[g * PIECE : (g + 1) * PIECE, at : at + CHUNK] = value


def put_rows(rows_s, half, w_in_hbm, w_out_hbm, sems, source):
    copies = []
    parts = 4
    height = HALF // parts
    for part in range(parts):
        put_shares(source, rows_s, range(part * height // PIECE, (part + 1) * height // PIECE))
        here = slice(part * height, (part + 1) * height)
        there = pl.ds(pl.multiple_of(half * HALF + part * height, height), height)
        for n, copy in enumerate(
            (
                (rows_s.at[here, :HID], w_in_hbm.at[there]),
                (rows_s.at[here, HID:], w_out_hbm.at[there]),
            )
        ):
            copies.append(pltpu.make_async_copy(*copy, sems.at[2 * part + n]))
            copies[-1].start()
    return copies


def mine_kernel(
    route_ref, received_ref, events_hbm, w_in_hbm, w_out_hbm, rows_s, events_s, sems
):
    copies = put_rows(rows_s, lax.axis_index("group"), w_in_hbm, w_out_hbm, sems, received_ref)
    for j in range(PIECES):
        slot = lax.shift_right_logical(route_ref[j], 5)
        piece = received_ref[lax.shift_right_logical(slot, 2), lax.bitwise_and(slot, 3)]
        events_s[j * PIECE : (j + 1) * PIECE, :] = piece[:, CHUNK:]
    copies.append(pltpu.make_async_copy(events_s, events_hbm, sems.at[8]))
    copies[-1].start()
    for copy in copies:
        copy.wait()


def mine_out(route, received):
    return pl.pallas_call(
        mine_kernel,
        out_shape=(
            jax.ShapeDtypeStruct((ROWS, D), BF16),
            jax.ShapeDtypeStruct((D, HID), F32),
            jax.ShapeDtypeStruct((D, D), F32),
        ),
        in_specs=[full_spec(pltpu.SMEM), full_spec()],
        out_specs=(full_spec(pltpu.HBM),) * 3,
        scratch_shapes=[
            pltpu.VMEM((HALF, HID + D), F32),
            pltpu.VMEM((ROWS, D), BF16),
            pltpu.SemaphoreType.DMA((9,)),
        ],
        compiler_params=pltpu.CompilerParams(vmem_limit_bytes=VMEM_SMALL),
        cost_estimate=pl.CostEstimate(flops=0, bytes_accessed=6_000_000, transcendentals=0),
        name="mine_out",
    )(route, received)


def theirs_kernel(theirs_ref, _, __, w_in_hbm, w_out_hbm, rows_s, sems):
    for copy in put_rows(rows_s, 1 - lax.axis_index("group"), w_in_hbm, w_out_hbm, sems, theirs_ref):
        copy.wait()


def theirs_out(theirs, w_in_grad, w_out_grad):
    return pl.pallas_call(
        theirs_kernel,
        out_shape=(
            jax.ShapeDtypeStruct((D, HID), F32),
            jax.ShapeDtypeStruct((D, D), F32),
        ),
        in_specs=[full_spec()] + [full_spec(pltpu.HBM)] * 2,
        out_specs=(full_spec(pltpu.HBM),) * 2,
        scratch_shapes=[
            pltpu.VMEM((HALF, HID + D), F32),
            pltpu.SemaphoreType.DMA((8,)),
        ],
        input_output_aliases={1: 0, 2: 1},
        compiler_params=pltpu.CompilerParams(vmem_limit_bytes=VMEM_SMALL),
        cost_estimate=pl.CostEstimate(flops=0, bytes_accessed=4_000_000, transcendentals=0),
        name="theirs_out",
    )(theirs, w_in_grad, w_out_grad)


def body(events, route, block_offset, hist_length, cotangent, w_in, w_out, rab):
    exchange = functools.partial(
        lax.all_to_all, axis_name="member", split_axis=0, concat_axis=0, tiled=True
    )
    swap = functools.partial(lax.ppermute, axis_name="group", perm=[(0, 1), (1, 0)])
    arrived = exchange(pack(route, events))
    other, left, up, gh, bal, mixed = layer(
        block_offset, hist_length, rab, arrived, cotangent, w_in, w_out
    )
    got = swap(other)
    joined = join(own_part(left, up, gh), got)
    received = exchange(joined.reshape(MEMBERS, PIECE, CHUNK))
    outputs, back = rest(block_offset, hist_length, gh, w_in, bal, up, arrived, mixed, w_out)
    received = exchange(total(received, back.reshape(MEMBERS, PIECE, D)))
    theirs = swap(received[:, :, :CHUNK])
    events_grad, w_in_grad, w_out_grad = mine_out(
        route, received.reshape(*SHARES[:3], CHUNK + D)
    )
    w_in_grad, w_out_grad = theirs_out(theirs.reshape(SHARES), w_in_grad, w_out_grad)
    return outputs, events_grad, w_in_grad, w_out_grad


def solution(mesh):
    placed = (
        P(("group", "member"), None),
        P(("group", "member")),
        P(("group", "member")),
        P(("group", "member")),
        P(("group", "member"), None),
        P(),
        P(),
        P(),
    )
    return jax.shard_map(
        body,
        mesh=mesh,
        in_specs=placed,
        out_specs=(P(("group", "member"), None), P(("group", "member"), None), P(), P()),
        check_vma=False,
    )
```

time: 123 us -> 120 us (0.976)
  blocking collectives: 36.8 us -> 66.9 us
  waiting for transfers between devices: 34 us -> 14.8 us
  starting transfers between devices: 22.7 us -> 10.7 us
  Pallas kernels: 28 us -> 26.4 us
    all_to_all x0 -> x1, blocking collectives: none -> 30 us  [body(): arrived = exchange(pack(route, events))]
    all_to_all x1 -> x0, waiting for transfers between devices: 17.9 us -> none  [body(): arrived = exchange(pack(route, events))]
    all_to_all x1 -> x0, starting transfers between devices: 12.1 us -> none  [body(): arrived = exchange(pack(route, events))]
    pallas_call x4, Pallas kernels: 22 us -> 20.5 us  [the longest x1 10.1 us: layer(): pl.pallas_call(layer_kernel, out_shape=(jax.ShapeDtypeStruct(SHARES, BF16...]
    all_to_all x1, waiting for transfers between devices: 13.9 us -> 12.7 us  [body(): received = exchange(joined.reshape(MEMBERS, PIECE, CHUNK))]
  transfers between devices with their start and end apart: 4 -> 3, of which waited for: 4 -> 3; matrix products, arithmetic and copies ran while one was open for 0% -> 0% of each run, Pallas kernels for 7% -> 8%
where the time goes in v3:
time: 120 us
  blocking collectives  66.9 us (56%)
  Pallas kernels  26.4 us (22%)
  waiting for transfers between devices  14.8 us (12%)
  starting transfers between devices  10.7 us (9%)
    all_to_all x1, blocking collectives, body(): received = exchange(total(received, back.reshape(MEMBERS, PIECE, D)))  36.8 us
    all_to_all x1, blocking collectives, body(): arrived = exchange(pack(route, events))  30 us
    all_to_all x1, waiting for transfers between devices, body(): received = exchange(joined.reshape(MEMBERS, PIECE, CHUNK))  12.7 us
    pallas_call x1, Pallas kernels, layer(): pl.pallas_call(layer_kernel, out_shape=(jax.ShapeDtypeStruct(SHARES, BF16...  10.1 us
    pallas_call x1, Pallas kernels, rest(): pl.pallas_call(rest_kernel, out_shape=(pltpu.HBM(rows, BF16), pltpu.HBM(c...  6.96 us
    all_to_all x1, starting transfers between devices, body(): received = exchange(joined.reshape(MEMBERS, PIECE, CHUNK))  4.86 us
    ppermute x1, starting transfers between devices, body(): got = swap(other)  3.18 us
    ppermute x1, starting transfers between devices, body(): theirs = swap(received[:, :, :CHUNK])  2.62 us
  transfers between devices with their start and end apart: 3, of which 3 were waited for; matrix products, arithmetic and copies ran while one was open for 0% of the time, Pallas kernels for 8%

profile of v3, /device:TPU:1, one launch (start us, length us, event | category | flops | bytes accessed | tf_op | source)
XLA Modules:
  0.0 119.8 jit_solution(6032946786189444201)
XLA Ops:
  0.6 2.2 %pack_pieces.1 = bf16[64,72,128]{2,1,0:T(8,128)(2,1)} custom-call(s32[32]{0:T(128)} %route_ref.1, bf16[512,512]{1,0:T(8,128)(2,1)} %events_hbm.1), custom_call_target="tpu_custom_call" | custom-call | tf_op jit(solution)/shard_map/pack_pieces/pallas_call | solution.py:86
  2.8 0.0 copy-start.4
  2.9 0.0 copy-start.5
  2.9 0.0 copy-start.6
  2.9 30.0 %all_to_all.15.arrived_ref.refs_4_ = bf16[64,72,128]{2,1,0:T(8,128)(2,1)S(1)} all-to-all(bf16[64,72,128]{2,1,0:T(8,128)(2,1)} %pack_pieces.1), channel_id=1, replica_groups=mesh['group'=2,'member'=64] {'member'}, dimensions={0} | all-to-all | bytes 2359296 | tf_op jit(solution)/shard_map/all_to_all | solution.py:666
  32.9 0.0 copy-done.4
  32.9 0.0 copy-done.5
  32.9 0.0 copy-done.6
  32.9 0.0 copy-start.1
  32.9 10.1 %layer.1 = (bf16[16,4,16,640]{3,2,1,0:T(8,128)(2,1)S(1)}, bf16[2,256,512]{2,1,0:T(8,128)(2,1)S(1)}, bf16[512,512]{1,0:T(8,128)(2,1)S(1)}, bf16[512,2048]{1,0:T(8...) custom-call(s32[4]{0:T(128)S(1)} %copy-done.5, s32[4]{0:T(128)S(1)} %copy-done.6, ...), custom_call_target="tpu_custom_call" | custom-call | flops 4000000000 | bytes 9000000 | tf_op jit(solution)/shard_map/layer/pallas_call | solution.py:520
  43.1 0.0 copy-done.1
  43.1 0.0 copy-start
  43.1 0.0 copy-start.2
  43.1 0.0 copy-start.7
  43.1 0.0 copy-start.8
  43.1 3.2 %collective-permute-start = (bf16[16,4,16,640]{3,2,1,0:T(8,128)(2,1)S(1)}, bf16[16,4,16,640]{3,2,1,0:T(8,128)(2,1)S(1)}, u32[]{:S(2)}, u32[]{:S(2)}) collective-permute-start(bf16[16,4,16,640]{3,2,1,0:T(8,128)(2,1)S(1)} %get-tuple-element.23), channel_id=1, source_target_pairs={{0,64},{64,0},{1,65},{65,1},{2,66},{66,2},{3,67},{67,3},{4,68},{68... | collective-permute-start | bytes 3932168 | tf_op jit(solution)/shard_map/ppermute | solution.py:670
  46.3 0.8 own_part.1.own_ref
  47.2 0.0 copy-done
  47.2 0.0 copy-done.2
  47.2 0.0 copy-done.7
  47.2 0.0 copy-done.8
  47.2 1.8 %collective-permute-done.got_ref = bf16[16,4,16,640]{3,2,1,0:T(8,128)(2,1)S(1)} collective-permute-done((bf16[16,4,16,640]{3,2,1,0:T(8,128)(2,1)S(1)}, bf16[16,4,16,640]{3,2,1,0:T(8,128)(2,1)S(1)}, u32[]{:S(2)}, u32[]{:S(2)}) %collective-permute-start) | collective-permute-done | bytes 1310752 | tf_op jit(solution)/shard_map/ppermute | solution.py:670
  49.0 1.2 join.1
  50.2 4.9 %all-to-all-start.1 = ((bf16[64,16,640]{2,1,0:T(8,128)(2,1)}), bf16[64,16,640]{2,1,0:T(8,128)(2,1)S(1)}, u32[]{:S(2)}, u32[]{:S(2)}) async-start(bf16[64,16,640]{2,1,0:T(8,128)(2,1)} %bitcast.6), calls=%async_computation.1 | async-start | bytes 2621440 | tf_op jit(solution)/shard_map/all_to_all | solution.py:672
  55.0 7.0 %rest.1 = (bf16[512,512]{1,0:T(8,128)(2,1)}, bf16[1024,512]{1,0:T(8,128)(2,1)}) custom-call(s32[4]{0:T(128)S(1)} %copy-done.5, s32[4]{0:T(128)S(1)} %copy-done.6, bf16[512,2048]{1,0:T(8,128)(2,1)} %copy-done, bf16[512,2048]{1,0:T(8,128)(2,1)} %refs_1_.1, bf16[512,512]{1,0:T(8,128)(2,1)} %copy-done.7, bf16[512,512]{1,0:T(8,128)(2,1)} %copy-done.2, ...), custom_call_target="tpu_custom_call" | custom-call | flops 2500000000 | bytes 9000000 | tf_op jit(solution)/shard_map/rest/pallas_call | solution.py:478
  62.0 12.7 %all-to-all-done.1.received_ref = bf16[64,16,640]{2,1,0:T(8,128)(2,1)S(1)} async-done(((bf16[64,16,640]{2,1,0:T(8,128)(2,1)}), bf16[64,16,640]{2,1,0:T(8,128)(2,1)S(1)}, u32[]{:S(2)}, u32[]{:S(2)}) %all-to-all-start.1) | async-done | bytes 1310752 | tf_op jit(solution)/shard_map/all_to_all | solution.py:672
  74.6 1.2 %total.1 = bf16[64,16,1152]{2,1,0:T(8,128)(2,1)S(1)} custom-call(bf16[64,16,640]{2,1,0:T(8,128)(2,1)S(1)} %all-to-all-done.1.received_ref, bf16[64,16,512]{2,1,0:T(8,128)(2,1)} %bitcast.7), custom_call_target="tpu_custom_call" | custom-call | flops 1000000 | bytes 4000000 | tf_op jit(solution)/shard_map/total/pallas_call | solution.py:562
  75.9 36.8 %all_to_all.16 = bf16[64,16,1152]{2,1,0:T(8,128)(2,1)S(1)} all-to-all(bf16[64,16,1152]{2,1,0:T(8,128)(2,1)S(1)} %total.1), channel_id=1, replica_groups=mesh['group'=2,'member'=64] {'member'}, dimensions={0} | all-to-all | bytes 4718592 | tf_op jit(solution)/shard_map/all_to_all | solution.py:674
  112.7 0.0 copy-start.3
  112.7 0.1 slice.4
  112.8 2.6 %collective-permute-start.1 = (bf16[64,16,640]{2,1,0:T(8,128)(2,1)S(1)}, bf16[64,16,640]{2,1,0:T(8,128)(2,1)S(1)}, u32[]{:S(2)}, u32[]{:S(2)}) collective-permute-start(bf16[64,16,640]{2,1,0:T(8,128)(2,1)S(1)} %slice.4), channel_id=1, source_target_pairs={{0,64},{64,0},{1,65},{65,1},{2,66},{66,2},{3,67},{67,3},{4,68},{68... | collective-permute-start | bytes 3932168 | tf_op jit(solution)/shard_map/ppermute | solution.py:675
  115.4 0.0 copy-done.3
  115.4 2.3 %mine_out.1 = (bf16[512,512]{1,0:T(8,128)(2,1)}, f32[512,2048]{1,0:T(8,128)}, f32[512,512]{1,0:T(8,128)}) custom-call(s32[32]{0:T(128)S(1)} %copy-done.3, bf16[16,4,16,1152]{3,2,1,0:T(8,128)(2,1)S(1)} %bitcast.4), custom_call_target="tpu_custom_call" | custom-call | bytes 6000000 | tf_op jit(solution)/shard_map/mine_out/pallas_call | solution.py:616
  117.8 0.3 collective-permute-done.1
  118.1 1.6 %theirs_out.1 = (f32[512,2048]{1,0:T(8,128)}, f32[512,512]{1,0:T(8,128)}) custom-call(bf16[16,4,16,640]{3,2,1,0:T(8,128)(2,1)S(1)} %bitcast.5, f32[512,2048]{1,0:T(8,128)} %get-tuple-element.26._, f32[512,512]{1,0:T(8,128)} %get-tuple-element.27.__), custom_call_target="tpu_custom_call", output_to_operand_aliasing={{0}: (1, {}), {1}: (2, {})} | custom-call | bytes 4000000 | tf_op jit(solution)/shard_map/theirs_out/pallas_call | solution.py:642
Async XLA Ops:
  2.8 30.1 %copy-start.4 = (f32[4,12]{1,0:T(4,128)S(1)}, f32[4,12]{1,0:T(4,128)}, u32[]{:S(2)}) copy-start(f32[4,12]{1,0:T(4,128)} %rab_ref.1) | copy-start | bytes 580
  2.9 30.1 %copy-start.5 = (s32[4]{0:T(128)S(1)}, s32[4]{0:T(128)}, u32[]{:S(2)}) copy-start(s32[4]{0:T(128)} %offset_ref.3) | copy-start | bytes 52
  2.9 30.1 %copy-start.6 = (s32[4]{0:T(128)S(1)}, s32[4]{0:T(128)}, u32[]{:S(2)}) copy-start(s32[4]{0:T(128)} %length_ref.3) | copy-start | bytes 52
  32.9 10.1 %copy-start.1 = (bf16[64,72,128]{2,1,0:T(8,128)(2,1)}, bf16[64,72,128]{2,1,0:T(8,128)(2,1)S(1)}, u32[]{:S(2)}) copy-start(bf16[64,72,128]{2,1,0:T(8,128)(2,1)S(1)} %all_to_all.15.arrived_ref.refs_4_) | copy-start | bytes 3538948
  43.1 4.1 %copy-start = (bf16[512,2048]{1,0:T(8,128)(2,1)}, bf16[512,2048]{1,0:T(8,128)(2,1)S(1)}, u32[]{:S(2)}) copy-start(bf16[512,2048]{1,0:T(8,128)(2,1)S(1)} %get-tuple-element.17.refs_0_.gh_ref) | copy-start | bytes 6291460
  43.1 4.1 %copy-start.2 = (bf16[512,512]{1,0:T(8,128)(2,1)}, bf16[512,512]{1,0:T(8,128)(2,1)S(1)}, u32[]{:S(2)}) copy-start(bf16[512,512]{1,0:T(8,128)(2,1)S(1)} %get-tuple-element.19.refs_3_.up_ref) | copy-start | bytes 1572868
  43.1 4.1 %copy-start.7 = (bf16[512,512]{1,0:T(8,128)(2,1)}, bf16[512,512]{1,0:T(8,128)(2,1)S(1)}, u32[]{:S(2)}) copy-start(bf16[512,512]{1,0:T(8,128)(2,1)S(1)} %get-tuple-element.18.refs_2_) | copy-start | bytes 1572868
  43.1 4.1 %copy-start.8 = (bf16[512,512]{1,0:T(8,128)(2,1)}, bf16[512,512]{1,0:T(8,128)(2,1)S(1)}, u32[]{:S(2)}) copy-start(bf16[512,512]{1,0:T(8,128)(2,1)S(1)} %get-tuple-element.20.refs_5_) | copy-start | bytes 1572868
  43.1 5.8 %collective-permute-start = (bf16[16,4,16,640]{3,2,1,0:T(8,128)(2,1)S(1)}, bf16[16,4,16,640]{3,2,1,0:T(8,128)(2,1)S(1)}, u32[]{:S(2)}, u32[]{:S(2)}) collective-permute-start(bf16[16,4,16,640]{3,2,1,0:T(8,128)(2,1)S(1)} %get-tuple-element.23), channel_id=1, source_target_pairs={{0,64},{64,0},{1,65},{65,1},{2,66},{66,2},{3,67},{67,3},{4,68},{68... | collective-permute-start | bytes 3932168 | tf_op jit(solution)/shard_map/ppermute | solution.py:670
  50.2 24.5 %all-to-all-start.1 = ((bf16[64,16,640]{2,1,0:T(8,128)(2,1)}), bf16[64,16,640]{2,1,0:T(8,128)(2,1)S(1)}, u32[]{:S(2)}, u32[]{:S(2)}) async-start(bf16[64,16,640]{2,1,0:T(8,128)(2,1)} %bitcast.6), calls=%async_computation.1 | async-start | bytes 2621440 | tf_op jit(solution)/shard_map/all_to_all | solution.py:672
  112.7 2.7 %copy-start.3 = (s32[32]{0:T(128)S(1)}, s32[32]{0:T(128)}, u32[]{:S(2)}) copy-start(s32[32]{0:T(128)} %route_ref.1) | copy-start | bytes 388
  112.8 5.3 %collective-permute-start.1 = (bf16[64,16,640]{2,1,0:T(8,128)(2,1)S(1)}, bf16[64,16,640]{2,1,0:T(8,128)(2,1)S(1)}, u32[]{:S(2)}, u32[]{:S(2)}) collective-permute-start(bf16[64,16,640]{2,1,0:T(8,128)(2,1)S(1)} %slice.4), channel_id=1, source_target_pairs={{0,64},{64,0},{1,65},{65,1},{2,66},{66,2},{3,67},{67,3},{4,68},{68... | collective-permute-start | bytes 3932168 | tf_op jit(solution)/shard_map/ppermute | solution.py:675

commit v4 on v3

--- a/solution.py
+++ b/solution.py
@@ -13,7 +13,6 @@
 F32 = jnp.float32
 VMEM_LIMIT = 32 * 1024 * 1024
 VMEM_SMALL = 16 * 1024 * 1024
-VMEM_MOST = 56 * 1024 * 1024
 
 ROWS, D, HID = 512, 512, 2048
 BLOCK, BLOCKS, HEADS, BUCKETS = 128, 4, 4, 12
@@ -49,7 +48,7 @@
     return pl.BlockSpec(memory_space=memory)
 
 
-def pack_kernel(route_hbm, events_hbm, out_hbm, route_s, events_s, out_s, sems):
+def pack_kernel(route_hbm, events_hbm, out_ref, route_s, events_s, sems):
     half = ROWS // 2
     loads = [pltpu.make_async_copy(route_hbm, route_s, sems.at[0])]
     for n in range(2):
@@ -59,7 +58,7 @@
         )
     for load in loads:
         load.start()
-    out_s[...] = jnp.zeros_like(out_s)
+    out_ref[...] = jnp.zeros_like(out_ref)
     for load in loads:
         load.wait()
     for j in range(PIECES):
@@ -67,34 +66,25 @@
         device = lax.shift_right_logical(target, 5)
         place = lax.bitwise_and(target, PIECES - 1)
         for k in range(D // 128):
-            out_s[device, k * PIECE : (k + 1) * PIECE, :] = events_s[
+            out_ref[device, k * PIECE : (k + 1) * PIECE, :] = events_s[
                 j * PIECE : (j + 1) * PIECE, k * 128 : (k + 1) * 128
             ]
         label = jnp.full((SLOT - 4 * PIECE, 128), (place + 1).astype(F32), F32)
-        out_s[device, 4 * PIECE :, :] = label.astype(BF16)
-    stores = []
-    for n in range(4):
-        part = pl.ds(n * (MEMBERS // 4), MEMBERS // 4)
-        stores.append(pltpu.make_async_copy(out_s.at[part], out_hbm.at[part], sems.at[3 + n]))
-        stores[-1].start()
-    for store in stores:
-        store.wait()
+        out_ref[device, 4 * PIECE :, :] = label.astype(BF16)
 
 
 def pack(route, events):
-    slots = (MEMBERS, SLOT, 128)
     return pl.pallas_call(
         pack_kernel,
-        out_shape=pltpu.HBM(slots, BF16),
+        out_shape=jax.ShapeDtypeStruct((MEMBERS, SLOT, 128), BF16),
         in_specs=[full_spec(pltpu.HBM)] * 2,
-        out_specs=full_spec(pltpu.HBM),
+        out_specs=full_spec(),
         scratch_shapes=[
             pltpu.SMEM((PIECES,), jnp.int32),
             pltpu.VMEM((ROWS, D), BF16),
-            pltpu.VMEM(slots, BF16),
-            pltpu.SemaphoreType.DMA((7,)),
+            pltpu.SemaphoreType.DMA((3,)),
         ],
-        compiler_params=pltpu.CompilerParams(vmem_limit_bytes=VMEM_MOST),
+        compiler_params=pltpu.CompilerParams(vmem_limit_bytes=VMEM_SMALL),
         name="pack_pieces",
     )(in_hbm(route), in_hbm(events))
 
@@ -188,11 +178,14 @@
     w_out_ref,
     sems,
 ):
-    copies = [
-        pltpu.make_async_copy(w_in_hbm, w_in_ref, sems.at[0]),
-        pltpu.make_async_copy(cot_hbm, cot_ref, sems.at[1]),
-        pltpu.make_async_copy(w_out_hbm, w_out_ref, sems.at[2]),
-    ]
+    copies = []
+    for n, start in enumerate((1024, 1536, 512, 0)):
+        cols = pl.ds(start, D)
+        copies.append(
+            pltpu.make_async_copy(w_in_hbm.at[:, cols], w_in_ref.at[:, cols], sems.at[n])
+        )
+    copies.append(pltpu.make_async_copy(cot_hbm, cot_ref, sems.at[4]))
+    copies.append(pltpu.make_async_copy(w_out_hbm, w_out_ref, sems.at[5]))
     for copy in copies:
         copy.start()
     core = lax.axis_index("group")
@@ -336,12 +329,13 @@
     gather(short_rows)
     for r in range(0, 256, 64):
         norm(r)
-    copies[0].wait()
     for k, n in enumerate(parts):
+        if k in (0, 1, 4, 6):
+            copies[(0, 1, 4, 6).index(k)].wait()
         project(long_rows, n)
         if k < 4:
             norm(256 + 64 * k)
-    for copy in copies[1:]:
+    for copy in copies[4:]:
         copy.wait()
     for i in range(BLOCKS):
         upstream(i)
@@ -530,7 +524,7 @@
         in_specs=[full_spec(pltpu.SMEM)] * 3 + [full_spec()] + [full_spec(pltpu.HBM)] * 3,
         out_specs=(full_spec(),) * 6,
         scratch_shapes=[pltpu.VMEM(shape, kind) for shape, kind in scratch]
-        + [pltpu.SemaphoreType.DMA((3,))],
+        + [pltpu.SemaphoreType.DMA((6,))],
         compiler_params=pltpu.CompilerParams(vmem_limit_bytes=VMEM_LIMIT),
         cost_estimate=pl.CostEstimate(
             flops=4_000_000_000, bytes_accessed=9_000_000, transcendentals=1_500_000

time: 120 us -> 118 us (0.983)
  Pallas kernels: 26.4 us -> 24.9 us
  transfers between devices with their start and end apart: 3 -> 3, of which waited for: 3 -> 3; matrix products, arithmetic and copies ran while one was open for 0% -> 0% of each run, Pallas kernels for 8% -> 9%
where the time goes in v4:
time: 118 us
  blocking collectives  66.6 us (56%)
  Pallas kernels  24.9 us (21%)
  waiting for transfers between devices  14.8 us (13%)
  starting transfers between devices  10.7 us (9%)
    all_to_all x1, blocking collectives, body(): received = exchange(total(received, back.reshape(MEMBERS, PIECE, D)))  36.8 us
    all_to_all x1, blocking collectives, body(): arrived = exchange(pack(route, events))  29.8 us
    all_to_all x1, waiting for transfers between devices, body(): received = exchange(joined.reshape(MEMBERS, PIECE, CHUNK))  12.7 us
    pallas_call x1, Pallas kernels, layer(): pl.pallas_call(layer_kernel, out_shape=(jax.ShapeDtypeStruct(SHARES, BF16...  9.59 us
    pallas_call x1, Pallas kernels, rest(): pl.pallas_call(rest_kernel, out_shape=(pltpu.HBM(rows, BF16), pltpu.HBM(c...  6.95 us
    all_to_all x1, starting transfers between devices, body(): received = exchange(joined.reshape(MEMBERS, PIECE, CHUNK))  4.86 us
    ppermute x1, starting transfers between devices, body(): got = swap(other)  3.18 us
    ppermute x1, starting transfers between devices, body(): theirs = swap(received[:, :, :CHUNK])  2.62 us
  transfers between devices with their start and end apart: 3, of which 3 were waited for; matrix products, arithmetic and copies ran while one was open for 0% of the time, Pallas kernels for 9%

profile of v4, /device:TPU:1, one launch (start us, length us, event | category | flops | bytes accessed | tf_op | source)
XLA Modules:
  0.0 118.1 jit_solution(3389243100536755385)
XLA Ops:
  0.6 1.2 pack_pieces.1
  1.8 0.0 copy-start.4
  1.8 0.0 copy-start.5
  1.8 0.0 copy-start.6
  1.8 29.8 %all_to_all.15.arrived_ref.refs_4_ = bf16[64,72,128]{2,1,0:T(8,128)(2,1)S(1)} all-to-all(bf16[64,72,128]{2,1,0:T(8,128)(2,1)S(1)} %pack_pieces.1), channel_id=1, replica_groups=mesh['group'=2,'member'=64] {'member'}, dimensions={0} | all-to-all | bytes 2359296 | tf_op jit(solution)/shard_map/all_to_all | solution.py:660
  31.7 0.0 copy-done.4
  31.7 0.0 copy-done.5
  31.7 0.0 copy-done.6
  31.7 0.0 copy-start.1
  31.7 9.6 %layer.1 = (bf16[16,4,16,640]{3,2,1,0:T(8,128)(2,1)S(1)}, bf16[2,256,512]{2,1,0:T(8,128)(2,1)S(1)}, bf16[512,512]{1,0:T(8,128)(2,1)S(1)}, bf16[512,2048]{1,0:T(8...) custom-call(s32[4]{0:T(128)S(1)} %copy-done.5, s32[4]{0:T(128)S(1)} %copy-done.6, ...), custom_call_target="tpu_custom_call" | custom-call | flops 4000000000 | bytes 9000000 | tf_op jit(solution)/shard_map/layer/pallas_call | solution.py:514
  41.3 0.0 copy-done.1
  41.3 0.0 copy-start
  41.3 0.0 copy-start.2
  41.3 0.0 copy-start.7
  41.3 0.0 copy-start.8
  41.3 3.2 %collective-permute-start = (bf16[16,4,16,640]{3,2,1,0:T(8,128)(2,1)S(1)}, bf16[16,4,16,640]{3,2,1,0:T(8,128)(2,1)S(1)}, u32[]{:S(2)}, u32[]{:S(2)}) collective-permute-start(bf16[16,4,16,640]{3,2,1,0:T(8,128)(2,1)S(1)} %get-tuple-element.23), channel_id=1, source_target_pairs={{0,64},{64,0},{1,65},{65,1},{2,66},{66,2},{3,67},{67,3},{4,68},{68... | collective-permute-start | bytes 3932168 | tf_op jit(solution)/shard_map/ppermute | solution.py:664
  44.5 0.8 own_part.1.own_ref
  45.4 0.0 copy-done
  45.4 0.0 copy-done.2
  45.4 0.0 copy-done.7
  45.4 0.0 copy-done.8
  45.4 1.8 %collective-permute-done.got_ref = bf16[16,4,16,640]{3,2,1,0:T(8,128)(2,1)S(1)} collective-permute-done((bf16[16,4,16,640]{3,2,1,0:T(8,128)(2,1)S(1)}, bf16[16,4,16,640]{3,2,1,0:T(8,128)(2,1)S(1)}, u32[]{:S(2)}, u32[]{:S(2)}) %collective-permute-start) | collective-permute-done | bytes 1310752 | tf_op jit(solution)/shard_map/ppermute | solution.py:664
  47.2 1.2 join.1
  48.4 4.9 %all-to-all-start.1 = ((bf16[64,16,640]{2,1,0:T(8,128)(2,1)}), bf16[64,16,640]{2,1,0:T(8,128)(2,1)S(1)}, u32[]{:S(2)}, u32[]{:S(2)}) async-start(bf16[64,16,640]{2,1,0:T(8,128)(2,1)} %bitcast.6), calls=%async_computation.1 | async-start | bytes 2621440 | tf_op jit(solution)/shard_map/all_to_all | solution.py:666
  53.2 6.9 %rest.1 = (bf16[512,512]{1,0:T(8,128)(2,1)}, bf16[1024,512]{1,0:T(8,128)(2,1)}) custom-call(s32[4]{0:T(128)S(1)} %copy-done.5, s32[4]{0:T(128)S(1)} %copy-done.6, bf16[512,2048]{1,0:T(8,128)(2,1)} %copy-done, bf16[512,2048]{1,0:T(8,128)(2,1)} %refs_1_.1, bf16[512,512]{1,0:T(8,128)(2,1)} %copy-done.7, bf16[512,512]{1,0:T(8,128)(2,1)} %copy-done.2, ...), custom_call_target="tpu_custom_call" | custom-call | flops 2500000000 | bytes 9000000 | tf_op jit(solution)/shard_map/rest/pallas_call | solution.py:472
  60.2 12.7 %all-to-all-done.1.received_ref = bf16[64,16,640]{2,1,0:T(8,128)(2,1)S(1)} async-done(((bf16[64,16,640]{2,1,0:T(8,128)(2,1)}), bf16[64,16,640]{2,1,0:T(8,128)(2,1)S(1)}, u32[]{:S(2)}, u32[]{:S(2)}) %all-to-all-start.1) | async-done | bytes 1310752 | tf_op jit(solution)/shard_map/all_to_all | solution.py:666
  72.9 1.2 %total.1 = bf16[64,16,1152]{2,1,0:T(8,128)(2,1)S(1)} custom-call(bf16[64,16,640]{2,1,0:T(8,128)(2,1)S(1)} %all-to-all-done.1.received_ref, bf16[64,16,512]{2,1,0:T(8,128)(2,1)} %bitcast.7), custom_call_target="tpu_custom_call" | custom-call | flops 1000000 | bytes 4000000 | tf_op jit(solution)/shard_map/total/pallas_call | solution.py:556
  74.1 36.8 %all_to_all.16 = bf16[64,16,1152]{2,1,0:T(8,128)(2,1)S(1)} all-to-all(bf16[64,16,1152]{2,1,0:T(8,128)(2,1)S(1)} %total.1), channel_id=1, replica_groups=mesh['group'=2,'member'=64] {'member'}, dimensions={0} | all-to-all | bytes 4718592 | tf_op jit(solution)/shard_map/all_to_all | solution.py:668
  110.9 0.0 copy-start.3
  110.9 0.1 slice.4
  111.0 2.6 %collective-permute-start.1 = (bf16[64,16,640]{2,1,0:T(8,128)(2,1)S(1)}, bf16[64,16,640]{2,1,0:T(8,128)(2,1)S(1)}, u32[]{:S(2)}, u32[]{:S(2)}) collective-permute-start(bf16[64,16,640]{2,1,0:T(8,128)(2,1)S(1)} %slice.4), channel_id=1, source_target_pairs={{0,64},{64,0},{1,65},{65,1},{2,66},{66,2},{3,67},{67,3},{4,68},{68... | collective-permute-start | bytes 3932168 | tf_op jit(solution)/shard_map/ppermute | solution.py:669
  113.7 0.0 copy-done.3
  113.7 2.3 %mine_out.1 = (bf16[512,512]{1,0:T(8,128)(2,1)}, f32[512,2048]{1,0:T(8,128)}, f32[512,512]{1,0:T(8,128)}) custom-call(s32[32]{0:T(128)S(1)} %copy-done.3, bf16[16,4,16,1152]{3,2,1,0:T(8,128)(2,1)S(1)} %bitcast.4), custom_call_target="tpu_custom_call" | custom-call | bytes 6000000 | tf_op jit(solution)/shard_map/mine_out/pallas_call | solution.py:610
  116.0 0.3 collective-permute-done.1
  116.3 1.6 %theirs_out.1 = (f32[512,2048]{1,0:T(8,128)}, f32[512,512]{1,0:T(8,128)}) custom-call(bf16[16,4,16,640]{3,2,1,0:T(8,128)(2,1)S(1)} %bitcast.5, f32[512,2048]{1,0:T(8,128)} %get-tuple-element.26._, f32[512,512]{1,0:T(8,128)} %get-tuple-element.27.__), custom_call_target="tpu_custom_call", output_to_operand_aliasing={{0}: (1, {}), {1}: (2, {})} | custom-call | bytes 4000000 | tf_op jit(solution)/shard_map/theirs_out/pallas_call | solution.py:636
Async XLA Ops:
  1.8 29.9 %copy-start.4 = (f32[4,12]{1,0:T(4,128)S(1)}, f32[4,12]{1,0:T(4,128)}, u32[]{:S(2)}) copy-start(f32[4,12]{1,0:T(4,128)} %rab_ref.1) | copy-start | bytes 580
  1.8 29.9 %copy-start.5 = (s32[4]{0:T(128)S(1)}, s32[4]{0:T(128)}, u32[]{:S(2)}) copy-start(s32[4]{0:T(128)} %offset_ref.3) | copy-start | bytes 52
  1.8 29.8 %copy-start.6 = (s32[4]{0:T(128)S(1)}, s32[4]{0:T(128)}, u32[]{:S(2)}) copy-start(s32[4]{0:T(128)} %length_ref.3) | copy-start | bytes 52
  31.7 9.6 %copy-start.1 = (bf16[64,72,128]{2,1,0:T(8,128)(2,1)}, bf16[64,72,128]{2,1,0:T(8,128)(2,1)S(1)}, u32[]{:S(2)}) copy-start(bf16[64,72,128]{2,1,0:T(8,128)(2,1)S(1)} %all_to_all.15.arrived_ref.refs_4_) | copy-start | bytes 3538948
  41.3 4.1 %copy-start = (bf16[512,2048]{1,0:T(8,128)(2,1)}, bf16[512,2048]{1,0:T(8,128)(2,1)S(1)}, u32[]{:S(2)}) copy-start(bf16[512,2048]{1,0:T(8,128)(2,1)S(1)} %get-tuple-element.17.refs_0_.gh_ref) | copy-start | bytes 6291460
  41.3 4.1 %copy-start.2 = (bf16[512,512]{1,0:T(8,128)(2,1)}, bf16[512,512]{1,0:T(8,128)(2,1)S(1)}, u32[]{:S(2)}) copy-start(bf16[512,512]{1,0:T(8,128)(2,1)S(1)} %get-tuple-element.19.refs_3_.up_ref) | copy-start | bytes 1572868
  41.3 4.1 %copy-start.7 = (bf16[512,512]{1,0:T(8,128)(2,1)}, bf16[512,512]{1,0:T(8,128)(2,1)S(1)}, u32[]{:S(2)}) copy-start(bf16[512,512]{1,0:T(8,128)(2,1)S(1)} %get-tuple-element.18.refs_2_) | copy-start | bytes 1572868
  41.3 4.1 %copy-start.8 = (bf16[512,512]{1,0:T(8,128)(2,1)}, bf16[512,512]{1,0:T(8,128)(2,1)S(1)}, u32[]{:S(2)}) copy-start(bf16[512,512]{1,0:T(8,128)(2,1)S(1)} %get-tuple-element.20.refs_5_) | copy-start | bytes 1572868
  41.3 5.8 %collective-permute-start = (bf16[16,4,16,640]{3,2,1,0:T(8,128)(2,1)S(1)}, bf16[16,4,16,640]{3,2,1,0:T(8,128)(2,1)S(1)}, u32[]{:S(2)}, u32[]{:S(2)}) collective-permute-start(bf16[16,4,16,640]{3,2,1,0:T(8,128)(2,1)S(1)} %get-tuple-element.23), channel_id=1, source_target_pairs={{0,64},{64,0},{1,65},{65,1},{2,66},{66,2},{3,67},{67,3},{4,68},{68... | collective-permute-start | bytes 3932168 | tf_op jit(solution)/shard_map/ppermute | solution.py:664
  48.4 24.5 %all-to-all-start.1 = ((bf16[64,16,640]{2,1,0:T(8,128)(2,1)}), bf16[64,16,640]{2,1,0:T(8,128)(2,1)S(1)}, u32[]{:S(2)}, u32[]{:S(2)}) async-start(bf16[64,16,640]{2,1,0:T(8,128)(2,1)} %bitcast.6), calls=%async_computation.1 | async-start | bytes 2621440 | tf_op jit(solution)/shard_map/all_to_all | solution.py:666
  110.9 2.7 %copy-start.3 = (s32[32]{0:T(128)S(1)}, s32[32]{0:T(128)}, u32[]{:S(2)}) copy-start(s32[32]{0:T(128)} %route_ref.1) | copy-start | bytes 388
  111.0 5.3 %collective-permute-start.1 = (bf16[64,16,640]{2,1,0:T(8,128)(2,1)S(1)}, bf16[64,16,640]{2,1,0:T(8,128)(2,1)S(1)}, u32[]{:S(2)}, u32[]{:S(2)}) collective-permute-start(bf16[64,16,640]{2,1,0:T(8,128)(2,1)S(1)} %slice.4), channel_id=1, source_target_pairs={{0,64},{64,0},{1,65},{65,1},{2,66},{66,2},{3,67},{67,3},{4,68},{68... | collective-permute-start | bytes 3932168 | tf_op jit(solution)/shard_map/ppermute | solution.py:669

commit v5 on v4

--- a/solution.py
+++ b/solution.py
@@ -159,7 +159,8 @@
     up_ref,
     gh_ref,
     bal_ref,
-    mixed_ref,
+    w_in_ref,
+    out_hbm,
     place_s,
     norm_s,
     hid_s,
@@ -174,8 +175,9 @@
     gctx_s,
     trans_s,
     cot_ref,
-    w_in_ref,
     w_out_ref,
+    mixed_ref,
+    out_s,
     sems,
 ):
     copies = []
@@ -290,6 +292,15 @@
         gm = gm_s[sl, :]
         gh_ref[sl, 0:D] = (gm * n * slope_s[sl, 0:D]).astype(BF16)
         gctx_s[sl, :] = normalized_back(gm * u, n, rstd).astype(BF16)
+
+    def output(rows):
+        product = dot(mixed_ref[rows, :], w_out_ref[...])
+        for i in range(rows.start // BLOCK, rows.stop // BLOCK):
+            here = slice(i * BLOCK, (i + 1) * BLOCK)
+            there = slice(here.start - rows.start, here.stop - rows.start)
+            value = bal_ref[here, :].astype(F32) + product[there, :]
+            value = jnp.where(live_column(length_ref, order, i), value, 0.0)
+            out_s[block_rows(order, i), :] = value.astype(BF16)
 
     def finish_grads(rows, head, gv, gq, gk):
         for part, grad in ((1, gv), (2, gq * SCALE), (3, gk * SCALE)):
@@ -348,10 +359,14 @@
         middle(64 * head)
         short_attend(head)
     trans_s[0] = norm_s[...].T
+    output(long_rows)
     for head in range(HEADS):
         long_back(head)
         middle(256 + 64 * head)
     trans_s[1] = mixed_ref[...].T
+    output(short_rows)
+    copies.append(pltpu.make_async_copy(out_s, out_hbm, sems.at[6]))
+    copies[-1].start()
     for head in range(HEADS):
         short_back(head)
 
@@ -364,6 +379,7 @@
         other_ref[at] = value.astype(BF16)
 
     weight_grads(trans_s[0, other_rows, :], trans_s[1, other_rows, :], gh_ref, up_ref, store)
+    copies[-1].wait()
 
 
 def weight_grads(normed_t, mixed_t, gh_ref, up_ref, store):
@@ -378,117 +394,75 @@
             store((slice(None), side, slice(None), slice(start, start + 128)), shares)
 
 
-def own_kernel(left_ref, up_ref, gh_ref, out_ref):
+def beside_kernel(
+    offset_ref,
+    arrived_ref,
+    left_ref,
+    up_ref,
+    gh_ref,
+    bal_ref,
+    w_in_ref,
+    own_ref,
+    back_ref,
+    gx_s,
+    gb_s,
+    place_s,
+):
+    gx_s[...] = dot_nt(gh_ref[...], w_in_ref[...])
+
     def store(at, value):
-        out_ref[at] = value.astype(BF16)
+        own_ref[at] = value.astype(BF16)
 
     weight_grads(left_ref[0], left_ref[1], gh_ref, up_ref, store)
-
-
-def own_part(left, up, gh):
-    return pl.pallas_call(
-        own_kernel,
-        out_shape=jax.ShapeDtypeStruct(SHARES, BF16),
-        in_specs=[full_spec()] * 3,
-        out_specs=full_spec(),
-        compiler_params=pltpu.CompilerParams(vmem_limit_bytes=VMEM_SMALL),
-        cost_estimate=pl.CostEstimate(
-            flops=700_000_000, bytes_accessed=6_000_000, transcendentals=0
-        ),
-        name="own_part",
-    )(left, up, gh)
-
-
-def join_kernel(own_ref, got_ref, out_hbm, out_s, sems):
-    parts = 4
-    step = SHARES[0] // parts
-    copies = []
-    for n in range(parts):
-        part = pl.ds(n * step, step)
-        out_s[part] = (own_ref[part].astype(F32) + got_ref[part].astype(F32)).astype(BF16)
-        copies.append(pltpu.make_async_copy(out_s.at[part], out_hbm.at[part], sems.at[n]))
-        copies[-1].start()
-    for copy in copies:
-        copy.wait()
-
-
-def join(own, got):
-    return pl.pallas_call(
-        join_kernel,
-        out_shape=pltpu.HBM(SHARES, BF16),
-        in_specs=[full_spec()] * 2,
-        out_specs=full_spec(pltpu.HBM),
-        scratch_shapes=[pltpu.VMEM(SHARES, BF16), pltpu.SemaphoreType.DMA((4,))],
-        compiler_params=pltpu.CompilerParams(vmem_limit_bytes=VMEM_SMALL),
-        cost_estimate=pl.CostEstimate(flops=1_000_000, bytes_accessed=4_000_000, transcendentals=0),
-        name="join",
-    )(own, got)
-
-
-def rest_kernel(offset_ref, length_ref, *refs):
-    hbm, (out_hbm, back_hbm) = refs[:7], refs[7:9]
-    here, (out_ref, back_ref, gx_s, gb_s, place_s, sems) = refs[9:16], refs[16:]
-    loads = [pltpu.make_async_copy(hbm[n], here[n], sems.at[n]) for n in range(7)]
-    for load in loads:
-        load.start()
-    gh_ref, w_in_ref, bal_ref, up_ref, arrived_ref, mixed_ref, w_out_ref = here
-    order = block_order(offset_ref)
-    loads[0].wait()
-    loads[1].wait()
-    gx_s[...] = dot_nt(gh_ref[...], w_in_ref[...])
-    loads[2].wait()
-    loads[3].wait()
     for r in range(0, ROWS, 64):
         sl = slice(r, r + 64)
         hat, rstd = normalized(bal_ref[sl, :].astype(F32))
         grad = normalized_back(gx_s[sl, :], hat, rstd)
         gb_s[sl, :] = (up_ref[sl, :].astype(F32) + grad).astype(BF16)
-    loads[4].wait()
-    goals = inner_goals(cell_goals(arrived_ref), order)
+    goals = inner_goals(cell_goals(arrived_ref), block_order(offset_ref))
     for b in range(BLOCKS):
         row = lax.broadcasted_iota(jnp.int32, (1, BLOCK), 1).astype(F32) + float(b * BLOCK)
         place_s[:, b * BLOCK : (b + 1) * BLOCK] = jnp.where(goals == row, 1.0, 0.0).astype(BF16)
     for n in range(0, D, 256):
         back_ref[:, n : n + 256] = dot(place_s[...], gb_s[:, n : n + 256]).astype(BF16)
-    stores = [pltpu.make_async_copy(back_ref, back_hbm, sems.at[7])]
-    stores[0].start()
-    loads[5].wait()
-    loads[6].wait()
-    gx_s[...] = dot(mixed_ref[...], w_out_ref[...])
-    for i in range(BLOCKS):
-        rows = slice(i * BLOCK, (i + 1) * BLOCK)
-        value = bal_ref[rows, :].astype(F32) + gx_s[rows, :]
-        value = jnp.where(live_column(length_ref, order, i), value, 0.0)
-        out_ref[block_rows(order, i), :] = value.astype(BF16)
-    stores.append(pltpu.make_async_copy(out_ref, out_hbm, sems.at[8]))
-    stores[1].start()
-    for store in stores:
-        store.wait()
-
-
-def rest(offsets, lengths, gh, w_in, bal, up, arrived, mixed, w_out):
-    operands = (gh, w_in, bal, up, arrived, mixed, w_out)
-    rows, cells = (ROWS, D), (MEMBERS * PIECE, D)
+
+
+def beside(offsets, arrived, left, up, gh, bal, w_in):
     return pl.pallas_call(
-        rest_kernel,
-        out_shape=(pltpu.HBM(rows, BF16), pltpu.HBM(cells, BF16)),
-        in_specs=[full_spec(pltpu.SMEM)] * 2 + [full_spec(pltpu.HBM)] * 7,
-        out_specs=(full_spec(pltpu.HBM),) * 2,
-        scratch_shapes=[pltpu.VMEM(x.shape, BF16) for x in operands]
-        + [
-            pltpu.VMEM(rows, BF16),
-            pltpu.VMEM(cells, BF16),
-            pltpu.VMEM(rows, F32),
-            pltpu.VMEM(rows, BF16),
+        beside_kernel,
+        out_shape=(
+            jax.ShapeDtypeStruct(SHARES, BF16),
+            jax.ShapeDtypeStruct((MEMBERS * PIECE, D), BF16),
+        ),
+        in_specs=[full_spec(pltpu.SMEM)] + [full_spec()] * 6,
+        out_specs=(full_spec(),) * 2,
+        scratch_shapes=[
+            pltpu.VMEM((ROWS, D), F32),
+            pltpu.VMEM((ROWS, D), BF16),
             pltpu.VMEM((MEMBERS * PIECE, ROWS), BF16),
-            pltpu.SemaphoreType.DMA((9,)),
         ],
         compiler_params=pltpu.CompilerParams(vmem_limit_bytes=VMEM_SMALL),
         cost_estimate=pl.CostEstimate(
-            flops=2_500_000_000, bytes_accessed=9_000_000, transcendentals=1_000
+            flops=3_000_000_000, bytes_accessed=2_000_000, transcendentals=1_000
         ),
-        name="rest",
-    )(offsets, lengths, *map(in_hbm, operands))
+        name="beside",
+    )(offsets, arrived, left, up, gh, bal, w_in)
+
+
+def join_kernel(own_ref, got_ref, out_ref):
+    out_ref[...] = (own_ref[...].astype(F32) + got_ref[...].astype(F32)).astype(BF16)
+
+
+def join(own, got):
+    return pl.pallas_call(
+        join_kernel,
+        out_shape=jax.ShapeDtypeStruct(SHARES, BF16),
+        in_specs=[full_spec()] * 2,
+        out_specs=full_spec(),
+        compiler_params=pltpu.CompilerParams(vmem_limit_bytes=VMEM_SMALL),
+        cost_estimate=pl.CostEstimate(flops=1_000_000, bytes_accessed=4_000_000, transcendentals=0),
+        name="join",
+    )(own, got)
 
 
 def layer(offsets, lengths, rab, arrived, cotangent, w_in, w_out):
@@ -507,8 +481,9 @@
         ((ROWS, D), BF16),
         ((2, D, ROWS), BF16),
         ((ROWS, D), BF16),
-        ((D, HID), BF16),
         ((D, D), BF16),
+        ((ROWS, D), BF16),
+        ((ROWS, D), BF16),
     ]
     rows = jax.ShapeDtypeStruct((ROWS, D), BF16)
     return pl.pallas_call(
@@ -519,12 +494,13 @@
             rows,
             jax.ShapeDtypeStruct((ROWS, HID), BF16),
             rows,
-            rows,
+            jax.ShapeDtypeStruct((D, HID), BF16),
+            pltpu.HBM((ROWS, D), BF16),
         ),
         in_specs=[full_spec(pltpu.SMEM)] * 3 + [full_spec()] + [full_spec(pltpu.HBM)] * 3,
-        out_specs=(full_spec(),) * 6,
+        out_specs=(full_spec(),) * 6 + (full_spec(pltpu.HBM),),
         scratch_shapes=[pltpu.VMEM(shape, kind) for shape, kind in scratch]
-        + [pltpu.SemaphoreType.DMA((6,))],
+        + [pltpu.SemaphoreType.DMA((7,))],
         compiler_params=pltpu.CompilerParams(vmem_limit_bytes=VMEM_LIMIT),
         cost_estimate=pl.CostEstimate(
             flops=4_000_000_000, bytes_accessed=9_000_000, transcendentals=1_500_000
@@ -533,36 +509,25 @@
     )(offsets, lengths, rab, arrived, *map(in_hbm, (cotangent, w_in, w_out)))
 
 
-def total_kernel(received_ref, back_hbm, out_ref, sems):
-    parts = 4
-    step = MEMBERS // parts
-    copies = []
-    for n in range(parts):
-        part = pl.ds(n * step, step)
-        copies.append(
-            pltpu.make_async_copy(back_hbm.at[part], out_ref.at[part, :, CHUNK:], sems.at[n])
-        )
-        copies[-1].start()
+def total_kernel(received_ref, back_ref, out_ref):
     total = received_ref[0].astype(F32)
     for m in range(1, MEMBERS):
         total += received_ref[m].astype(F32)
     total = (total * (1.0 / 256.0)).astype(BF16)
     out_ref[:, :, :CHUNK] = jnp.broadcast_to(total[None], (MEMBERS, PIECE, CHUNK))
-    for copy in copies:
-        copy.wait()
+    out_ref[:, :, CHUNK:] = back_ref[...]
 
 
 def total(received, back):
     return pl.pallas_call(
         total_kernel,
         out_shape=jax.ShapeDtypeStruct((MEMBERS, PIECE, CHUNK + D), BF16),
-        in_specs=[full_spec(), full_spec(pltpu.HBM)],
+        in_specs=[full_spec()] * 2,
         out_specs=full_spec(),
-        scratch_shapes=[pltpu.SemaphoreType.DMA((4,))],
         compiler_params=pltpu.CompilerParams(vmem_limit_bytes=VMEM_SMALL),
         cost_estimate=pl.CostEstimate(flops=1_000_000, bytes_accessed=4_000_000, transcendentals=0),
         name="total",
-    )(received, in_hbm(back))
+    )(received, back)
 
 
 def put_shares(source, rows_s, groups):
@@ -593,11 +558,16 @@
 
 
 def mine_kernel(
-    route_ref, received_ref, events_hbm, w_in_hbm, w_out_hbm, rows_s, events_s, sems
+    route_hbm, received_ref, events_hbm, w_in_hbm, w_out_hbm, route_s, rows_s, events_s, sems
 ):
-    copies = put_rows(rows_s, lax.axis_index("group"), w_in_hbm, w_out_hbm, sems, received_ref)
+    load = pltpu.make_async_copy(route_hbm, route_s, sems.at[9])
+    load.start()
+    copies = put_rows(
+        rows_s, lax.axis_index("group"), w_in_hbm, w_out_hbm, sems, received_ref
+    )
+    load.wait()
     for j in range(PIECES):
-        slot = lax.shift_right_logical(route_ref[j], 5)
+        slot = lax.shift_right_logical(route_s[j], 5)
         piece = received_ref[lax.shift_right_logical(slot, 2), lax.bitwise_and(slot, 3)]
         events_s[j * PIECE : (j + 1) * PIECE, :] = piece[:, CHUNK:]
     copies.append(pltpu.make_async_copy(events_s, events_hbm, sems.at[8]))
@@ -614,17 +584,18 @@
             jax.ShapeDtypeStruct((D, HID), F32),
             jax.ShapeDtypeStruct((D, D), F32),
         ),
-        in_specs=[full_spec(pltpu.SMEM), full_spec()],
+        in_specs=[full_spec(pltpu.HBM), full_spec()],
         out_specs=(full_spec(pltpu.HBM),) * 3,
         scratch_shapes=[
+            pltpu.SMEM((PIECES,), jnp.int32),
             pltpu.VMEM((HALF, HID + D), F32),
             pltpu.VMEM((ROWS, D), BF16),
-            pltpu.SemaphoreType.DMA((9,)),
+            pltpu.SemaphoreType.DMA((10,)),
         ],
         compiler_params=pltpu.CompilerParams(vmem_limit_bytes=VMEM_SMALL),
         cost_estimate=pl.CostEstimate(flops=0, bytes_accessed=6_000_000, transcendentals=0),
         name="mine_out",
-    )(route, received)
+    )(in_hbm(route), received)
 
 
 def theirs_kernel(theirs_ref, _, __, w_in_hbm, w_out_hbm, rows_s, sems):
@@ -658,13 +629,12 @@
     )
     swap = functools.partial(lax.ppermute, axis_name="group", perm=[(0, 1), (1, 0)])
     arrived = exchange(pack(route, events))
-    other, left, up, gh, bal, mixed = layer(
+    other, left, up, gh, bal, w_in_here, outputs = layer(
         block_offset, hist_length, rab, arrived, cotangent, w_in, w_out
     )
     got = swap(other)
-    joined = join(own_part(left, up, gh), got)
-    received = exchange(joined.reshape(MEMBERS, PIECE, CHUNK))
-    outputs, back = rest(block_offset, hist_length, gh, w_in, bal, up, arrived, mixed, w_out)
+    own, back = beside(block_offset, arrived, left, up, gh, bal, w_in_here)
+    received = exchange(join(own, got).reshape(MEMBERS, PIECE, CHUNK))
     received = exchange(total(received, back.reshape(MEMBERS, PIECE, D)))
     theirs = swap(received[:, :, :CHUNK])
     events_grad, w_in_grad, w_out_grad = mine_out(

time: 118 us -> 118 us (level)
  blocking collectives: 66.6 us -> 90.7 us
  waiting for transfers between devices: 14.8 us -> 0.87 us
  Pallas kernels: 24.9 us -> 19.2 us
  starting transfers between devices: 10.7 us -> 5.86 us
    all_to_all x0 -> x1, blocking collectives: none -> 24 us  [body(): received = exchange(join(own, got).reshape(MEMBERS, PIECE, CHUNK))]
    all_to_all x1 -> x0, waiting for transfers between devices: 12.7 us -> none  [body(): received = exchange(joined.reshape(MEMBERS, PIECE, CHUNK))]
    pallas_call x3 -> x2, Pallas kernels: 8.97 us -> 3.93 us  [the longest x1 3.63 us: beside(): pl.pallas_call(beside_kernel, out_shape=(jax.ShapeDtypeStruct(SHARES, BF1...]
    all_to_all x1 -> x0, starting transfers between devices: 4.86 us -> none  [body(): received = exchange(joined.reshape(MEMBERS, PIECE, CHUNK))]
    ppermute x1, waiting for transfers between devices: 1.77 us -> 0.01 us  [body(): got = swap(other)]
  transfers between devices with their start and end apart: 3 -> 2, of which waited for: 3 -> 1; matrix products, arithmetic and copies ran while one was open for 0% -> 0% of each run, Pallas kernels for 9% -> 5%
where the time goes in v5:
time: 118 us
  blocking collectives  90.7 us (77%)
  Pallas kernels  19.2 us (16%)
  starting transfers between devices  5.86 us (5%)
    all_to_all x1, blocking collectives, body(): received = exchange(total(received, back.reshape(MEMBERS, PIECE, D)))  36.9 us
    all_to_all x1, blocking collectives, body(): arrived = exchange(pack(route, events))  29.8 us
    all_to_all x1, blocking collectives, body(): received = exchange(join(own, got).reshape(MEMBERS, PIECE, CHUNK))  24 us
    pallas_call x1, Pallas kernels, layer(): pl.pallas_call(layer_kernel, out_shape=(jax.ShapeDtypeStruct(SHARES, BF16...  10.4 us
    pallas_call x1, Pallas kernels, beside(): pl.pallas_call(beside_kernel, out_shape=(jax.ShapeDtypeStruct(SHARES, BF1...  3.63 us
    ppermute x1, starting transfers between devices, body(): got = swap(other)  3.36 us
    ppermute x1, starting transfers between devices, body(): theirs = swap(received[:, :, :CHUNK])  2.5 us
  transfers between devices with their start and end apart: 2, of which 1 were waited for; matrix products, arithmetic and copies ran while one was open for 0% of the time, Pallas kernels for 5%

profile of v5, /device:TPU:1, one launch (start us, length us, event | category | flops | bytes accessed | tf_op | source)
XLA Modules:
  0.0 117.7 jit_solution(11549167592337637217)
XLA Ops:
  0.6 1.2 pack_pieces.1
  1.8 0.0 copy-start
  1.8 0.0 copy-start.1
  1.8 0.0 copy-start.2
  1.8 29.8 %all_to_all.15.arrived_ref = bf16[64,72,128]{2,1,0:T(8,128)(2,1)S(1)} all-to-all(bf16[64,72,128]{2,1,0:T(8,128)(2,1)S(1)} %pack_pieces.1), channel_id=1, replica_groups=mesh['group'=2,'member'=64] {'member'}, dimensions={0} | all-to-all | bytes 2359296 | tf_op jit(solution)/shard_map/all_to_all | solution.py:631
  31.7 0.0 copy-done
  31.7 0.0 copy-done.1
  31.7 0.0 copy-done.2
  31.7 10.4 %layer.1 = (bf16[16,4,16,640]{3,2,1,0:T(8,128)(2,1)S(1)}, bf16[2,256,512]{2,1,0:T(8,128)(2,1)S(1)}, bf16[512,512]{1,0:T(8,128)(2,1)S(1)}, bf16[512,2048]{1,0:T(8...) custom-call(s32[4]{0:T(128)S(1)} %copy-done.2, ...), custom_call_target="tpu_custom_call" | custom-call | flops 4000000000 | bytes 9000000 | tf_op jit(solution)/shard_map/layer/pallas_call | solution.py:489
  42.1 3.4 %collective-permute-start = (bf16[16,4,16,640]{3,2,1,0:T(8,128)(2,1)S(1)}, bf16[16,4,16,640]{3,2,1,0:T(8,128)(2,1)S(1)}, u32[]{:S(2)}, u32[]{:S(2)}) collective-permute-start(bf16[16,4,16,640]{3,2,1,0:T(8,128)(2,1)S(1)} %get-tuple-element.25), channel_id=1, source_target_pairs={{0,64},{64,0},{1,65},{65,1},{2,66},{66,2},{3,67},{67,3},{4,68},{68... | collective-permute-start | bytes 3932168 | tf_op jit(solution)/shard_map/ppermute | solution.py:635
  45.5 3.6 %beside.1 = (bf16[16,4,16,640]{3,2,1,0:T(8,128)(2,1)S(1)}, bf16[1024,512]{1,0:T(8,128)(2,1)S(1)}) custom-call(s32[4]{0:T(128)S(1)} %copy-done.2, bf16[64,72,128]{2,1,0:T(8,128)(2,1)S(1)} %all_to_all.15.arrived_ref, bf16[2,256,512]{2,1,0:T(8,128)(2,1)S(1)} %get-tuple-element.19.left_ref, bf16[512,512]{1,0:T(8,128)(2,1)S(1)} %get-tuple-element.20.up_ref, ...), custom_call_target="tpu_custom_call" | custom-call | flops 3000000000 | bytes 2000000 | tf_op jit(solution)/shard_map/beside/pallas_call | solution.py:431
  49.1 0.0 collective-permute-done.got_ref
  49.1 0.3 join.1
  49.4 24.0 %all_to_all.16.received_ref = bf16[64,16,640]{2,1,0:T(8,128)(2,1)S(1)} all-to-all(bf16[64,16,640]{2,1,0:T(8,128)(2,1)S(1)} %bitcast.5), channel_id=1, replica_groups=mesh['group'=2,'member'=64] {'member'}, dimensions={0} | all-to-all | bytes 2621440 | tf_op jit(solution)/shard_map/all_to_all | solution.py:637
  73.4 0.3 total.1
  73.7 36.9 %all_to_all.17 = bf16[64,16,1152]{2,1,0:T(8,128)(2,1)S(1)} all-to-all(bf16[64,16,1152]{2,1,0:T(8,128)(2,1)S(1)} %total.1), channel_id=1, replica_groups=mesh['group'=2,'member'=64] {'member'}, dimensions={0} | all-to-all | bytes 4718592 | tf_op jit(solution)/shard_map/all_to_all | solution.py:638
  110.6 0.1 slice.4
  110.8 2.5 %collective-permute-start.1 = (bf16[64,16,640]{2,1,0:T(8,128)(2,1)S(1)}, bf16[64,16,640]{2,1,0:T(8,128)(2,1)S(1)}, u32[]{:S(2)}, u32[]{:S(2)}) collective-permute-start(bf16[64,16,640]{2,1,0:T(8,128)(2,1)S(1)} %slice.4), channel_id=1, source_target_pairs={{0,64},{64,0},{1,65},{65,1},{2,66},{66,2},{3,67},{67,3},{4,68},{68... | collective-permute-start | bytes 3932168 | tf_op jit(solution)/shard_map/ppermute | solution.py:639
  113.3 1.8 %mine_out.1 = (bf16[512,512]{1,0:T(8,128)(2,1)}, f32[512,2048]{1,0:T(8,128)}, f32[512,512]{1,0:T(8,128)}) custom-call(s32[32]{0:T(128)} %route_hbm.3, bf16[16,4,16,1152]{3,2,1,0:T(8,128)(2,1)S(1)} %bitcast.4), custom_call_target="tpu_custom_call" | custom-call | bytes 6000000 | tf_op jit(solution)/shard_map/mine_out/pallas_call | solution.py:580
  115.0 0.9 collective-permute-done.1
  115.9 1.6 %theirs_out.1 = (f32[512,2048]{1,0:T(8,128)}, f32[512,512]{1,0:T(8,128)}) custom-call(bf16[16,4,16,640]{3,2,1,0:T(8,128)(2,1)S(1)} %bitcast.6, f32[512,2048]{1,0:T(8,128)} %get-tuple-element.28._, f32[512,512]{1,0:T(8,128)} %get-tuple-element.29.__), custom_call_target="tpu_custom_call", output_to_operand_aliasing={{0}: (1, {}), {1}: (2, {})} | custom-call | bytes 4000000 | tf_op jit(solution)/shard_map/theirs_out/pallas_call | solution.py:607
Async XLA Ops:
  1.8 29.9 %copy-start = (f32[4,12]{1,0:T(4,128)S(1)}, f32[4,12]{1,0:T(4,128)}, u32[]{:S(2)}) copy-start(f32[4,12]{1,0:T(4,128)} %rab_ref.1) | copy-start | bytes 580
  1.8 29.9 %copy-start.1 = (s32[4]{0:T(128)S(1)}, s32[4]{0:T(128)}, u32[]{:S(2)}) copy-start(s32[4]{0:T(128)} %length_ref.1) | copy-start | bytes 52
  1.8 29.8 %copy-start.2 = (s32[4]{0:T(128)S(1)}, s32[4]{0:T(128)}, u32[]{:S(2)}) copy-start(s32[4]{0:T(128)} %offset_ref.3) | copy-start | bytes 52
  42.1 7.0 %collective-permute-start = (bf16[16,4,16,640]{3,2,1,0:T(8,128)(2,1)S(1)}, bf16[16,4,16,640]{3,2,1,0:T(8,128)(2,1)S(1)}, u32[]{:S(2)}, u32[]{:S(2)}) collective-permute-start(bf16[16,4,16,640]{3,2,1,0:T(8,128)(2,1)S(1)} %get-tuple-element.25), channel_id=1, source_target_pairs={{0,64},{64,0},{1,65},{65,1},{2,66},{66,2},{3,67},{67,3},{4,68},{68... | collective-permute-start | bytes 3932168 | tf_op jit(solution)/shard_map/ppermute | solution.py:635
  110.8 5.2 %collective-permute-start.1 = (bf16[64,16,640]{2,1,0:T(8,128)(2,1)S(1)}, bf16[64,16,640]{2,1,0:T(8,128)(2,1)S(1)}, u32[]{:S(2)}, u32[]{:S(2)}) collective-permute-start(bf16[64,16,640]{2,1,0:T(8,128)(2,1)S(1)} %slice.4), channel_id=1, source_target_pairs={{0,64},{64,0},{1,65},{65,1},{2,66},{66,2},{3,67},{67,3},{4,68},{68... | collective-permute-start | bytes 3932168 | tf_op jit(solution)/shard_map/ppermute | solution.py:639

commit v6 on v5

--- a/solution.py
+++ b/solution.py
@@ -151,15 +151,14 @@
     length_ref,
     rab_ref,
     arrived_ref,
-    cot_hbm,
-    w_in_hbm,
-    w_out_hbm,
+    cot_ref,
+    w_in_ref,
+    w_out_ref,
     other_ref,
     left_ref,
     up_ref,
     gh_ref,
     bal_ref,
-    w_in_ref,
     out_hbm,
     place_s,
     norm_s,
@@ -174,22 +173,10 @@
     gm_s,
     gctx_s,
     trans_s,
-    cot_ref,
-    w_out_ref,
     mixed_ref,
     out_s,
-    sems,
+    sem,
 ):
-    copies = []
-    for n, start in enumerate((1024, 1536, 512, 0)):
-        cols = pl.ds(start, D)
-        copies.append(
-            pltpu.make_async_copy(w_in_hbm.at[:, cols], w_in_ref.at[:, cols], sems.at[n])
-        )
-    copies.append(pltpu.make_async_copy(cot_hbm, cot_ref, sems.at[4]))
-    copies.append(pltpu.make_async_copy(w_out_hbm, w_out_ref, sems.at[5]))
-    for copy in copies:
-        copy.start()
     core = lax.axis_index("group")
     order = block_order(offset_ref)
     long_rows, short_rows = slice(0, 2 * BLOCK), slice(2 * BLOCK, 4 * BLOCK)
@@ -341,13 +328,9 @@
     for r in range(0, 256, 64):
         norm(r)
     for k, n in enumerate(parts):
-        if k in (0, 1, 4, 6):
-            copies[(0, 1, 4, 6).index(k)].wait()
         project(long_rows, n)
         if k < 4:
             norm(256 + 64 * k)
-    for copy in copies[4:]:
-        copy.wait()
     for i in range(BLOCKS):
         upstream(i)
     gm_s[...] = dot_nt(up_ref[...], w_out_ref[...])
@@ -365,8 +348,8 @@
         middle(256 + 64 * head)
     trans_s[1] = mixed_ref[...].T
     output(short_rows)
-    copies.append(pltpu.make_async_copy(out_s, out_hbm, sems.at[6]))
-    copies[-1].start()
+    out_copy = pltpu.make_async_copy(out_s, out_hbm, sem)
+    out_copy.start()
     for head in range(HEADS):
         short_back(head)
 
@@ -379,7 +362,7 @@
         other_ref[at] = value.astype(BF16)
 
     weight_grads(trans_s[0, other_rows, :], trans_s[1, other_rows, :], gh_ref, up_ref, store)
-    copies[-1].wait()
+    out_copy.wait()
 
 
 def weight_grads(normed_t, mixed_t, gh_ref, up_ref, store):
@@ -481,8 +464,6 @@
         ((ROWS, D), BF16),
         ((2, D, ROWS), BF16),
         ((ROWS, D), BF16),
-        ((D, D), BF16),
-        ((ROWS, D), BF16),
         ((ROWS, D), BF16),
     ]
     rows = jax.ShapeDtypeStruct((ROWS, D), BF16)
@@ -494,19 +475,18 @@
             rows,
             jax.ShapeDtypeStruct((ROWS, HID), BF16),
             rows,
-            jax.ShapeDtypeStruct((D, HID), BF16),
             pltpu.HBM((ROWS, D), BF16),
         ),
-        in_specs=[full_spec(pltpu.SMEM)] * 3 + [full_spec()] + [full_spec(pltpu.HBM)] * 3,
-        out_specs=(full_spec(),) * 6 + (full_spec(pltpu.HBM),),
+        in_specs=[full_spec(pltpu.SMEM)] * 3 + [full_spec()] * 4,
+        out_specs=(full_spec(),) * 5 + (full_spec(pltpu.HBM),),
         scratch_shapes=[pltpu.VMEM(shape, kind) for shape, kind in scratch]
-        + [pltpu.SemaphoreType.DMA((7,))],
+        + [pltpu.SemaphoreType.DMA],
         compiler_params=pltpu.CompilerParams(vmem_limit_bytes=VMEM_LIMIT),
         cost_estimate=pl.CostEstimate(
             flops=4_000_000_000, bytes_accessed=9_000_000, transcendentals=1_500_000
         ),
         name="layer",
-    )(offsets, lengths, rab, arrived, *map(in_hbm, (cotangent, w_in, w_out)))
+    )(offsets, lengths, rab, arrived, cotangent, w_in, w_out)
 
 
 def total_kernel(received_ref, back_ref, out_ref):
@@ -629,11 +609,11 @@
     )
     swap = functools.partial(lax.ppermute, axis_name="group", perm=[(0, 1), (1, 0)])
     arrived = exchange(pack(route, events))
-    other, left, up, gh, bal, w_in_here, outputs = layer(
+    other, left, up, gh, bal, outputs = layer(
         block_offset, hist_length, rab, arrived, cotangent, w_in, w_out
     )
     got = swap(other)
-    own, back = beside(block_offset, arrived, left, up, gh, bal, w_in_here)
+    own, back = beside(block_offset, arrived, left, up, gh, bal, w_in)
     received = exchange(join(own, got).reshape(MEMBERS, PIECE, CHUNK))
     received = exchange(total(received, back.reshape(MEMBERS, PIECE, D)))
     theirs = swap(received[:, :, :CHUNK])

time: 118 us -> 116 us (0.983)
  Pallas kernels: 19.2 us -> 17.6 us
    pallas_call x1, Pallas kernels: 10.4 us -> 8.72 us  [layer(): pl.pallas_call(layer_kernel, out_shape=(jax.ShapeDtypeStruct(SHARES, BF16...]
where the time goes in v6:
time: 116 us
  blocking collectives  90.7 us (78%)
  Pallas kernels  17.6 us (15%)
  starting transfers between devices  5.69 us (5%)
    all_to_all x1, blocking collectives, body(): received = exchange(total(received, back.reshape(MEMBERS, PIECE, D)))  36.9 us
    all_to_all x1, blocking collectives, body(): arrived = exchange(pack(route, events))  29.8 us
    all_to_all x1, blocking collectives, body(): received = exchange(join(own, got).reshape(MEMBERS, PIECE, CHUNK))  24 us
    pallas_call x1, Pallas kernels, layer(): pl.pallas_call(layer_kernel, out_shape=(jax.ShapeDtypeStruct(SHARES, BF16...  8.72 us
    pallas_call x1, Pallas kernels, beside(): pl.pallas_call(beside_kernel, out_shape=(jax.ShapeDtypeStruct(SHARES, BF1...  3.63 us
    ppermute x1, starting transfers between devices, body(): got = swap(other)  3.19 us
    ppermute x1, starting transfers between devices, body(): theirs = swap(received[:, :, :CHUNK])  2.5 us
  transfers between devices with their start and end apart: 2, of which 1 were waited for; matrix products, arithmetic and copies ran while one was open for 0% of the time, Pallas kernels for 5%

profile of v6, /device:TPU:1, one launch (start us, length us, event | category | flops | bytes accessed | tf_op | source)
XLA Modules:
  0.0 116.0 jit_solution(11807339182354596831)
XLA Ops:
  0.6 0.0 copy-start.1
  0.6 0.0 copy-start.2
  0.7 1.3 %pack_pieces.1 = bf16[64,72,128]{2,1,0:T(8,128)(2,1)S(1)} custom-call(s32[32]{0:T(128)} %route_hbm.3, bf16[512,512]{1,0:T(8,128)(2,1)} %events_hbm.1), custom_call_target="tpu_custom_call" | custom-call | tf_op jit(solution)/shard_map/pack_pieces/pallas_call | solution.py:77
  1.9 0.0 copy-start
  1.9 0.0 copy-start.3
  1.9 0.0 copy-start.4
  1.9 0.0 copy-start.5
  2.0 29.8 %all_to_all.15.arrived_ref = bf16[64,72,128]{2,1,0:T(8,128)(2,1)S(1)} all-to-all(bf16[64,72,128]{2,1,0:T(8,128)(2,1)S(1)} %pack_pieces.1), channel_id=1, replica_groups=mesh['group'=2,'member'=64] {'member'}, dimensions={0} | all-to-all | bytes 2359296 | tf_op jit(solution)/shard_map/all_to_all | solution.py:611
  31.8 0.0 copy-done.1
  31.8 0.0 copy-done.2
  31.8 0.0 copy-done
  31.8 0.0 copy-done.3
  31.8 0.0 copy-done.4
  31.8 0.0 copy-done.5
  31.8 8.7 %layer.1 = (bf16[16,4,16,640]{3,2,1,0:T(8,128)(2,1)S(1)}, bf16[2,256,512]{2,1,0:T(8,128)(2,1)S(1)}, bf16[512,512]{1,0:T(8,128)(2,1)S(1)}, bf16[512,2048]{1,0:T(8...) custom-call(s32[4]{0:T(128)S(1)} %copy-done.5, s32[4]{0:T(128)S(1)} %copy-done.4, ...), custom_call_target="tpu_custom_call" | custom-call | flops 4000000000 | bytes 9000000 | tf_op jit(solution)/shard_map/layer/pallas_call | solution.py:470
  40.6 3.2 %collective-permute-start = (bf16[16,4,16,640]{3,2,1,0:T(8,128)(2,1)S(1)}, bf16[16,4,16,640]{3,2,1,0:T(8,128)(2,1)S(1)}, u32[]{:S(2)}, u32[]{:S(2)}) collective-permute-start(bf16[16,4,16,640]{3,2,1,0:T(8,128)(2,1)S(1)} %get-tuple-element.23), channel_id=1, source_target_pairs={{0,64},{64,0},{1,65},{65,1},{2,66},{66,2},{3,67},{67,3},{4,68},{68... | collective-permute-start | bytes 3932168 | tf_op jit(solution)/shard_map/ppermute | solution.py:615
  43.7 3.6 %beside.1 = (bf16[16,4,16,640]{3,2,1,0:T(8,128)(2,1)S(1)}, bf16[1024,512]{1,0:T(8,128)(2,1)S(1)}) custom-call(s32[4]{0:T(128)S(1)} %copy-done.5, bf16[64,72,128]{2,1,0:T(8,128)(2,1)S(1)} %all_to_all.15.arrived_ref, bf16[2,256,512]{2,1,0:T(8,128)(2,1)S(1)} %get-tuple-element.18.left_ref, bf16[512,512]{1,0:T(8,128)(2,1)S(1)} %get-tuple-element.19.up_ref, ...), custom_call_target="tpu_custom_call" | custom-call | flops 3000000000 | bytes 2000000 | tf_op jit(solution)/shard_map/beside/pallas_call | solution.py:414
  47.4 0.0 collective-permute-done.got_ref
  47.4 0.3 join.1
  47.7 24.0 %all_to_all.16.received_ref = bf16[64,16,640]{2,1,0:T(8,128)(2,1)S(1)} all-to-all(bf16[64,16,640]{2,1,0:T(8,128)(2,1)S(1)} %bitcast.5), channel_id=1, replica_groups=mesh['group'=2,'member'=64] {'member'}, dimensions={0} | all-to-all | bytes 2621440 | tf_op jit(solution)/shard_map/all_to_all | solution.py:617
  71.7 0.3 total.1
  72.0 36.9 %all_to_all.17 = bf16[64,16,1152]{2,1,0:T(8,128)(2,1)S(1)} all-to-all(bf16[64,16,1152]{2,1,0:T(8,128)(2,1)S(1)} %total.1), channel_id=1, replica_groups=mesh['group'=2,'member'=64] {'member'}, dimensions={0} | all-to-all | bytes 4718592 | tf_op jit(solution)/shard_map/all_to_all | solution.py:618
  108.9 0.1 slice.4
  109.1 2.5 %collective-permute-start.1 = (bf16[64,16,640]{2,1,0:T(8,128)(2,1)S(1)}, bf16[64,16,640]{2,1,0:T(8,128)(2,1)S(1)}, u32[]{:S(2)}, u32[]{:S(2)}) collective-permute-start(bf16[64,16,640]{2,1,0:T(8,128)(2,1)S(1)} %slice.4), channel_id=1, source_target_pairs={{0,64},{64,0},{1,65},{65,1},{2,66},{66,2},{3,67},{67,3},{4,68},{68... | collective-permute-start | bytes 3932168 | tf_op jit(solution)/shard_map/ppermute | solution.py:619
  111.6 1.8 %mine_out.1 = (bf16[512,512]{1,0:T(8,128)(2,1)}, f32[512,2048]{1,0:T(8,128)}, f32[512,512]{1,0:T(8,128)}) custom-call(s32[32]{0:T(128)} %route_hbm.3, bf16[16,4,16,1152]{3,2,1,0:T(8,128)(2,1)S(1)} %bitcast.4), custom_call_target="tpu_custom_call" | custom-call | bytes 6000000 | tf_op jit(solution)/shard_map/mine_out/pallas_call | solution.py:560
  113.3 0.9 collective-permute-done.1
  114.2 1.6 %theirs_out.1 = (f32[512,2048]{1,0:T(8,128)}, f32[512,512]{1,0:T(8,128)}) custom-call(bf16[16,4,16,640]{3,2,1,0:T(8,128)(2,1)S(1)} %bitcast.6, f32[512,2048]{1,0:T(8,128)} %get-tuple-element.26._, f32[512,512]{1,0:T(8,128)} %get-tuple-element.27.__), custom_call_target="tpu_custom_call", output_to_operand_aliasing={{0}: (1, {}), {1}: (2, {})} | custom-call | bytes 4000000 | tf_op jit(solution)/shard_map/theirs_out/pallas_call | solution.py:587
Async XLA Ops:
  0.6 31.2 %copy-start.1 = (bf16[512,512]{1,0:T(8,128)(2,1)S(1)}, bf16[512,512]{1,0:T(8,128)(2,1)}, u32[]{:S(2)}) copy-start(bf16[512,512]{1,0:T(8,128)(2,1)} %cot_ref.1) | copy-start | bytes 1572868
  0.6 31.1 %copy-start.2 = (bf16[512,512]{1,0:T(8,128)(2,1)S(1)}, bf16[512,512]{1,0:T(8,128)(2,1)}, u32[]{:S(2)}) copy-start(bf16[512,512]{1,0:T(8,128)(2,1)} %w_out_ref.1) | copy-start | bytes 1572868
  1.9 29.9 %copy-start = (bf16[512,2048]{1,0:T(8,128)(2,1)S(1)}, bf16[512,2048]{1,0:T(8,128)(2,1)}, u32[]{:S(2)}) copy-start(bf16[512,2048]{1,0:T(8,128)(2,1)} %w_in_ref.3) | copy-start | bytes 6291460
  1.9 29.9 %copy-start.3 = (f32[4,12]{1,0:T(4,128)S(1)}, f32[4,12]{1,0:T(4,128)}, u32[]{:S(2)}) copy-start(f32[4,12]{1,0:T(4,128)} %rab_ref.1) | copy-start | bytes 580
  1.9 29.9 %copy-start.4 = (s32[4]{0:T(128)S(1)}, s32[4]{0:T(128)}, u32[]{:S(2)}) copy-start(s32[4]{0:T(128)} %length_ref.1) | copy-start | bytes 52
  1.9 29.9 %copy-start.5 = (s32[4]{0:T(128)S(1)}, s32[4]{0:T(128)}, u32[]{:S(2)}) copy-start(s32[4]{0:T(128)} %offset_ref.3) | copy-start | bytes 52
  40.6 6.8 %collective-permute-start = (bf16[16,4,16,640]{3,2,1,0:T(8,128)(2,1)S(1)}, bf16[16,4,16,640]{3,2,1,0:T(8,128)(2,1)S(1)}, u32[]{:S(2)}, u32[]{:S(2)}) collective-permute-start(bf16[16,4,16,640]{3,2,1,0:T(8,128)(2,1)S(1)} %get-tuple-element.23), channel_id=1, source_target_pairs={{0,64},{64,0},{1,65},{65,1},{2,66},{66,2},{3,67},{67,3},{4,68},{68... | collective-permute-start | bytes 3932168 | tf_op jit(solution)/shard_map/ppermute | solution.py:615
  109.1 5.2 %collective-permute-start.1 = (bf16[64,16,640]{2,1,0:T(8,128)(2,1)S(1)}, bf16[64,16,640]{2,1,0:T(8,128)(2,1)S(1)}, u32[]{:S(2)}, u32[]{:S(2)}) collective-permute-start(bf16[64,16,640]{2,1,0:T(8,128)(2,1)S(1)} %slice.4), channel_id=1, source_target_pairs={{0,64},{64,0},{1,65},{65,1},{2,66},{66,2},{3,67},{67,3},{4,68},{68... | collective-permute-start | bytes 3932168 | tf_op jit(solution)/shard_map/ppermute | solution.py:619

commit v7 on v6

--- a/solution.py
+++ b/solution.py
@@ -159,7 +159,7 @@
     up_ref,
     gh_ref,
     bal_ref,
-    out_hbm,
+    mixed_ref,
     place_s,
     norm_s,
     hid_s,
@@ -173,9 +173,6 @@
     gm_s,
     gctx_s,
     trans_s,
-    mixed_ref,
-    out_s,
-    sem,
 ):
     core = lax.axis_index("group")
     order = block_order(offset_ref)
@@ -279,15 +276,6 @@
         gm = gm_s[sl, :]
         gh_ref[sl, 0:D] = (gm * n * slope_s[sl, 0:D]).astype(BF16)
         gctx_s[sl, :] = normalized_back(gm * u, n, rstd).astype(BF16)
-
-    def output(rows):
-        product = dot(mixed_ref[rows, :], w_out_ref[...])
-        for i in range(rows.start // BLOCK, rows.stop // BLOCK):
-            here = slice(i * BLOCK, (i + 1) * BLOCK)
-            there = slice(here.start - rows.start, here.stop - rows.start)
-            value = bal_ref[here, :].astype(F32) + product[there, :]
-            value = jnp.where(live_column(length_ref, order, i), value, 0.0)
-            out_s[block_rows(order, i), :] = value.astype(BF16)
 
     def finish_grads(rows, head, gv, gq, gk):
         for part, grad in ((1, gv), (2, gq * SCALE), (3, gk * SCALE)):
@@ -342,14 +330,10 @@
         middle(64 * head)
         short_attend(head)
     trans_s[0] = norm_s[...].T
-    output(long_rows)
     for head in range(HEADS):
         long_back(head)
         middle(256 + 64 * head)
     trans_s[1] = mixed_ref[...].T
-    output(short_rows)
-    out_copy = pltpu.make_async_copy(out_s, out_hbm, sem)
-    out_copy.start()
     for head in range(HEADS):
         short_back(head)
 
@@ -362,7 +346,6 @@
         other_ref[at] = value.astype(BF16)
 
     weight_grads(trans_s[0, other_rows, :], trans_s[1, other_rows, :], gh_ref, up_ref, store)
-    out_copy.wait()
 
 
 def weight_grads(normed_t, mixed_t, gh_ref, up_ref, store):
@@ -463,8 +446,6 @@
         ((ROWS, D), F32),
         ((ROWS, D), BF16),
         ((2, D, ROWS), BF16),
-        ((ROWS, D), BF16),
-        ((ROWS, D), BF16),
     ]
     rows = jax.ShapeDtypeStruct((ROWS, D), BF16)
     return pl.pallas_call(
@@ -475,12 +456,11 @@
             rows,
             jax.ShapeDtypeStruct((ROWS, HID), BF16),
             rows,
-            pltpu.HBM((ROWS, D), BF16),
+            rows,
         ),
         in_specs=[full_spec(pltpu.SMEM)] * 3 + [full_spec()] * 4,
-        out_specs=(full_spec(),) * 5 + (full_spec(pltpu.HBM),),
-        scratch_shapes=[pltpu.VMEM(shape, kind) for shape, kind in scratch]
-        + [pltpu.SemaphoreType.DMA],
+        out_specs=(full_spec(),) * 6,
+        scratch_shapes=[pltpu.VMEM(shape, kind) for shape, kind in scratch],
         compiler_params=pltpu.CompilerParams(vmem_limit_bytes=VMEM_LIMIT),
         cost_estimate=pl.CostEstimate(
             flops=4_000_000_000, bytes_accessed=9_000_000, transcendentals=1_500_000
@@ -518,14 +498,14 @@
             rows_s[g * PIECE : (g + 1) * PIECE, at : at + CHUNK] = value
 
 
-def put_rows(rows_s, half, w_in_hbm, w_out_hbm, sems, source):
+def put_rows(rows_s, first, w_in_hbm, w_out_hbm, sems, source):
     copies = []
-    parts = 4
-    height = HALF // parts
+    height = 64
+    parts = rows_s.shape[0] // height
     for part in range(parts):
         put_shares(source, rows_s, range(part * height // PIECE, (part + 1) * height // PIECE))
         here = slice(part * height, (part + 1) * height)
-        there = pl.ds(pl.multiple_of(half * HALF + part * height, height), height)
+        there = pl.ds(pl.multiple_of(first + part * height, height), height)
         for n, copy in enumerate(
             (
                 (rows_s.at[here, :HID], w_in_hbm.at[there]),
@@ -538,12 +518,37 @@
 
 
 def mine_kernel(
-    route_hbm, received_ref, events_hbm, w_in_hbm, w_out_hbm, route_s, rows_s, events_s, sems
+    route_hbm,
+    offset_ref,
+    length_ref,
+    received_ref,
+    bal_ref,
+    mixed_ref,
+    w_out_ref,
+    events_hbm,
+    w_in_grad_hbm,
+    w_out_grad_hbm,
+    out_hbm,
+    route_s,
+    rows_s,
+    events_s,
+    product_s,
+    out_s,
+    sems,
 ):
     load = pltpu.make_async_copy(route_hbm, route_s, sems.at[9])
     load.start()
-    copies = put_rows(
-        rows_s, lax.axis_index("group"), w_in_hbm, w_out_hbm, sems, received_ref
+    product_s[...] = dot(mixed_ref[...], w_out_ref[...])
+    order = block_order(offset_ref)
+    for i in range(BLOCKS):
+        rows = slice(i * BLOCK, (i + 1) * BLOCK)
+        value = bal_ref[rows, :].astype(F32) + product_s[rows, :]
+        value = jnp.where(live_column(length_ref, order, i), value, 0.0)
+        out_s[block_rows(order, i), :] = value.astype(BF16)
+    copies = [pltpu.make_async_copy(out_s, out_hbm, sems.at[10])]
+    copies[0].start()
+    copies += put_rows(
+        rows_s, lax.axis_index("group") * HALF, w_in_grad_hbm, w_out_grad_hbm, sems, received_ref
     )
     load.wait()
     for j in range(PIECES):
@@ -556,30 +561,37 @@
         copy.wait()
 
 
-def mine_out(route, received):
+def mine_out(route, offsets, lengths, received, bal, mixed, w_out):
+    rows = (ROWS, D)
     return pl.pallas_call(
         mine_kernel,
         out_shape=(
-            jax.ShapeDtypeStruct((ROWS, D), BF16),
+            jax.ShapeDtypeStruct(rows, BF16),
             jax.ShapeDtypeStruct((D, HID), F32),
             jax.ShapeDtypeStruct((D, D), F32),
+            jax.ShapeDtypeStruct(rows, BF16),
         ),
-        in_specs=[full_spec(pltpu.HBM), full_spec()],
-        out_specs=(full_spec(pltpu.HBM),) * 3,
+        in_specs=[full_spec(pltpu.HBM)] + [full_spec(pltpu.SMEM)] * 2 + [full_spec()] * 4,
+        out_specs=(full_spec(pltpu.HBM),) * 4,
         scratch_shapes=[
             pltpu.SMEM((PIECES,), jnp.int32),
             pltpu.VMEM((HALF, HID + D), F32),
-            pltpu.VMEM((ROWS, D), BF16),
-            pltpu.SemaphoreType.DMA((10,)),
+            pltpu.VMEM(rows, BF16),
+            pltpu.VMEM(rows, F32),
+            pltpu.VMEM(rows, BF16),
+            pltpu.SemaphoreType.DMA((11,)),
         ],
         compiler_params=pltpu.CompilerParams(vmem_limit_bytes=VMEM_SMALL),
-        cost_estimate=pl.CostEstimate(flops=0, bytes_accessed=6_000_000, transcendentals=0),
+        cost_estimate=pl.CostEstimate(
+            flops=300_000_000, bytes_accessed=6_000_000, transcendentals=0
+        ),
         name="mine_out",
-    )(in_hbm(route), received)
+    )(in_hbm(route), offsets, lengths, received, bal, mixed, w_out)
 
 
 def theirs_kernel(theirs_ref, _, __, w_in_hbm, w_out_hbm, rows_s, sems):
-    for copy in put_rows(rows_s, 1 - lax.axis_index("group"), w_in_hbm, w_out_hbm, sems, theirs_ref):
+    first = (1 - lax.axis_index("group")) * HALF
+    for copy in put_rows(rows_s, first, w_in_hbm, w_out_hbm, sems, theirs_ref):
         copy.wait()
 
 
@@ -598,7 +610,7 @@
         ],
         input_output_aliases={1: 0, 2: 1},
         compiler_params=pltpu.CompilerParams(vmem_limit_bytes=VMEM_SMALL),
-        cost_estimate=pl.CostEstimate(flops=0, bytes_accessed=4_000_000, transcendentals=0),
+        cost_estimate=pl.CostEstimate(flops=0, bytes_accessed=2_000_000, transcendentals=0),
         name="theirs_out",
     )(theirs, w_in_grad, w_out_grad)
 
@@ -609,7 +621,7 @@
     )
     swap = functools.partial(lax.ppermute, axis_name="group", perm=[(0, 1), (1, 0)])
     arrived = exchange(pack(route, events))
-    other, left, up, gh, bal, outputs = layer(
+    other, left, up, gh, bal, mixed = layer(
         block_offset, hist_length, rab, arrived, cotangent, w_in, w_out
     )
     got = swap(other)
@@ -617,8 +629,14 @@
     received = exchange(join(own, got).reshape(MEMBERS, PIECE, CHUNK))
     received = exchange(total(received, back.reshape(MEMBERS, PIECE, D)))
     theirs = swap(received[:, :, :CHUNK])
-    events_grad, w_in_grad, w_out_grad = mine_out(
-        route, received.reshape(*SHARES[:3], CHUNK + D)
+    events_grad, w_in_grad, w_out_grad, outputs = mine_out(
+        route,
+        block_offset,
+        hist_length,
+        received.reshape(*SHARES[:3], CHUNK + D),
+        bal,
+        mixed,
+        w_out,
     )
     w_in_grad, w_out_grad = theirs_out(theirs.reshape(SHARES), w_in_grad, w_out_grad)
     return outputs, events_grad, w_in_grad, w_out_grad

time: 116 us -> 116 us (level)
    pallas_call x1, Pallas kernels: 1.78 us -> 2.95 us  [mine_out(): pl.pallas_call(mine_kernel, out_shape=(jax.ShapeDtypeStruct(rows, BF16),...]
  transfers between devices with their start and end apart: 2 -> 2, of which waited for: 1 -> 0; matrix products, arithmetic and copies ran while one was open for 0% -> 0% of each run, Pallas kernels for 5% -> 6%
where the time goes in v7:
time: 116 us
  blocking collectives  90.7 us (78%)
  Pallas kernels  18.5 us (16%)
  starting transfers between devices  5.67 us (5%)
    all_to_all x1, blocking collectives, body(): received = exchange(total(received, back.reshape(MEMBERS, PIECE, D)))  36.9 us
    all_to_all x1, blocking collectives, body(): arrived = exchange(pack(route, events))  29.8 us
    all_to_all x1, blocking collectives, body(): received = exchange(join(own, got).reshape(MEMBERS, PIECE, CHUNK))  24 us
    pallas_call x1, Pallas kernels, layer(): pl.pallas_call(layer_kernel, out_shape=(jax.ShapeDtypeStruct(SHARES, BF16...  8.45 us
    pallas_call x1, Pallas kernels, beside(): pl.pallas_call(beside_kernel, out_shape=(jax.ShapeDtypeStruct(SHARES, BF1...  3.63 us
    ppermute x1, starting transfers between devices, body(): got = swap(other)  3.17 us
    pallas_call x1, Pallas kernels, mine_out(): pl.pallas_call(mine_kernel, out_shape=(jax.ShapeDtypeStruct(rows, BF16),...  2.95 us
    ppermute x1, starting transfers between devices, body(): theirs = swap(received[:, :, :CHUNK])  2.5 us
  transfers between devices with their start and end apart: 2, of which 0 were waited for; matrix products, arithmetic and copies ran while one was open for 0% of the time, Pallas kernels for 6%

profile of v7, /device:TPU:1, one launch (start us, length us, event | category | flops | bytes accessed | tf_op | source)
XLA Modules:
  0.0 116.0 jit_solution(11499456402947086585)
XLA Ops:
  0.6 0.0 copy-start.3
  0.6 1.3 %pack_pieces.1 = bf16[64,72,128]{2,1,0:T(8,128)(2,1)S(1)} custom-call(s32[32]{0:T(128)} %route_hbm.3, bf16[512,512]{1,0:T(8,128)(2,1)} %events_hbm.1), custom_call_target="tpu_custom_call" | custom-call | tf_op jit(solution)/shard_map/pack_pieces/pallas_call | solution.py:77
  2.0 0.0 copy-start
  2.0 0.0 copy-start.1
  2.0 0.0 copy-start.2
  2.0 0.0 copy-start.4
  2.0 0.0 copy-start.5
  2.0 29.8 %all_to_all.15.arrived_ref = bf16[64,72,128]{2,1,0:T(8,128)(2,1)S(1)} all-to-all(bf16[64,72,128]{2,1,0:T(8,128)(2,1)S(1)} %pack_pieces.1), channel_id=1, replica_groups=mesh['group'=2,'member'=64] {'member'}, dimensions={0} | all-to-all | bytes 2359296 | tf_op jit(solution)/shard_map/all_to_all | solution.py:623
  31.8 0.0 copy-done.3
  31.9 0.0 copy-done
  31.9 0.0 copy-done.1
  31.9 0.0 copy-done.2
  31.9 0.0 copy-done.4
  31.9 0.0 copy-done.5
  31.9 8.4 %layer.1 = (bf16[16,4,16,640]{3,2,1,0:T(8,128)(2,1)S(1)}, bf16[2,256,512]{2,1,0:T(8,128)(2,1)S(1)}, bf16[512,512]{1,0:T(8,128)(2,1)S(1)}, bf16[512,2048]{1,0:T(8...) custom-call(s32[4]{0:T(128)S(1)} %copy-done.1, s32[4]{0:T(128)S(1)} %copy-done.2, ...), custom_call_target="tpu_custom_call" | custom-call | flops 4000000000 | bytes 9000000 | tf_op jit(solution)/shard_map/layer/pallas_call | solution.py:451
  40.3 3.2 %collective-permute-start = (bf16[16,4,16,640]{3,2,1,0:T(8,128)(2,1)S(1)}, bf16[16,4,16,640]{3,2,1,0:T(8,128)(2,1)S(1)}, u32[]{:S(2)}, u32[]{:S(2)}) collective-permute-start(bf16[16,4,16,640]{3,2,1,0:T(8,128)(2,1)S(1)} %get-tuple-element.23), channel_id=1, source_target_pairs={{0,64},{64,0},{1,65},{65,1},{2,66},{66,2},{3,67},{67,3},{4,68},{68... | collective-permute-start | bytes 3932168 | tf_op jit(solution)/shard_map/ppermute | solution.py:627
  43.5 3.6 %beside.1 = (bf16[16,4,16,640]{3,2,1,0:T(8,128)(2,1)S(1)}, bf16[1024,512]{1,0:T(8,128)(2,1)S(1)}) custom-call(s32[4]{0:T(128)S(1)} %copy-done.1, bf16[64,72,128]{2,1,0:T(8,128)(2,1)S(1)} %all_to_all.15.arrived_ref, bf16[2,256,512]{2,1,0:T(8,128)(2,1)S(1)} %get-tuple-element.18.left_ref, bf16[512,512]{1,0:T(8,128)(2,1)S(1)} %get-tuple-element.19.up_ref, ...), custom_call_target="tpu_custom_call" | custom-call | flops 3000000000 | bytes 2000000 | tf_op jit(solution)/shard_map/beside/pallas_call | solution.py:397
  47.2 0.0 collective-permute-done.got_ref
  47.2 0.3 join.1
  47.5 24.0 %all_to_all.16.received_ref = bf16[64,16,640]{2,1,0:T(8,128)(2,1)S(1)} all-to-all(bf16[64,16,640]{2,1,0:T(8,128)(2,1)S(1)} %bitcast.5), channel_id=1, replica_groups=mesh['group'=2,'member'=64] {'member'}, dimensions={0} | all-to-all | bytes 2621440 | tf_op jit(solution)/shard_map/all_to_all | solution.py:629
  71.5 0.3 total.1
  71.8 36.9 %all_to_all.17 = bf16[64,16,1152]{2,1,0:T(8,128)(2,1)S(1)} all-to-all(bf16[64,16,1152]{2,1,0:T(8,128)(2,1)S(1)} %total.1), channel_id=1, replica_groups=mesh['group'=2,'member'=64] {'member'}, dimensions={0} | all-to-all | bytes 4718592 | tf_op jit(solution)/shard_map/all_to_all | solution.py:630
  108.7 0.1 slice.4
  108.8 2.5 %collective-permute-start.1 = (bf16[64,16,640]{2,1,0:T(8,128)(2,1)S(1)}, bf16[64,16,640]{2,1,0:T(8,128)(2,1)S(1)}, u32[]{:S(2)}, u32[]{:S(2)}) collective-permute-start(bf16[64,16,640]{2,1,0:T(8,128)(2,1)S(1)} %slice.4), channel_id=1, source_target_pairs={{0,64},{64,0},{1,65},{65,1},{2,66},{66,2},{3,67},{67,3},{4,68},{68... | collective-permute-start | bytes 3932168 | tf_op jit(solution)/shard_map/ppermute | solution.py:631
  111.3 2.9 %mine_out.1 = (bf16[512,512]{1,0:T(8,128)(2,1)}, f32[512,2048]{1,0:T(8,128)}, f32[512,512]{1,0:T(8,128)}, bf16[512,512]{1,0:T(8,128)(2,1)}) custom-call(s32[32]{0:T(128)} %route_hbm.3, s32[4]{0:T(128)S(1)} %copy-done.1, s32[4]{0:T(128)S(1)} %copy-done.2, bf16[16,4,16,1152]{3,2,1,0:T(8,128)(2,1)S(1)} %bitcast.4, ...), custom_call_target="tpu_custom_call" | custom-call | flops 300000000 | bytes 6000000 | tf_op jit(solution)/shard_map/mine_out/pallas_call | solution.py:566
  114.3 0.0 collective-permute-done.1
  114.3 1.6 %theirs_out.1 = (f32[512,2048]{1,0:T(8,128)}, f32[512,512]{1,0:T(8,128)}) custom-call(bf16[16,4,16,640]{3,2,1,0:T(8,128)(2,1)S(1)} %bitcast.6, f32[512,2048]{1,0:T(8,128)} %get-tuple-element.28._, f32[512,512]{1,0:T(8,128)} %get-tuple-element.29.__), custom_call_target="tpu_custom_call", output_to_operand_aliasing={{0}: (1, {}), {1}: (2, {})} | custom-call | bytes 2000000 | tf_op jit(solution)/shard_map/theirs_out/pallas_call | solution.py:599
Async XLA Ops:
  0.6 31.2 %copy-start.3 = (bf16[512,2048]{1,0:T(8,128)(2,1)S(1)}, bf16[512,2048]{1,0:T(8,128)(2,1)}, u32[]{:S(2)}) copy-start(bf16[512,2048]{1,0:T(8,128)(2,1)} %w_in_ref.3) | copy-start | bytes 6291460
  2.0 29.9 %copy-start = (bf16[512,512]{1,0:T(8,128)(2,1)S(1)}, bf16[512,512]{1,0:T(8,128)(2,1)}, u32[]{:S(2)}) copy-start(bf16[512,512]{1,0:T(8,128)(2,1)} %w_out_ref.3) | copy-start | bytes 1572868
  2.0 29.9 %copy-start.1 = (s32[4]{0:T(128)S(1)}, s32[4]{0:T(128)}, u32[]{:S(2)}) copy-start(s32[4]{0:T(128)} %offset_ref.5) | copy-start | bytes 52
  2.0 29.9 %copy-start.2 = (s32[4]{0:T(128)S(1)}, s32[4]{0:T(128)}, u32[]{:S(2)}) copy-start(s32[4]{0:T(128)} %length_ref.3) | copy-start | bytes 52
  2.0 29.9 %copy-start.4 = (bf16[512,512]{1,0:T(8,128)(2,1)S(1)}, bf16[512,512]{1,0:T(8,128)(2,1)}, u32[]{:S(2)}) copy-start(bf16[512,512]{1,0:T(8,128)(2,1)} %cot_ref.1) | copy-start | bytes 1572868
  2.0 29.9 %copy-start.5 = (f32[4,12]{1,0:T(4,128)S(1)}, f32[4,12]{1,0:T(4,128)}, u32[]{:S(2)}) copy-start(f32[4,12]{1,0:T(4,128)} %rab_ref.1) | copy-start | bytes 580
  40.3 6.8 %collective-permute-start = (bf16[16,4,16,640]{3,2,1,0:T(8,128)(2,1)S(1)}, bf16[16,4,16,640]{3,2,1,0:T(8,128)(2,1)S(1)}, u32[]{:S(2)}, u32[]{:S(2)}) collective-permute-start(bf16[16,4,16,640]{3,2,1,0:T(8,128)(2,1)S(1)} %get-tuple-element.23), channel_id=1, source_target_pairs={{0,64},{64,0},{1,65},{65,1},{2,66},{66,2},{3,67},{67,3},{4,68},{68... | collective-permute-start | bytes 3932168 | tf_op jit(solution)/shard_map/ppermute | solution.py:627
  108.8 5.5 %collective-permute-start.1 = (bf16[64,16,640]{2,1,0:T(8,128)(2,1)S(1)}, bf16[64,16,640]{2,1,0:T(8,128)(2,1)S(1)}, u32[]{:S(2)}, u32[]{:S(2)}) collective-permute-start(bf16[64,16,640]{2,1,0:T(8,128)(2,1)S(1)} %slice.4), channel_id=1, source_target_pairs={{0,64},{64,0},{1,65},{65,1},{2,66},{66,2},{3,67},{67,3},{4,68},{68... | collective-permute-start | bytes 3932168 | tf_op jit(solution)/shard_map/ppermute | solution.py:631

commit v8 on v7

--- a/solution.py
+++ b/solution.py
@@ -349,12 +349,12 @@
 
 
 def weight_grads(normed_t, mixed_t, gh_ref, up_ref, store):
-    for at in range(0, HID + D, 256):
+    for at in range(0, HID + D, D):
         if at < HID:
-            value = dot(normed_t, gh_ref[:, at : at + 256])
+            value = dot(normed_t, gh_ref[:, at : at + D])
         else:
-            value = dot(mixed_t, up_ref[:, at - HID : at - HID + 256])
-        for n in (0, 128):
+            value = dot(mixed_t, up_ref[...])
+        for n in range(0, D, 128):
             side, start = (at + n) // CHUNK, (at + n) % CHUNK
             shares = value[:, n : n + 128].reshape(HALF // PIECE, PIECE, 128)
             store((slice(None), side, slice(None), slice(start, start + 128)), shares)

time: 116 us -> 116 us (level)
  no operation moved by 1% of the time
where the time goes in v8:
time: 116 us
  blocking collectives  90.7 us (78%)
  Pallas kernels  18.5 us (16%)
  starting transfers between devices  5.67 us (5%)
    all_to_all x1, blocking collectives, body(): received = exchange(total(received, back.reshape(MEMBERS, PIECE, D)))  36.9 us
    all_to_all x1, blocking collectives, body(): arrived = exchange(pack(route, events))  29.8 us
    all_to_all x1, blocking collectives, body(): received = exchange(join(own, got).reshape(MEMBERS, PIECE, CHUNK))  24 us
    pallas_call x1, Pallas kernels, layer(): pl.pallas_call(layer_kernel, out_shape=(jax.ShapeDtypeStruct(SHARES, BF16...  8.45 us
    pallas_call x1, Pallas kernels, beside(): pl.pallas_call(beside_kernel, out_shape=(jax.ShapeDtypeStruct(SHARES, BF1...  3.63 us
    ppermute x1, starting transfers between devices, body(): got = swap(other)  3.17 us
    pallas_call x1, Pallas kernels, mine_out(): pl.pallas_call(mine_kernel, out_shape=(jax.ShapeDtypeStruct(rows, BF16),...  2.95 us
    ppermute x1, starting transfers between devices, body(): theirs = swap(received[:, :, :CHUNK])  2.5 us
  transfers between devices with their start and end apart: 2, of which 0 were waited for; matrix products, arithmetic and copies ran while one was open for 0% of the time, Pallas kernels for 6%

profile of v8, /device:TPU:1, one launch (start us, length us, event | category | flops | bytes accessed | tf_op | source)
XLA Modules:
  0.0 116.0 jit_solution(11499456402947086585)
XLA Ops:
  0.6 0.0 copy-start.3
  0.6 1.3 %pack_pieces.1 = bf16[64,72,128]{2,1,0:T(8,128)(2,1)S(1)} custom-call(s32[32]{0:T(128)} %route_hbm.3, bf16[512,512]{1,0:T(8,128)(2,1)} %events_hbm.1), custom_call_target="tpu_custom_call" | custom-call | tf_op jit(solution)/shard_map/pack_pieces/pallas_call | solution.py:77
  2.0 0.0 copy-start
  2.0 0.0 copy-start.1
  2.0 0.0 copy-start.2
  2.0 0.0 copy-start.4
  2.0 0.0 copy-start.5
  2.0 29.8 %all_to_all.15.arrived_ref = bf16[64,72,128]{2,1,0:T(8,128)(2,1)S(1)} all-to-all(bf16[64,72,128]{2,1,0:T(8,128)(2,1)S(1)} %pack_pieces.1), channel_id=1, replica_groups=mesh['group'=2,'member'=64] {'member'}, dimensions={0} | all-to-all | bytes 2359296 | tf_op jit(solution)/shard_map/all_to_all | solution.py:623
  31.8 0.0 copy-done.3
  31.9 0.0 copy-done
  31.9 0.0 copy-done.1
  31.9 0.0 copy-done.2
  31.9 0.0 copy-done.4
  31.9 0.0 copy-done.5
  31.9 8.4 %layer.1 = (bf16[16,4,16,640]{3,2,1,0:T(8,128)(2,1)S(1)}, bf16[2,256,512]{2,1,0:T(8,128)(2,1)S(1)}, bf16[512,512]{1,0:T(8,128)(2,1)S(1)}, bf16[512,2048]{1,0:T(8...) custom-call(s32[4]{0:T(128)S(1)} %copy-done.1, s32[4]{0:T(128)S(1)} %copy-done.2, ...), custom_call_target="tpu_custom_call" | custom-call | flops 4000000000 | bytes 9000000 | tf_op jit(solution)/shard_map/layer/pallas_call | solution.py:451
  40.3 3.2 %collective-permute-start = (bf16[16,4,16,640]{3,2,1,0:T(8,128)(2,1)S(1)}, bf16[16,4,16,640]{3,2,1,0:T(8,128)(2,1)S(1)}, u32[]{:S(2)}, u32[]{:S(2)}) collective-permute-start(bf16[16,4,16,640]{3,2,1,0:T(8,128)(2,1)S(1)} %get-tuple-element.23), channel_id=1, source_target_pairs={{0,64},{64,0},{1,65},{65,1},{2,66},{66,2},{3,67},{67,3},{4,68},{68... | collective-permute-start | bytes 3932168 | tf_op jit(solution)/shard_map/ppermute | solution.py:627
  43.5 3.6 %beside.1 = (bf16[16,4,16,640]{3,2,1,0:T(8,128)(2,1)S(1)}, bf16[1024,512]{1,0:T(8,128)(2,1)S(1)}) custom-call(s32[4]{0:T(128)S(1)} %copy-done.1, bf16[64,72,128]{2,1,0:T(8,128)(2,1)S(1)} %all_to_all.15.arrived_ref, bf16[2,256,512]{2,1,0:T(8,128)(2,1)S(1)} %get-tuple-element.18.left_ref, bf16[512,512]{1,0:T(8,128)(2,1)S(1)} %get-tuple-element.19.up_ref, ...), custom_call_target="tpu_custom_call" | custom-call | flops 3000000000 | bytes 2000000 | tf_op jit(solution)/shard_map/beside/pallas_call | solution.py:397
  47.2 0.0 collective-permute-done.got_ref
  47.2 0.3 join.1
  47.5 24.0 %all_to_all.16.received_ref = bf16[64,16,640]{2,1,0:T(8,128)(2,1)S(1)} all-to-all(bf16[64,16,640]{2,1,0:T(8,128)(2,1)S(1)} %bitcast.5), channel_id=1, replica_groups=mesh['group'=2,'member'=64] {'member'}, dimensions={0} | all-to-all | bytes 2621440 | tf_op jit(solution)/shard_map/all_to_all | solution.py:629
  71.5 0.3 total.1
  71.8 36.9 %all_to_all.17 = bf16[64,16,1152]{2,1,0:T(8,128)(2,1)S(1)} all-to-all(bf16[64,16,1152]{2,1,0:T(8,128)(2,1)S(1)} %total.1), channel_id=1, replica_groups=mesh['group'=2,'member'=64] {'member'}, dimensions={0} | all-to-all | bytes 4718592 | tf_op jit(solution)/shard_map/all_to_all | solution.py:630
  108.7 0.1 slice.4
  108.8 2.5 %collective-permute-start.1 = (bf16[64,16,640]{2,1,0:T(8,128)(2,1)S(1)}, bf16[64,16,640]{2,1,0:T(8,128)(2,1)S(1)}, u32[]{:S(2)}, u32[]{:S(2)}) collective-permute-start(bf16[64,16,640]{2,1,0:T(8,128)(2,1)S(1)} %slice.4), channel_id=1, source_target_pairs={{0,64},{64,0},{1,65},{65,1},{2,66},{66,2},{3,67},{67,3},{4,68},{68... | collective-permute-start | bytes 3932168 | tf_op jit(solution)/shard_map/ppermute | solution.py:631
  111.3 2.9 %mine_out.1 = (bf16[512,512]{1,0:T(8,128)(2,1)}, f32[512,2048]{1,0:T(8,128)}, f32[512,512]{1,0:T(8,128)}, bf16[512,512]{1,0:T(8,128)(2,1)}) custom-call(s32[32]{0:T(128)} %route_hbm.3, s32[4]{0:T(128)S(1)} %copy-done.1, s32[4]{0:T(128)S(1)} %copy-done.2, bf16[16,4,16,1152]{3,2,1,0:T(8,128)(2,1)S(1)} %bitcast.4, ...), custom_call_target="tpu_custom_call" | custom-call | flops 300000000 | bytes 6000000 | tf_op jit(solution)/shard_map/mine_out/pallas_call | solution.py:566
  114.3 0.0 collective-permute-done.1
  114.3 1.6 %theirs_out.1 = (f32[512,2048]{1,0:T(8,128)}, f32[512,512]{1,0:T(8,128)}) custom-call(bf16[16,4,16,640]{3,2,1,0:T(8,128)(2,1)S(1)} %bitcast.6, f32[512,2048]{1,0:T(8,128)} %get-tuple-element.28._, f32[512,512]{1,0:T(8,128)} %get-tuple-element.29.__), custom_call_target="tpu_custom_call", output_to_operand_aliasing={{0}: (1, {}), {1}: (2, {})} | custom-call | bytes 2000000 | tf_op jit(solution)/shard_map/theirs_out/pallas_call | solution.py:599
Async XLA Ops:
  0.6 31.2 %copy-start.3 = (bf16[512,2048]{1,0:T(8,128)(2,1)S(1)}, bf16[512,2048]{1,0:T(8,128)(2,1)}, u32[]{:S(2)}) copy-start(bf16[512,2048]{1,0:T(8,128)(2,1)} %w_in_ref.3) | copy-start | bytes 6291460
  2.0 29.9 %copy-start = (bf16[512,512]{1,0:T(8,128)(2,1)S(1)}, bf16[512,512]{1,0:T(8,128)(2,1)}, u32[]{:S(2)}) copy-start(bf16[512,512]{1,0:T(8,128)(2,1)} %w_out_ref.3) | copy-start | bytes 1572868
  2.0 29.9 %copy-start.1 = (s32[4]{0:T(128)S(1)}, s32[4]{0:T(128)}, u32[]{:S(2)}) copy-start(s32[4]{0:T(128)} %offset_ref.5) | copy-start | bytes 52
  2.0 29.9 %copy-start.2 = (s32[4]{0:T(128)S(1)}, s32[4]{0:T(128)}, u32[]{:S(2)}) copy-start(s32[4]{0:T(128)} %length_ref.3) | copy-start | bytes 52
  2.0 29.9 %copy-start.4 = (bf16[512,512]{1,0:T(8,128)(2,1)S(1)}, bf16[512,512]{1,0:T(8,128)(2,1)}, u32[]{:S(2)}) copy-start(bf16[512,512]{1,0:T(8,128)(2,1)} %cot_ref.1) | copy-start | bytes 1572868
  2.0 29.9 %copy-start.5 = (f32[4,12]{1,0:T(4,128)S(1)}, f32[4,12]{1,0:T(4,128)}, u32[]{:S(2)}) copy-start(f32[4,12]{1,0:T(4,128)} %rab_ref.1) | copy-start | bytes 580
  40.3 6.8 %collective-permute-start = (bf16[16,4,16,640]{3,2,1,0:T(8,128)(2,1)S(1)}, bf16[16,4,16,640]{3,2,1,0:T(8,128)(2,1)S(1)}, u32[]{:S(2)}, u32[]{:S(2)}) collective-permute-start(bf16[16,4,16,640]{3,2,1,0:T(8,128)(2,1)S(1)} %get-tuple-element.23), channel_id=1, source_target_pairs={{0,64},{64,0},{1,65},{65,1},{2,66},{66,2},{3,67},{67,3},{4,68},{68... | collective-permute-start | bytes 3932168 | tf_op jit(solution)/shard_map/ppermute | solution.py:627
  108.8 5.5 %collective-permute-start.1 = (bf16[64,16,640]{2,1,0:T(8,128)(2,1)S(1)}, bf16[64,16,640]{2,1,0:T(8,128)(2,1)S(1)}, u32[]{:S(2)}, u32[]{:S(2)}) collective-permute-start(bf16[64,16,640]{2,1,0:T(8,128)(2,1)S(1)} %slice.4), channel_id=1, source_target_pairs={{0,64},{64,0},{1,65},{65,1},{2,66},{66,2},{3,67},{67,3},{4,68},{68... | collective-permute-start | bytes 3932168 | tf_op jit(solution)/shard_map/ppermute | solution.py:631
